TPU v7x, 256 devices: a whole 4x4x8 slice. The times are simulated.
256 devices in a mesh: tm: 16 (over z, core), space: 16 (over y, x).
Axes of the slice: x: 4, y: 4, z: 8, core: 2. Of those that a mesh axis runs over, the one named last changes fastest.
Arguments:
- forcing: float32 [128, 64, 32, 128], P('tm', 'space'), may hold values from -6 to 6
- c_guess: float32 [32, 64, 32, 128], P('tm', 'space'), may hold values from -6 to 6
- initial: float32 [64, 32, 128], P('space'), may hold values from -6 to 6
- porosity: float32 [64, 32, 128], P('space'), may hold values from 0.5 to 4
- permeability: float32 [3, 64, 32, 128], P(None, 'space'), may hold values from 0.1 to 10
Outputs:
- fine_state: float32 [128, 64, 32, 128], P('tm', 'space')
- coarse_state: float32 [32, 64, 32, 128], P('tm', 'space')
- coarse_source: float32 [16, 64, 32, 128], P('tm', 'space')
All inputs are finite; a program needn't handle non-finite values.
Results may differ from a plain program's by a relative error of at most 0.00002.
Values sent between devices are 32-bit elements; how exact they have to be, the bound alone decides.
No kernel may reach another device: no remote copies, remote signals or barrier semaphores. Data moves between devices by JAX's collectives and lax.ppermute only.
A program may use at most 64 MiB of HBM per device.

v0:
```python
import jax
import jax.numpy as jnp
from jax import lax
from jax.sharding import PartitionSpec as P

CF = 4
SWEEPS = 4


storage_rate = 2.0


def padded_2(cells, sides, width):
    for axis, dim in sides:
        count = lax.axis_size(axis)
        ends = count - 1
        head = lax.slice_in_dim(cells, 0, width, axis=dim)
        tail = lax.slice_in_dim(cells, cells.shape[dim] - width, cells.shape[dim], axis=dim)
        cells = jnp.concatenate(
            [
                lax.ppermute(tail, axis, [(i, (i + 1) % count) for i in range(ends)]),
                cells,
                lax.ppermute(head, axis, [((i + 1) % count, i) for i in range(ends)]),
            ],
            axis=dim,
        )
    return cells


def passed_along(value, axis, steps):
    count = lax.axis_size(axis)
    first, last = (max(0, -steps), min(count, count - steps))
    return lax.ppermute(value, axis, [(source, source + steps) for source in range(first, last)])


def harmonic_faces(padded, dimension):
    length = padded.shape[dimension]
    lower_k = lax.slice_in_dim(padded, 0, length - 1, axis=dimension)
    upper_k = lax.slice_in_dim(padded, 1, length, axis=dimension)
    faces = 2.0 * lower_k * upper_k / (lower_k + upper_k)
    count = length - 1
    return (
        lax.slice_in_dim(faces, 0, count - 1, axis=dimension),
        lax.slice_in_dim(faces, 1, count, axis=dimension),
    )


def faces_along(perm_k, dimension):
    length = perm_k.shape[dimension]
    leading = lax.slice_in_dim(perm_k, 0, 1, axis=dimension)
    trailing = lax.slice_in_dim(perm_k, length - 1, length, axis=dimension)
    return harmonic_faces(jnp.concatenate([leading, perm_k, trailing], dimension), dimension)


def lower_upper(field, dimension):
    dimension = dimension % field.ndim
    length = field.shape[dimension]
    empty = jnp.zeros_like(lax.slice_in_dim(field, 0, 1, axis=dimension))
    lower = jnp.concatenate(
        [empty, lax.slice_in_dim(field, 0, length - 1, axis=dimension)], dimension
    )
    upper = jnp.concatenate([lax.slice_in_dim(field, 1, length, axis=dimension), empty], dimension)
    return (lower, upper)


def relax_sweep(center, z_lower, z_upper, right_side, coefficients, inverse_diag):
    west, east, south, north, below, above = coefficients
    x_lower, x_upper = lower_upper(center, -1)
    y_lower, y_upper = lower_upper(center, -2)
    total = (
        right_side
        + (west * x_lower + east * x_upper)
        + (south * y_lower + north * y_upper)
        + (below * z_lower + above * z_upper)
    )
    return total * inverse_diag


def advance(state, source_term, factors, coefficients, coupling, storage):
    factor = jnp.asarray(factors, jnp.float32).reshape(-1, 1, 1, 1)
    storage_now = storage * factor
    inverse_diag = 1.0 / (storage_now + coupling)
    right_side = storage_now * state + source_term
    iterate = state
    for sweep in range(SWEEPS):
        padded = padded_2(iterate, (("space", 1),), 1)
        iterate = relax_sweep(
            iterate, padded[:, :-2], padded[:, 2:], right_side, coefficients, inverse_diag
        )
    return iterate


def on_device(forcing, c_guess, initial, porosity, permeability):
    west, east = faces_along(permeability[0], 2)
    south, north = faces_along(permeability[1], 1)
    perm_z = permeability[2]
    padded_z = padded_2(perm_z, (("space", 0),), 1)
    position = lax.axis_index("space")
    lower_rim = jnp.where(position == 0, perm_z[:1], padded_z[:1])
    upper_rim = jnp.where(position == lax.axis_size("space") - 1, perm_z[-1:], padded_z[-1:])
    below, above = harmonic_faces(jnp.concatenate([lower_rim, perm_z, upper_rim], 0), 0)
    coefficients = (west, east, south, north, below, above)
    coupling = west + east + (south + north) + (below + above)
    storage = porosity * storage_rate

    def step_batch(state, source_term, factors):
        return advance(state, source_term, factors, coefficients, coupling, storage)

    step_count = forcing.shape[0]
    cells = forcing.shape[1:]
    blocks = forcing.reshape((2, CF) + cells)
    first_slab = lax.axis_index("tm") == 0
    empty = jnp.zeros_like(initial)

    def frelax(previous):
        current = previous
        results = []
        for section in range(CF - 1):
            current = step_batch(current, blocks[:, section], [1.0, 1.0])
            results.append(current)
        return jnp.stack(results, 1)

    received = passed_along(c_guess[1], "tm", 1)
    previous = jnp.stack([jnp.where(first_slab, initial, received), c_guess[0]])
    early_fine = frelax(previous)
    relaxed_c = step_batch(early_fine[:, CF - 2], blocks[:, CF - 1], [1.0, 1.0])
    received = passed_along(relaxed_c[1], "tm", 1)
    previous_c = jnp.stack([jnp.where(first_slab, initial, received), relaxed_c[0]])
    late_fine = frelax(previous_c)
    fine_state = jnp.concatenate([late_fine, relaxed_c[:, None]], 1).reshape((step_count,) + cells)
    restricted = step_batch(
        jnp.concatenate([late_fine[:, CF - 2], previous_c], 0),
        jnp.concatenate([blocks[:, CF - 1], jnp.zeros_like(previous_c)], 0),
        [1.0, 1.0, 1.0 / CF, 1.0 / CF],
    )
    level_source = restricted[:2] - relaxed_c + relaxed_c - restricted[2:]
    coarse_factor = [1.0 / CF]
    coarse_first = step_batch(previous_c[0:1], empty[None], coarse_factor)[0] + level_source[0]
    coarse_last = step_batch(coarse_first[None], empty[None], coarse_factor)[0] + level_source[1]
    received = passed_along(coarse_last, "tm", 1)
    previous_two = jnp.where(first_slab, initial, received)
    coarse_again = step_batch(previous_two[None], empty[None], coarse_factor)[0] + level_source[0]
    coarse_state = jnp.stack([coarse_again, coarse_last])
    paired = step_batch(
        jnp.stack([coarse_again, previous_two]),
        jnp.stack([empty, empty]),
        [1.0 / CF, 1.0 / (2 * CF)],
    )
    second_residual = paired[0] + level_source[1] - coarse_last
    coarse_source = second_residual + coarse_last - paired[1]
    return (fine_state, coarse_state, coarse_source[None])


def solution(mesh):
    return jax.shard_map(
        on_device,
        mesh=mesh,
        in_specs=(
            P("tm", "space", None, None),
            P("tm", "space", None, None),
            P("space", None, None),
            P("space", None, None),
            P(None, "space", None, None),
        ),
        out_specs=(
            P("tm", "space", None, None),
            P("tm", "space", None, None),
            P("tm", "space", None, None),
        ),
        check_vma=False,
    )
```

profile of v0, /device:TPU:136, one launch (start us, length us, event | category | flops | bytes accessed | tf_op | source)
XLA Modules:
  0.0 518.7 jit_solution(5488098578446507085)
XLA Ops:
  4.8 4.6 collective-permute-start.2
  19.3 6.0 %collective-permute-start.4 = (f32[2,1,32,128]{3,2,1,0:T(8,128)S(1)}, f32[2,1,32,128]{3,2,1,0:T(8,128)S(1)}, u32[]{:S(2)}, u32[]{:S(2)}) collective-permute-start(f32[2,1,32,128]{3,2,1,0:T(8,128)S(1)} %get-tuple-element.239), channel_id=1, source_target_pairs={{1,0},{2,1},{3,2},{4,3},{5,4},{6,5},{7,6},{8,7},{9,8},{10,9},{11,1... | collective-permute-start | bytes 98312 | tf_op jit(solution)/shard_map/ppermute | solution.py:23
  29.1 6.3 %collective-permute-start.6 = (f32[2,1,32,128]{3,2,1,0:T(8,128)S(1)}, f32[2,1,32,128]{3,2,1,0:T(8,128)S(1)}, u32[]{:S(2)}, u32[]{:S(2)}) collective-permute-start(f32[2,1,32,128]{3,2,1,0:T(8,128)S(1)} %get-tuple-element.233), channel_id=1, source_target_pairs={{1,0},{2,1},{3,2},{4,3},{5,4},{6,5},{7,6},{8,7},{9,8},{10,9},{11,1... | collective-permute-start | bytes 98312 | tf_op jit(solution)/shard_map/ppermute | solution.py:23
  41.0 4.5 collective-permute-start.8
  47.4 6.3 %collective-permute-start.10 = (f32[2,1,32,128]{3,2,1,0:T(8,128)S(1)}, f32[2,1,32,128]{3,2,1,0:T(8,128)S(1)}, u32[]{:S(2)}, u32[]{:S(2)}) collective-permute-start(f32[2,1,32,128]{3,2,1,0:T(8,128)S(1)} %get-tuple-element.221), channel_id=1, source_target_pairs={{1,0},{2,1},{3,2},{4,3},{5,4},{6,5},{7,6},{8,7},{9,8},{10,9},{11,1... | collective-permute-start | bytes 98312 | tf_op jit(solution)/shard_map/ppermute | solution.py:23
  55.7 6.0 %collective-permute-done.9 = f32[2,1,32,128]{3,2,1,0:T(8,128)S(1)} collective-permute-done((f32[2,1,32,128]{3,2,1,0:T(8,128)S(1)}, f32[2,1,32,128]{3,2,1,0:T(8,128)S(1)}, u32[]{:S(2)}, u32[]{:S(2)}) %collective-permute-start.9) | collective-permute-done | bytes 32800 | tf_op jit(solution)/shard_map/ppermute | solution.py:21
  63.9 6.0 %collective-permute-start.12 = (f32[2,1,32,128]{3,2,1,0:T(8,128)S(1)}, f32[2,1,32,128]{3,2,1,0:T(8,128)S(1)}, u32[]{:S(2)}, u32[]{:S(2)}) collective-permute-start(f32[2,1,32,128]{3,2,1,0:T(8,128)S(1)} %get-tuple-element.215), channel_id=1, source_target_pairs={{1,0},{2,1},{3,2},{4,3},{5,4},{6,5},{7,6},{8,7},{9,8},{10,9},{11,1... | collective-permute-start | bytes 98312 | tf_op jit(solution)/shard_map/ppermute | solution.py:23
  73.7 6.3 %collective-permute-start.14 = (f32[2,1,32,128]{3,2,1,0:T(8,128)S(1)}, f32[2,1,32,128]{3,2,1,0:T(8,128)S(1)}, u32[]{:S(2)}, u32[]{:S(2)}) collective-permute-start(f32[2,1,32,128]{3,2,1,0:T(8,128)S(1)} %get-tuple-element.209), channel_id=1, source_target_pairs={{1,0},{2,1},{3,2},{4,3},{5,4},{6,5},{7,6},{8,7},{9,8},{10,9},{11,1... | collective-permute-start | bytes 98312 | tf_op jit(solution)/shard_map/ppermute | solution.py:23
  85.7 4.5 collective-permute-start.16
  95.9 4.5 collective-permute-start.18
  106.0 4.5 collective-permute-start.20
  126.3 4.5 collective-permute-start.24
  156.8 4.5 collective-permute-start.30
  167.1 4.5 collective-permute-start.32
  185.5 4.8 collective-permute-done.35
  200.8 6.0 %collective-permute-start.37 = (f32[2,1,32,128]{3,2,1,0:T(8,128)S(1)}, f32[2,1,32,128]{3,2,1,0:T(8,128)S(1)}, u32[]{:S(2)}, u32[]{:S(2)}) collective-permute-start(f32[2,1,32,128]{3,2,1,0:T(8,128)S(1)} %get-tuple-element.141), channel_id=1, source_target_pairs={{1,0},{2,1},{3,2},{4,3},{5,4},{6,5},{7,6},{8,7},{9,8},{10,9},{11,1... | collective-permute-start | bytes 98312 | tf_op jit(solution)/shard_map/ppermute | solution.py:23
  209.0 6.0 %collective-permute-start.63 = (f32[1,1,32,128]{3,2,1,0:T(8,128)S(1)}, f32[1,1,32,128]{3,2,1,0:T(8,128)S(1)}, u32[]{:S(2)}, u32[]{:S(2)}) collective-permute-start(f32[1,1,32,128]{3,2,1,0:T(8,128)S(1)} %get-tuple-element.312), channel_id=1, source_target_pairs={{1,0},{2,1},{3,2},{4,3},{5,4},{6,5},{7,6},{8,7},{9,8},{10,9},{11,1... | collective-permute-start | bytes 49160 | tf_op jit(solution)/shard_map/ppermute | solution.py:23
  218.7 6.3 %collective-permute-start.65 = (f32[1,1,32,128]{3,2,1,0:T(8,128)S(1)}, f32[1,1,32,128]{3,2,1,0:T(8,128)S(1)}, u32[]{:S(2)}, u32[]{:S(2)}) collective-permute-start(f32[1,1,32,128]{3,2,1,0:T(8,128)S(1)} %get-tuple-element.306), channel_id=1, source_target_pairs={{1,0},{2,1},{3,2},{4,3},{5,4},{6,5},{7,6},{8,7},{9,8},{10,9},{11,1... | collective-permute-start | bytes 49160 | tf_op jit(solution)/shard_map/ppermute | solution.py:23
  226.9 6.0 %collective-permute-start.39 = (f32[2,1,32,128]{3,2,1,0:T(8,128)S(1)}, f32[2,1,32,128]{3,2,1,0:T(8,128)S(1)}, u32[]{:S(2)}, u32[]{:S(2)}) collective-permute-start(f32[2,1,32,128]{3,2,1,0:T(8,128)S(1)} %get-tuple-element.135), channel_id=1, source_target_pairs={{1,0},{2,1},{3,2},{4,3},{5,4},{6,5},{7,6},{8,7},{9,8},{10,9},{11,1... | collective-permute-start | bytes 98312 | tf_op jit(solution)/shard_map/ppermute | solution.py:23
  235.1 6.0 %collective-permute-start.67 = (f32[1,1,32,128]{3,2,1,0:T(8,128)S(1)}, f32[1,1,32,128]{3,2,1,0:T(8,128)S(1)}, u32[]{:S(2)}, u32[]{:S(2)}) collective-permute-start(f32[1,1,32,128]{3,2,1,0:T(8,128)S(1)} %get-tuple-element.300), channel_id=1, source_target_pairs={{1,0},{2,1},{3,2},{4,3},{5,4},{6,5},{7,6},{8,7},{9,8},{10,9},{11,1... | collective-permute-start | bytes 49160 | tf_op jit(solution)/shard_map/ppermute | solution.py:23
  243.4 6.0 %collective-permute-start.41 = (f32[2,1,32,128]{3,2,1,0:T(8,128)S(1)}, f32[2,1,32,128]{3,2,1,0:T(8,128)S(1)}, u32[]{:S(2)}, u32[]{:S(2)}) collective-permute-start(f32[2,1,32,128]{3,2,1,0:T(8,128)S(1)} %get-tuple-element.129), channel_id=1, source_target_pairs={{1,0},{2,1},{3,2},{4,3},{5,4},{6,5},{7,6},{8,7},{9,8},{10,9},{11,1... | collective-permute-start | bytes 98312 | tf_op jit(solution)/shard_map/ppermute | solution.py:23
  253.2 6.3 %collective-permute-start.43 = (f32[2,1,32,128]{3,2,1,0:T(8,128)S(1)}, f32[2,1,32,128]{3,2,1,0:T(8,128)S(1)}, u32[]{:S(2)}, u32[]{:S(2)}) collective-permute-start(f32[2,1,32,128]{3,2,1,0:T(8,128)S(1)} %get-tuple-element.123), channel_id=1, source_target_pairs={{1,0},{2,1},{3,2},{4,3},{5,4},{6,5},{7,6},{8,7},{9,8},{10,9},{11,1... | collective-permute-start | bytes 98312 | tf_op jit(solution)/shard_map/ppermute | solution.py:23
  265.2 4.5 collective-permute-start.45
  315.9 4.7 collective-permute-start.55
  336.2 4.5 collective-permute-start.59
  420.1 4.5 collective-permute-start.83
  436.8 4.5 collective-permute-start.86
  446.7 4.5 collective-permute-start.88
  466.4 4.5 collective-permute-start.92
  487.1 4.5 collective-permute-start.96
  503.6 6.3 %collective-permute-start.100 = (f32[2,1,32,128]{3,2,1,0:T(8,128)S(1)}, f32[2,1,32,128]{3,2,1,0:T(8,128)S(1)}, u32[]{:S(2)}, u32[]{:S(2)}) collective-permute-start(f32[2,1,32,128]{3,2,1,0:T(8,128)S(1)} %get-tuple-element.49), channel_id=1, source_target_pairs={{1,0},{2,1},{3,2},{4,3},{5,4},{6,5},{7,6},{8,7},{9,8},{10,9},{11,1... | collective-permute-start | bytes 98312 | tf_op jit(solution)/shard_map/ppermute | solution.py:23
  512.0 6.0 %collective-permute-done.99 = f32[2,1,32,128]{3,2,1,0:T(8,128)S(1)} collective-permute-done((f32[2,1,32,128]{3,2,1,0:T(8,128)S(1)}, f32[2,1,32,128]{3,2,1,0:T(8,128)S(1)}, u32[]{:S(2)}, u32[]{:S(2)}) %collective-permute-start.99) | collective-permute-done | bytes 32800 | tf_op jit(solution)/shard_map/ppermute | solution.py:21
  (395 shorter events, 346.0 us)
Async XLA Ops:
  1.4 11.1 %collective-permute-start.1 = (f32[1,32,128]{2,1,0:T(8,128)S(1)}, f32[1,32,128]{2,1,0:T(8,128)S(1)}, u32[]{:S(2)}, u32[]{:S(2)}) collective-permute-start(f32[1,32,128]{2,1,0:T(8,128)S(1)} %get-tuple-element.42), channel_id=1, source_target_pairs={{0,1},{1,2},{2,3},{3,4},{4,5},{5,6},{6,7},{7,8},{8,9},{9,10},{10,1... | collective-permute-start | bytes 49160 | tf_op jit(solution)/shard_map/ppermute | solution.py:21
  37.3 8.3 %collective-permute-start.7 = (f32[2,1,32,128]{3,2,1,0:T(8,128)S(1)}, f32[2,1,32,128]{3,2,1,0:T(8,128)S(1)}, u32[]{:S(2)}, u32[]{:S(2)}) collective-permute-start(f32[2,1,32,128]{3,2,1,0:T(8,128)S(1)} %get-tuple-element.226), channel_id=1, source_target_pairs={{0,1},{1,2},{2,3},{3,4},{4,5},{5,6},{6,7},{7,8},{8,9},{9,10},{10,1... | collective-permute-start | bytes 98312 | tf_op jit(solution)/shard_map/ppermute | solution.py:21
  71.8 8.5 %collective-permute-start.13 = (f32[2,1,32,128]{3,2,1,0:T(8,128)S(1)}, f32[2,1,32,128]{3,2,1,0:T(8,128)S(1)}, u32[]{:S(2)}, u32[]{:S(2)}) collective-permute-start(f32[2,1,32,128]{3,2,1,0:T(8,128)S(1)} %get-tuple-element.208), channel_id=1, source_target_pairs={{0,1},{1,2},{2,3},{3,4},{4,5},{5,6},{6,7},{7,8},{8,9},{9,10},{10,1... | collective-permute-start | bytes 98312 | tf_op jit(solution)/shard_map/ppermute | solution.py:21
  82.0 8.3 %collective-permute-start.15 = (f32[2,1,32,128]{3,2,1,0:T(8,128)S(1)}, f32[2,1,32,128]{3,2,1,0:T(8,128)S(1)}, u32[]{:S(2)}, u32[]{:S(2)}) collective-permute-start(f32[2,1,32,128]{3,2,1,0:T(8,128)S(1)} %get-tuple-element.202), channel_id=1, source_target_pairs={{0,1},{1,2},{2,3},{3,4},{4,5},{5,6},{6,7},{7,8},{8,9},{9,10},{10,1... | collective-permute-start | bytes 98312 | tf_op jit(solution)/shard_map/ppermute | solution.py:21
  92.1 8.3 %collective-permute-start.17 = (f32[2,1,32,128]{3,2,1,0:T(8,128)S(1)}, f32[2,1,32,128]{3,2,1,0:T(8,128)S(1)}, u32[]{:S(2)}, u32[]{:S(2)}) collective-permute-start(f32[2,1,32,128]{3,2,1,0:T(8,128)S(1)} %get-tuple-element.196), channel_id=1, source_target_pairs={{0,1},{1,2},{2,3},{3,4},{4,5},{5,6},{6,7},{7,8},{8,9},{9,10},{10,1... | collective-permute-start | bytes 98312 | tf_op jit(solution)/shard_map/ppermute | solution.py:21
  112.4 8.3 %collective-permute-start.21 = (f32[2,1,32,128]{3,2,1,0:T(8,128)S(1)}, f32[2,1,32,128]{3,2,1,0:T(8,128)S(1)}, u32[]{:S(2)}, u32[]{:S(2)}) collective-permute-start(f32[2,1,32,128]{3,2,1,0:T(8,128)S(1)} %get-tuple-element.184), channel_id=1, source_target_pairs={{0,1},{1,2},{2,3},{3,4},{4,5},{5,6},{6,7},{7,8},{8,9},{9,10},{10,1... | collective-permute-start | bytes 98312 | tf_op jit(solution)/shard_map/ppermute | solution.py:21
  122.6 8.3 %collective-permute-start.23 = (f32[2,1,32,128]{3,2,1,0:T(8,128)S(1)}, f32[2,1,32,128]{3,2,1,0:T(8,128)S(1)}, u32[]{:S(2)}, u32[]{:S(2)}) collective-permute-start(f32[2,1,32,128]{3,2,1,0:T(8,128)S(1)} %get-tuple-element.178), channel_id=1, source_target_pairs={{0,1},{1,2},{2,3},{3,4},{4,5},{5,6},{6,7},{7,8},{8,9},{9,10},{10,1... | collective-permute-start | bytes 98312 | tf_op jit(solution)/shard_map/ppermute | solution.py:21
  132.7 8.3 %collective-permute-start.25 = (f32[2,1,32,128]{3,2,1,0:T(8,128)S(1)}, f32[2,1,32,128]{3,2,1,0:T(8,128)S(1)}, u32[]{:S(2)}, u32[]{:S(2)}) collective-permute-start(f32[2,1,32,128]{3,2,1,0:T(8,128)S(1)} %get-tuple-element.172), channel_id=1, source_target_pairs={{0,1},{1,2},{2,3},{3,4},{4,5},{5,6},{6,7},{7,8},{8,9},{9,10},{10,1... | collective-permute-start | bytes 98312 | tf_op jit(solution)/shard_map/ppermute | solution.py:21
  142.9 8.3 %collective-permute-start.27 = (f32[2,1,32,128]{3,2,1,0:T(8,128)S(1)}, f32[2,1,32,128]{3,2,1,0:T(8,128)S(1)}, u32[]{:S(2)}, u32[]{:S(2)}) collective-permute-start(f32[2,1,32,128]{3,2,1,0:T(8,128)S(1)} %get-tuple-element.166), channel_id=1, source_target_pairs={{0,1},{1,2},{2,3},{3,4},{4,5},{5,6},{6,7},{7,8},{8,9},{9,10},{10,1... | collective-permute-start | bytes 98312 | tf_op jit(solution)/shard_map/ppermute | solution.py:21
  153.0 8.5 %collective-permute-start.29 = (f32[2,1,32,128]{3,2,1,0:T(8,128)S(1)}, f32[2,1,32,128]{3,2,1,0:T(8,128)S(1)}, u32[]{:S(2)}, u32[]{:S(2)}) collective-permute-start(f32[2,1,32,128]{3,2,1,0:T(8,128)S(1)} %get-tuple-element.160), channel_id=1, source_target_pairs={{0,1},{1,2},{2,3},{3,4},{4,5},{5,6},{6,7},{7,8},{8,9},{9,10},{10,1... | collective-permute-start | bytes 98312 | tf_op jit(solution)/shard_map/ppermute | solution.py:21
  163.2 8.4 %collective-permute-start.31 = (f32[2,1,32,128]{3,2,1,0:T(8,128)S(1)}, f32[2,1,32,128]{3,2,1,0:T(8,128)S(1)}, u32[]{:S(2)}, u32[]{:S(2)}) collective-permute-start(f32[2,1,32,128]{3,2,1,0:T(8,128)S(1)} %get-tuple-element.154), channel_id=1, source_target_pairs={{0,1},{1,2},{2,3},{3,4},{4,5},{5,6},{6,7},{7,8},{8,9},{9,10},{10,1... | collective-permute-start | bytes 98312 | tf_op jit(solution)/shard_map/ppermute | solution.py:21
  173.5 8.3 %collective-permute-start.33 = (f32[2,1,32,128]{3,2,1,0:T(8,128)S(1)}, f32[2,1,32,128]{3,2,1,0:T(8,128)S(1)}, u32[]{:S(2)}, u32[]{:S(2)}) collective-permute-start(f32[2,1,32,128]{3,2,1,0:T(8,128)S(1)} %get-tuple-element.148), channel_id=1, source_target_pairs={{0,1},{1,2},{2,3},{3,4},{4,5},{5,6},{6,7},{7,8},{8,9},{9,10},{10,1... | collective-permute-start | bytes 98312 | tf_op jit(solution)/shard_map/ppermute | solution.py:21
  190.6 16.3 %collective-permute-start.60 = (f32[1,1,32,128]{3,2,1,0:T(8,128)S(1)}, f32[1,1,32,128]{3,2,1,0:T(8,128)S(1)}, u32[]{:S(2)}, u32[]{:S(2)}) collective-permute-start(f32[1,1,32,128]{3,2,1,0:T(8,128)S(1)} %get-tuple-element.317), channel_id=1, source_target_pairs={{0,1},{1,2},{2,3},{3,4},{4,5},{5,6},{6,7},{7,8},{8,9},{9,10},{10,1... | collective-permute-start | bytes 49160 | tf_op jit(solution)/shard_map/ppermute | solution.py:21
  194.3 12.5 %collective-permute-start.61 = (f32[1,1,32,128]{3,2,1,0:T(8,128)S(1)}, f32[1,1,32,128]{3,2,1,0:T(8,128)S(1)}, u32[]{:S(2)}, u32[]{:S(2)}) collective-permute-start(f32[1,1,32,128]{3,2,1,0:T(8,128)S(1)} %get-tuple-element.318), channel_id=1, source_target_pairs={{1,0},{2,1},{3,2},{4,3},{5,4},{6,5},{7,6},{8,7},{9,8},{10,9},{11,1... | collective-permute-start | bytes 49160 | tf_op jit(solution)/shard_map/ppermute | solution.py:23
  198.9 16.2 %collective-permute-start.36 = (f32[2,1,32,128]{3,2,1,0:T(8,128)S(1)}, f32[2,1,32,128]{3,2,1,0:T(8,128)S(1)}, u32[]{:S(2)}, u32[]{:S(2)}) collective-permute-start(f32[2,1,32,128]{3,2,1,0:T(8,128)S(1)} %get-tuple-element.140), channel_id=1, source_target_pairs={{0,1},{1,2},{2,3},{3,4},{4,5},{5,6},{6,7},{7,8},{8,9},{9,10},{10,1... | collective-permute-start | bytes 98312 | tf_op jit(solution)/shard_map/ppermute | solution.py:21
  200.8 14.3 %collective-permute-start.37 = (f32[2,1,32,128]{3,2,1,0:T(8,128)S(1)}, f32[2,1,32,128]{3,2,1,0:T(8,128)S(1)}, u32[]{:S(2)}, u32[]{:S(2)}) collective-permute-start(f32[2,1,32,128]{3,2,1,0:T(8,128)S(1)} %get-tuple-element.141), channel_id=1, source_target_pairs={{1,0},{2,1},{3,2},{4,3},{5,4},{6,5},{7,6},{8,7},{9,8},{10,9},{11,1... | collective-permute-start | bytes 98312 | tf_op jit(solution)/shard_map/ppermute | solution.py:23
  207.1 8.3 %collective-permute-start.62 = (f32[1,1,32,128]{3,2,1,0:T(8,128)S(1)}, f32[1,1,32,128]{3,2,1,0:T(8,128)S(1)}, u32[]{:S(2)}, u32[]{:S(2)}) collective-permute-start(f32[1,1,32,128]{3,2,1,0:T(8,128)S(1)} %get-tuple-element.311), channel_id=1, source_target_pairs={{0,1},{1,2},{2,3},{3,4},{4,5},{5,6},{6,7},{7,8},{8,9},{9,10},{10,1... | collective-permute-start | bytes 49160 | tf_op jit(solution)/shard_map/ppermute | solution.py:21
  216.7 16.2 %collective-permute-start.64 = (f32[1,1,32,128]{3,2,1,0:T(8,128)S(1)}, f32[1,1,32,128]{3,2,1,0:T(8,128)S(1)}, u32[]{:S(2)}, u32[]{:S(2)}) collective-permute-start(f32[1,1,32,128]{3,2,1,0:T(8,128)S(1)} %get-tuple-element.305), channel_id=1, source_target_pairs={{0,1},{1,2},{2,3},{3,4},{4,5},{5,6},{6,7},{7,8},{8,9},{9,10},{10,1... | collective-permute-start | bytes 49160 | tf_op jit(solution)/shard_map/ppermute | solution.py:21
  218.7 14.3 %collective-permute-start.65 = (f32[1,1,32,128]{3,2,1,0:T(8,128)S(1)}, f32[1,1,32,128]{3,2,1,0:T(8,128)S(1)}, u32[]{:S(2)}, u32[]{:S(2)}) collective-permute-start(f32[1,1,32,128]{3,2,1,0:T(8,128)S(1)} %get-tuple-element.306), channel_id=1, source_target_pairs={{1,0},{2,1},{3,2},{4,3},{5,4},{6,5},{7,6},{8,7},{9,8},{10,9},{11,1... | collective-permute-start | bytes 49160 | tf_op jit(solution)/shard_map/ppermute | solution.py:23
  225.0 16.2 %collective-permute-start.38 = (f32[2,1,32,128]{3,2,1,0:T(8,128)S(1)}, f32[2,1,32,128]{3,2,1,0:T(8,128)S(1)}, u32[]{:S(2)}, u32[]{:S(2)}) collective-permute-start(f32[2,1,32,128]{3,2,1,0:T(8,128)S(1)} %get-tuple-element.134), channel_id=1, source_target_pairs={{0,1},{1,2},{2,3},{3,4},{4,5},{5,6},{6,7},{7,8},{8,9},{9,10},{10,1... | collective-permute-start | bytes 98312 | tf_op jit(solution)/shard_map/ppermute | solution.py:21
  226.9 14.3 %collective-permute-start.39 = (f32[2,1,32,128]{3,2,1,0:T(8,128)S(1)}, f32[2,1,32,128]{3,2,1,0:T(8,128)S(1)}, u32[]{:S(2)}, u32[]{:S(2)}) collective-permute-start(f32[2,1,32,128]{3,2,1,0:T(8,128)S(1)} %get-tuple-element.135), channel_id=1, source_target_pairs={{1,0},{2,1},{3,2},{4,3},{5,4},{6,5},{7,6},{8,7},{9,8},{10,9},{11,1... | collective-permute-start | bytes 98312 | tf_op jit(solution)/shard_map/ppermute | solution.py:23
  233.2 153.2 %collective-permute-start.66 = (f32[1,1,32,128]{3,2,1,0:T(8,128)S(1)}, f32[1,1,32,128]{3,2,1,0:T(8,128)S(1)}, u32[]{:S(2)}, u32[]{:S(2)}) collective-permute-start(f32[1,1,32,128]{3,2,1,0:T(8,128)S(1)} %get-tuple-element.299), channel_id=1, source_target_pairs={{0,1},{1,2},{2,3},{3,4},{4,5},{5,6},{6,7},{7,8},{8,9},{9,10},{10,1... | collective-permute-start | bytes 49160 | tf_op jit(solution)/shard_map/ppermute | solution.py:21
  235.1 151.3 %collective-permute-start.67 = (f32[1,1,32,128]{3,2,1,0:T(8,128)S(1)}, f32[1,1,32,128]{3,2,1,0:T(8,128)S(1)}, u32[]{:S(2)}, u32[]{:S(2)}) collective-permute-start(f32[1,1,32,128]{3,2,1,0:T(8,128)S(1)} %get-tuple-element.300), channel_id=1, source_target_pairs={{1,0},{2,1},{3,2},{4,3},{5,4},{6,5},{7,6},{8,7},{9,8},{10,9},{11,1... | collective-permute-start | bytes 49160 | tf_op jit(solution)/shard_map/ppermute | solution.py:23
  251.3 8.5 %collective-permute-start.42 = (f32[2,1,32,128]{3,2,1,0:T(8,128)S(1)}, f32[2,1,32,128]{3,2,1,0:T(8,128)S(1)}, u32[]{:S(2)}, u32[]{:S(2)}) collective-permute-start(f32[2,1,32,128]{3,2,1,0:T(8,128)S(1)} %get-tuple-element.122), channel_id=1, source_target_pairs={{0,1},{1,2},{2,3},{3,4},{4,5},{5,6},{6,7},{7,8},{8,9},{9,10},{10,1... | collective-permute-start | bytes 98312 | tf_op jit(solution)/shard_map/ppermute | solution.py:21
  271.6 8.3 %collective-permute-start.46 = (f32[2,1,32,128]{3,2,1,0:T(8,128)S(1)}, f32[2,1,32,128]{3,2,1,0:T(8,128)S(1)}, u32[]{:S(2)}, u32[]{:S(2)}) collective-permute-start(f32[2,1,32,128]{3,2,1,0:T(8,128)S(1)} %get-tuple-element.110), channel_id=1, source_target_pairs={{0,1},{1,2},{2,3},{3,4},{4,5},{5,6},{6,7},{7,8},{8,9},{9,10},{10,1... | collective-permute-start | bytes 98312 | tf_op jit(solution)/shard_map/ppermute | solution.py:21
  312.2 8.5 %collective-permute-start.54 = (f32[2,1,32,128]{3,2,1,0:T(8,128)S(1)}, f32[2,1,32,128]{3,2,1,0:T(8,128)S(1)}, u32[]{:S(2)}, u32[]{:S(2)}) collective-permute-start(f32[2,1,32,128]{3,2,1,0:T(8,128)S(1)} %get-tuple-element.86), channel_id=1, source_target_pairs={{0,1},{1,2},{2,3},{3,4},{4,5},{5,6},{6,7},{7,8},{8,9},{9,10},{10,1... | collective-permute-start | bytes 98312 | tf_op jit(solution)/shard_map/ppermute | solution.py:21
  342.7 9.0 %collective-permute-start.68 = (f32[4,1,32,128]{3,2,1,0:T(8,128)S(1)}, f32[4,1,32,128]{3,2,1,0:T(8,128)S(1)}, u32[]{:S(2)}, u32[]{:S(2)}) collective-permute-start(f32[4,1,32,128]{3,2,1,0:T(8,128)S(1)} %get-tuple-element.35), channel_id=1, source_target_pairs={{0,1},{1,2},{2,3},{3,4},{4,5},{5,6},{6,7},{7,8},{8,9},{9,10},{10,1... | collective-permute-start | bytes 196616 | tf_op jit(solution)/shard_map/ppermute | solution.py:21
  354.5 8.7 %collective-permute-start.70 = (f32[4,1,32,128]{3,2,1,0:T(8,128)S(1)}, f32[4,1,32,128]{3,2,1,0:T(8,128)S(1)}, u32[]{:S(2)}, u32[]{:S(2)}) collective-permute-start(f32[4,1,32,128]{3,2,1,0:T(8,128)S(1)} %get-tuple-element.29), channel_id=1, source_target_pairs={{0,1},{1,2},{2,3},{3,4},{4,5},{5,6},{6,7},{7,8},{8,9},{9,10},{10,1... | collective-permute-start | bytes 196616 | tf_op jit(solution)/shard_map/ppermute | solution.py:21
  365.2 8.6 %collective-permute-start.72 = (f32[4,1,32,128]{3,2,1,0:T(8,128)S(1)}, f32[4,1,32,128]{3,2,1,0:T(8,128)S(1)}, u32[]{:S(2)}, u32[]{:S(2)}) collective-permute-start(f32[4,1,32,128]{3,2,1,0:T(8,128)S(1)} %get-tuple-element.23), channel_id=1, source_target_pairs={{0,1},{1,2},{2,3},{3,4},{4,5},{5,6},{6,7},{7,8},{8,9},{9,10},{10,1... | collective-permute-start | bytes 196616 | tf_op jit(solution)/shard_map/ppermute | solution.py:21
  375.9 8.6 %collective-permute-start.74 = (f32[4,1,32,128]{3,2,1,0:T(8,128)S(1)}, f32[4,1,32,128]{3,2,1,0:T(8,128)S(1)}, u32[]{:S(2)}, u32[]{:S(2)}) collective-permute-start(f32[4,1,32,128]{3,2,1,0:T(8,128)S(1)} %get-tuple-element.17), channel_id=1, source_target_pairs={{0,1},{1,2},{2,3},{3,4},{4,5},{5,6},{6,7},{7,8},{8,9},{9,10},{10,1... | collective-permute-start | bytes 196616 | tf_op jit(solution)/shard_map/ppermute | solution.py:21
  386.6 8.3 %collective-permute-start.76 = (f32[1,1,32,128]{3,2,1,0:T(8,128)S(1)}, f32[1,1,32,128]{3,2,1,0:T(8,128)S(1)}, u32[]{:S(2)}, u32[]{:S(2)}) collective-permute-start(f32[1,1,32,128]{3,2,1,0:T(8,128)S(1)} %get-tuple-element.293), channel_id=1, source_target_pairs={{0,1},{1,2},{2,3},{3,4},{4,5},{5,6},{6,7},{7,8},{8,9},{9,10},{10,1... | collective-permute-start | bytes 49160 | tf_op jit(solution)/shard_map/ppermute | solution.py:21
  472.6 8.9 %collective-permute-start.93 = (f32[2,1,32,128]{3,2,1,0:T(8,128)S(1)}, f32[2,1,32,128]{3,2,1,0:T(8,128)S(1)}, u32[]{:S(2)}, u32[]{:S(2)}) collective-permute-start(f32[2,1,32,128]{3,2,1,0:T(8,128)S(1)} %get-tuple-element.66), channel_id=1, source_target_pairs={{0,1},{1,2},{2,3},{3,4},{4,5},{5,6},{6,7},{7,8},{8,9},{9,10},{10,1... | collective-permute-start | bytes 98312 | tf_op jit(solution)/shard_map/ppermute | solution.py:21
  (75 other events, 514.8 us)
where the time goes:
time: 522 us; the launch traced here: 519 us
  starting transfers between devices  408 us (78%)
  waiting for transfers between devices  86.9 us (17%)
  other arithmetic  10.3 us (2%)
  local copies, waits for them, and re-layouts  10 us (2%)
    ppermute x49, starting transfers between devices, padded_2(): lax.ppermute(head, axis, [((i + 1) % count, i) for i in range(ends)])  243 us
    ppermute x49, starting transfers between devices, padded_2(): lax.ppermute(tail, axis, [(i, (i + 1) % count) for i in range(ends)])  160 us
    ppermute x49, waiting for transfers between devices, padded_2(): lax.ppermute(head, axis, [((i + 1) % count, i) for i in range(ends)])  60.3 us
    ppermute x49, waiting for transfers between devices, padded_2(): lax.ppermute(tail, axis, [(i, (i + 1) % count) for i in range(ends)])  14.1 us
    ppermute x3, waiting for transfers between devices, passed_along(): lax.ppermute(value, axis, [(source, source + steps) for source in range(f...  12.4 us
  transfers between devices with their start and end apart: 101, of which 53 were waited for; matrix products, arithmetic and copies ran while one was open for 2% of the time, Pallas kernels for 0%

commit v1 on v0

v1 whole, which is shorter than its diff:
```python
import jax
import jax.numpy as jnp
from jax import lax
from jax.experimental import pallas as pl
from jax.experimental.pallas import tpu as pltpu
from jax.sharding import PartitionSpec as P

CF = 4
SLAB = 4
EDGE = SLAB - 1
ROWS = 4

storage_rate = 2.0


def shifted(value, dt, ds):
    times = lax.axis_size("tm")
    slabs = lax.axis_size("space")
    pairs = [
        (t * slabs + s, ((t + dt) % times) * slabs + (s + ds) % slabs)
        for t in range(times)
        for s in range(slabs)
    ]
    return lax.ppermute(value, ("tm", "space"), pairs)


def call(kernel, name, outs, *args, scratch=()):
    in_vmem = [pltpu.with_memory_space_constraint(a, pltpu.VMEM) for a in args]
    spec = pl.BlockSpec(memory_space=pltpu.VMEM)
    return pl.pallas_call(
        kernel,
        out_shape=[pltpu.VMEM(shape, jnp.float32) for shape in outs],
        in_specs=[spec] * len(args),
        out_specs=[spec] * len(outs),
        scratch_shapes=[pltpu.VMEM(shape, jnp.float32) for shape in scratch],
        name=name,
        compiler_params=pltpu.CompilerParams(vmem_limit_bytes=16 * 2**20),
    )(*in_vmem)


PLANE = (ROWS, 8, 128)


def plane_of(ref, *at):
    return [ref[(*at, pl.ds(j, 8, stride=ROWS), slice(None))] for j in range(ROWS)]


def put_plane(ref, at, rows):
    for j in range(ROWS):
        ref[(*at, pl.ds(j, 8, stride=ROWS), slice(None))] = rows[j]


def x_lower(v):
    return pltpu.roll(v, 1, 1)


def x_upper(v):
    return pltpu.roll(v, 127, 1)


def y_lower(rows):
    return [pltpu.roll(rows[-1], 1, 0)] + rows[:-1]


def y_upper(rows):
    return rows[1:] + [pltpu.roll(rows[0], 7, 0)]


def rows_at(ref, *at):
    return [ref[(*at, j)] for j in range(ROWS)]


def put_rows(ref, at, rows):
    for j in range(ROWS):
        ref[(*at, j)] = rows[j]


WEST, EAST, SOUTH, NORTH, BELOW, ABOVE, STORAGE, FINE, COARSE, COARSEST = range(10)
REACH = SLAB + 2 * EDGE
FACTORS = {FINE: 1.0, COARSE: 1.0 / CF, COARSEST: 1.0 / (2 * CF)}


def step(coef, levels, window, source, put, near, far, right):
    count = len(levels)
    for turn in range(4):
        planes = REACH - 2 * turn
        out = [near, far, near, None][turn]
        held = [None, near, far, near][turn]
        for p in range(planes):
            at = p + turn
            links = [rows_at(coef, kind, at) for kind in range(6)]
            inverses = {level: rows_at(coef, level, at) for level in set(levels)}
            for b in range(count):
                if turn == 0:
                    lower, middle, upper = window(b, p), window(b, p + 1), window(b, p + 2)
                    stored = rows_at(coef, STORAGE, at)
                    factor = FACTORS[levels[b]]
                    if factor != 1.0:
                        stored = [s * factor for s in stored]
                    rhs = [s * v for s, v in zip(stored, middle)]
                    if source is not None:
                        rhs = [r + f for r, f in zip(rhs, source(b, p))]
                    if 0 < p < planes - 1:
                        put_rows(right, (b, p - 1), rhs)
                else:
                    lower, middle, upper = [rows_at(held, b, p + k) for k in range(3)]
                    rhs = rows_at(right, b, at - 1)
                south_of, north_of = y_lower(middle), y_upper(middle)
                result = []
                for j in range(ROWS):
                    west, east, south, north, below, above = [link[j] for link in links]
                    total = rhs[j] + (west * x_lower(middle[j]) + east * x_upper(middle[j]))
                    total = total + (south * south_of[j] + north * north_of[j])
                    total = total + (below * lower[j] + above * upper[j])
                    result.append(total * inverses[levels[b]][j])
                if out is None:
                    put(b, p, result)
                else:
                    put_rows(out, (b, p), result)


def scratch_of(count):
    return [(count, 10) + PLANE, (count, 8) + PLANE, (count, 8) + PLANE]


def windows(lo, own, hi):
    def window(b, p):
        if p < SLAB:
            return rows_at(lo, b, p)
        if p < 2 * SLAB:
            return rows_at(own, b, p - SLAB)
        return rows_at(hi, b, p - 2 * SLAB)

    return window


UP_GUESS, UP_FORCE, UP_X, UP_Y, UP_PORE, UP_Z = 0, 4, 10, 13, 16, 19
MESSAGE = 23


def prepare_kernel(forcing, guess, initial, porosity, permeability, up, down, up_later, down_later, on, own_force, own_guess, own_field):
    last_time = lax.axis_index("tm") == lax.axis_size("tm") - 1
    for z in range(SLAB):
        for b in range(2):
            for i in range(CF):
                rows = plane_of(forcing, b * CF + i, z)
                put_rows(own_force, (b, i, z), rows)
                for target, later, skip in ((up, up_later, 1), (down, down_later, 0)):
                    if 0 <= z - skip < EDGE:
                        if i == 0:
                            put_rows(target, (UP_FORCE + EDGE * b + z - skip,), rows)
                        else:
                            put_rows(later, (b, i - 1, z - skip), rows)
        rows = plane_of(guess, 0, z)
        put_rows(own_guess, (z,), rows)
        put_rows(up, (UP_GUESS + z,), rows)
        put_rows(down, (UP_GUESS + z,), rows)
        first, other = plane_of(initial, z), plane_of(guess, 1, z)
        put_rows(on, (z,), [jnp.where(last_time, a, b) for a, b in zip(first, other)])
        for kind in range(4):
            rows = plane_of(permeability, kind, z) if kind < 3 else plane_of(porosity, z)
            put_rows(own_field, (kind, z), rows)
            start = [UP_X, UP_Y, UP_Z, UP_PORE][kind]
            for target, skip in ((up, 1), (down, 0)):
                if kind == 2:
                    put_rows(target, (start + z,), rows)
                elif 0 <= z - skip < EDGE:
                    put_rows(target, (start + z - skip,), rows)


def harmonic(lower, upper):
    return [2.0 * a * b / (a + b) for a, b in zip(lower, upper)]


def coefficients(lo, hi, field, coef):
    position = lax.axis_index("space")
    column = lax.broadcasted_iota(jnp.int32, (8, 128), 1)
    row = lax.broadcasted_iota(jnp.int32, (8, 128), 0)
    zero = jnp.zeros((8, 128), jnp.float32)

    def held(kind, p):
        start = [UP_X, UP_Y, UP_Z, UP_PORE][kind]
        if kind == 2:
            p, width = p + 1, SLAB
        else:
            width = EDGE
        if p < width:
            return rows_at(lo, start + p)
        if p < width + SLAB:
            return rows_at(field, kind, p - width)
        return rows_at(hi, start + p - width - SLAB)

    above_before = None
    for p in range(REACH):
        kx, ky, kz, pore = [held(kind, p) for kind in range(4)]
        side = harmonic(kx, [x_upper(k) for k in kx])
        east_link = [jnp.where(column == 127, zero, v) for v in side]
        east = [jnp.where(column == 127, k, v) for k, v in zip(kx, side)]
        side = [x_lower(v) for v in side]
        west_link = [jnp.where(column == 0, zero, v) for v in side]
        west = [jnp.where(column == 0, k, v) for k, v in zip(kx, side)]
        side = harmonic(ky, y_upper(ky))
        north_link, north = list(side), list(side)
        north_link[-1] = jnp.where(row == 7, zero, side[-1])
        north[-1] = jnp.where(row == 7, ky[-1], side[-1])
        side = y_lower(side)
        south_link, south = list(side), list(side)
        south_link[0] = jnp.where(row == 0, zero, side[0])
        south[0] = jnp.where(row == 0, ky[0], side[0])
        below_link = below = above_before if p else harmonic(held(2, p - 1), kz)
        above_link = above = above_before = harmonic(kz, held(2, p + 1))
        if p == EDGE:
            floor = position == 0
            below = [jnp.where(floor, k, v) for k, v in zip(kz, below)]
            below_link = [jnp.where(floor, zero, v) for v in below_link]
        if p == EDGE + SLAB - 1:
            top = position == lax.axis_size("space") - 1
            above = [jnp.where(top, k, v) for k, v in zip(kz, above)]
            above_link = [jnp.where(top, zero, v) for v in above_link]
        for kind, rows in enumerate([west_link, east_link, south_link, north_link, below_link, above_link]):
            put_rows(coef, (kind, p), rows)
        stored = [storage_rate * v for v in pore]
        put_rows(coef, (STORAGE, p), stored)
        for j in range(ROWS):
            coupling = ((west[j] + east[j]) + (south[j] + north[j])) + (below[j] + above[j])
            for level, factor in FACTORS.items():
                coef[level, p, j] = 1.0 / (stored[j] * factor + coupling)


def first_kernel(guess, low, mid, high, lo, hi, force, field, coef, state, near, far, right):
    coefficients(lo, hi, field, coef)

    def window(b, p):
        part, at = divmod(p, SLAB)
        if b == 0:
            return rows_at([low, mid, high][part], at)
        return rows_at([lo, guess, hi][part], at)

    def source(b, p):
        if p < EDGE:
            return rows_at(lo, UP_FORCE + EDGE * b + p)
        if p < EDGE + SLAB:
            return rows_at(force, b, 0, p - EDGE)
        return rows_at(hi, UP_FORCE + EDGE * b + p - EDGE - SLAB)

    step(coef, [FINE, FINE], window, source, lambda b, p, rows: put_rows(state, (b, p), rows), near, far, right)


def early_kernel(section):
    def kernel(own, lo, hi, force, force_lo, force_hi, coef, state, near, far, right):
        def source(b, p):
            if p < EDGE:
                return rows_at(force_lo, b, section - 1, p)
            if p < EDGE + SLAB:
                return rows_at(force, b, section, p - EDGE)
            return rows_at(force_hi, b, section - 1, p - EDGE - SLAB)

        put = lambda b, p, rows: put_rows(state, (b, p), rows)
        step(coef, [FINE, FINE], windows(lo, own, hi), source, put, near, far, right)

    return kernel


def pass_kernel(relaxed, initial, on):
    last_time = lax.axis_index("tm") == lax.axis_size("tm") - 1
    for z in range(SLAB):
        rows = [jnp.where(last_time, a, b) for a, b in zip(plane_of(initial, z), rows_at(relaxed, 1, z))]
        put_rows(on, (z,), rows)


def change_kernel(arrived, mid, relaxed, guess, change):
    for z in range(SLAB):
        for j in range(ROWS):
            change[0, z, j] = arrived[z, j] - mid[z, j]
            change[1, z, j] = relaxed[0, z, j] - guess[z, j]


def late_kernel(own, lo, hi, coef, state, near, far, right):
    put = lambda b, p, rows: put_rows(state, (b, p), rows)
    step(coef, [FINE, FINE], windows(lo, own, hi), None, put, near, far, right)


def fine_kernel(early0, early1, early2, relaxed, late0, late1, late2, fine):
    for b in range(2):
        for z in range(SLAB):
            for i, (early, late) in enumerate(((early0, late0), (early1, late1), (early2, late2))):
                rows = [u + d for u, d in zip(rows_at(early, b, z), rows_at(late, b, z))]
                put_plane(fine, (b * CF + i, z), rows)
            put_plane(fine, (b * CF + CF - 1, z), rows_at(relaxed, b, z))


def last_kernel(change, lo, hi, relaxed, coef, last, on, near, far, right):
    last_time = lax.axis_index("tm") == lax.axis_size("tm") - 1

    def window(b, p):
        part, at = divmod(p, SLAB)
        return rows_at(change, 0, at) if part == 1 else rows_at([lo, None, hi][part], at)

    def put(b, p, rows):
        moved = rows_at(change, 1, p)
        rows = [a + d for a, d in zip(moved, rows)]
        put_rows(last, (p,), [u + d for u, d in zip(rows_at(relaxed, 1, p), rows)])
        put_rows(on, (p,), [jnp.where(last_time, 0.0, d) for d in rows])

    step(coef, [COARSE], window, None, put, near, far, right)


def again_kernel(
    low, mid, high, start_lo, start_hi, change_lo, change_hi, arrived, change, relaxed, coef,
    moved, again, third, near, far, right,
):
    def window(b, p):
        part, at = divmod(p, SLAB)
        epsilon = rows_at([low, mid, high][part], at)
        if b == 0:
            return epsilon
        if part == 1:
            start = rows_at(arrived, at)
        else:
            start = [
                u + d
                for u, d in zip(
                    rows_at([start_lo, None, start_hi][part], at), rows_at([change_lo, None, change_hi][part], 0, at)
                )
            ]
        return [u + e for u, e in zip(start, epsilon)]

    def put(b, p, rows):
        if b == 0:
            put_rows(moved, (p,), rows)
            point = [u + d for u, d in zip(rows_at(relaxed, 0, p), rows_at(change, 0, p))]
            put_rows(again, (p,), [u + d for u, d in zip(point, rows)])
        else:
            put_rows(third, (p,), rows)

    step(coef, [COARSE, COARSEST], window, None, put, near, far, right)


def source_kernel(moved, lo, hi, last, again, third, coef, state, source, near, far, right):
    def window(b, p):
        part, at = divmod(p, SLAB)
        return rows_at([lo, moved, hi][part], at)

    def put(b, p, rows):
        point = rows_at(last, p)
        put_plane(source, (0, p), [(d + u) - w for d, u, w in zip(rows, point, rows_at(third, p))])
        put_plane(state, (1, p), point)
        put_plane(state, (0, p), rows_at(again, p))

    step(coef, [COARSE], window, None, put, near, far, right)


def on_device(forcing, c_guess, initial, porosity, permeability):
    four = (SLAB,) + PLANE
    both = (2,) + four

    up, down, up_later, down_later, on, force, guess, field = call(
        prepare_kernel,
        "prepare",
        [
            (MESSAGE,) + PLANE,
            (MESSAGE,) + PLANE,
            (2, CF - 1, EDGE) + PLANE,
            (2, CF - 1, EDGE) + PLANE,
            four,
            (2, CF) + four,
            four,
            (4,) + four,
        ],
        forcing,
        c_guess,
        initial,
        porosity,
        permeability,
    )
    lo, hi = shifted(up, 0, 1), shifted(down, 0, -1)
    low, mid, high = shifted(on, 1, 1), shifted(on, 1, 0), shifted(on, 1, -1)
    force_lo, force_hi = shifted(up_later, 0, 1), shifted(down_later, 0, -1)
    coef, state = call(
        first_kernel, "first", [(10, REACH) + PLANE, both], guess, low, mid, high, lo, hi, force, field,
        scratch=scratch_of(2),
    )
    early = [state]
    for section in range(1, CF):
        state_lo, state_hi = shifted(state, 0, 1), shifted(state, 0, -1)
        (state,) = call(
            early_kernel(section), f"early{section}", [both], state, state_lo, state_hi, force, force_lo, force_hi,
            coef, scratch=scratch_of(2),
        )
        early.append(state)
    relaxed = early[-1]

    (on,) = call(pass_kernel, "pass", [four], relaxed, initial)
    arrived = shifted(on, 1, 0)
    (change,) = call(change_kernel, "change", [both], arrived, mid, relaxed, guess)
    start_lo, start_hi = low, high
    late = []
    change_lo = change_hi = None
    for section in range(CF):
        state_lo, state_hi = shifted(change, 0, 1), shifted(change, 0, -1)
        if section == 0:
            change_lo, change_hi = state_lo, state_hi
        (change,) = call(
            late_kernel, f"late{section}", [both], change, state_lo, state_hi, coef, scratch=scratch_of(2)
        )
        late.append(change)
    (fine_state,) = call(fine_kernel, "fine", [forcing.shape], *early, *late[: CF - 1])

    state_lo, state_hi = shifted(change[0], 0, 1), shifted(change[0], 0, -1)
    last, on = call(
        last_kernel, "last", [four, four], change, state_lo, state_hi, relaxed, coef, scratch=scratch_of(1)
    )
    low, mid, high = shifted(on, 1, 1), shifted(on, 1, 0), shifted(on, 1, -1)
    moved, again, third = call(
        again_kernel, "again", [four] * 3, low, mid, high, start_lo, start_hi, change_lo, change_hi,
        arrived, change, relaxed, coef, scratch=scratch_of(2),
    )
    state_lo, state_hi = shifted(moved, 0, 1), shifted(moved, 0, -1)
    coarse_state, coarse_source = call(
        source_kernel, "source", [(2,) + initial.shape, (1,) + initial.shape], moved, state_lo, state_hi, last, again,
        third, coef, scratch=scratch_of(1),
    )
    return (fine_state, coarse_state, coarse_source)


def solution(mesh):
    return jax.shard_map(
        on_device,
        mesh=mesh,
        in_specs=(
            P("tm", "space", None, None),
            P("tm", "space", None, None),
            P("space", None, None),
            P("space", None, None),
            P(None, "space", None, None),
        ),
        out_specs=(
            P("tm", "space", None, None),
            P("tm", "space", None, None),
            P("tm", "space", None, None),
        ),
        check_vma=False,
    )
```

time: 522 us -> 138 us (0.26)
  the two profiles are of different devices: /device:TPU:136 before, /device:TPU:0 now
where the time goes in v1:
time: 138 us; the launch traced here: 137 us
  waiting for transfers between devices  91.6 us (66%)
  starting transfers between devices  31.6 us (23%)
  Pallas kernels  6.73 us (5%)
  local copies, waits for them, and re-layouts  6.63 us (5%)
    ppermute x29, waiting for transfers between devices, shifted(): return lax.ppermute(value, ('tm', 'space'), pairs)  91.6 us
    ppermute x29, starting transfers between devices, shifted(): return lax.ppermute(value, ('tm', 'space'), pairs)  31.6 us
    pallas_call x15, Pallas kernels, call(): pl.pallas_call(kernel, out_shape=[pltpu.VMEM(shape, jnp.float32) for shap...  6.73 us
    unnamed x13, local copies, waits for them, and re-layouts  6.63 us
  transfers between devices with their start and end apart: 29, of which 24 were waited for; matrix products, arithmetic and copies ran while one was open for 1% of the time, Pallas kernels for 1%

profile of v1, /device:TPU:0, one launch (start us, length us, event | category | flops | bytes accessed | tf_op | source)
XLA Modules:
  0.0 137.4 jit_solution(11936874222800760667)
XLA Ops:
  5.4 5.3 %collective-permute-start.4 = (f32[23,4,8,128]{3,2,1,0:T(8,128)S(1)}, f32[23,4,8,128]{3,2,1,0:T(8,128)S(1)}, u32[]{:S(2)}, u32[]{:S(2)}) collective-permute-start(f32[23,4,8,128]{3,2,1,0:T(8,128)S(1)} %get-tuple-element.23), channel_id=1, source_target_pairs={{0,15},{1,0},{2,1},{3,2},{4,3},{5,4},{6,5},{7,6},{8,7},{9,8},{10,9... | collective-permute-start | bytes 1130504 | tf_op jit(solution)/shard_map/ppermute | solution.py:24
  10.8 5.3 %collective-permute-start.8 = (f32[2,3,3,4,8,128]{5,4,3,2,1,0:T(8,128)S(1)}, f32[2,3,3,4,8,128]{5,4,3,2,1,0:T(8,128)S(1)}, u32[]{:S(2)}, u32[]{:S(2)}) collective-permute-start(f32[2,3,3,4,8,128]{5,4,3,2,1,0:T(8,128)S(1)} %get-tuple-element.28), channel_id=1, source_target_pairs={{0,15},{1,0},{2,1},{3,2},{4,3},{5,4},{6,5},{7,6},{8,7},{9,8},{10,9... | collective-permute-start | bytes 884744 | tf_op jit(solution)/shard_map/ppermute | solution.py:24
  16.1 3.1 %collective-permute-done.2.high.start_hi = f32[4,4,8,128]{3,2,1,0:T(8,128)S(1)} collective-permute-done((f32[4,4,8,128]{3,2,1,0:T(8,128)S(1)}, f32[4,4,8,128]{3,2,1,0:T(8,128)S(1)}, u32[]{:S(2)}, u32[]{:S(2)}) %collective-permute-start.2) | collective-permute-done | bytes 65568 | tf_op jit(solution)/shard_map/ppermute | solution.py:24
  19.2 7.3 %collective-permute-done.1.mid = f32[4,4,8,128]{3,2,1,0:T(8,128)S(1)} collective-permute-done((f32[4,4,8,128]{3,2,1,0:T(8,128)S(1)}, f32[4,4,8,128]{3,2,1,0:T(8,128)S(1)}, u32[]{:S(2)}, u32[]{:S(2)}) %collective-permute-start.1) | collective-permute-done | bytes 65568 | tf_op jit(solution)/shard_map/ppermute | solution.py:24
  26.5 9.2 %collective-permute-done.low.start_lo = f32[4,4,8,128]{3,2,1,0:T(8,128)S(1)} collective-permute-done((f32[4,4,8,128]{3,2,1,0:T(8,128)S(1)}, f32[4,4,8,128]{3,2,1,0:T(8,128)S(1)}, u32[]{:S(2)}, u32[]{:S(2)}) %collective-permute-start) | collective-permute-done | bytes 65568 | tf_op jit(solution)/shard_map/ppermute | solution.py:24
  36.6 3.6 %collective-permute-start.6 = (f32[2,4,4,8,128]{4,3,2,1,0:T(8,128)S(1)}, f32[2,4,4,8,128]{4,3,2,1,0:T(8,128)S(1)}, u32[]{:S(2)}, u32[]{:S(2)}) collective-permute-start(f32[2,4,4,8,128]{4,3,2,1,0:T(8,128)S(1)} %get-tuple-element.26.own.early0), channel_id=1, source_target_pairs={{0,15},{1,0},{2,1},{3,2},{4,3},{5,4},{6,5},{7,6},{8,7},{9,8},{10,9... | collective-permute-start | bytes 393224 | tf_op jit(solution)/shard_map/ppermute | solution.py:24
  40.2 2.5 %collective-permute-done.6.hi = f32[2,4,4,8,128]{4,3,2,1,0:T(8,128)S(1)} collective-permute-done((f32[2,4,4,8,128]{4,3,2,1,0:T(8,128)S(1)}, f32[2,4,4,8,128]{4,3,2,1,0:T(8,128)S(1)}, u32[]{:S(2)}, u32[]{:S(2)}) %collective-permute-start.6) | collective-permute-done | bytes 131104 | tf_op jit(solution)/shard_map/ppermute | solution.py:24
  42.7 5.8 %collective-permute-done.5.lo = f32[2,4,4,8,128]{4,3,2,1,0:T(8,128)S(1)} collective-permute-done((f32[2,4,4,8,128]{4,3,2,1,0:T(8,128)S(1)}, f32[2,4,4,8,128]{4,3,2,1,0:T(8,128)S(1)}, u32[]{:S(2)}, u32[]{:S(2)}) %collective-permute-start.5) | collective-permute-done | bytes 131104 | tf_op jit(solution)/shard_map/ppermute | solution.py:24
  49.2 2.0 %collective-permute-start.9 = (f32[2,4,4,8,128]{4,3,2,1,0:T(8,128)S(1)}, f32[2,4,4,8,128]{4,3,2,1,0:T(8,128)S(1)}, u32[]{:S(2)}, u32[]{:S(2)}) collective-permute-start(f32[2,4,4,8,128]{4,3,2,1,0:T(8,128)S(1)} %early1.1.own), channel_id=1, source_target_pairs={{0,1},{1,2},{2,3},{3,4},{4,5},{5,6},{6,7},{7,8},{8,9},{9,10},{10,1... | collective-permute-start | bytes 393224 | tf_op jit(solution)/shard_map/ppermute | solution.py:24
  51.2 2.9 %collective-permute-done.10.hi = f32[2,4,4,8,128]{4,3,2,1,0:T(8,128)S(1)} collective-permute-done((f32[2,4,4,8,128]{4,3,2,1,0:T(8,128)S(1)}, f32[2,4,4,8,128]{4,3,2,1,0:T(8,128)S(1)}, u32[]{:S(2)}, u32[]{:S(2)}) %collective-permute-start.10) | collective-permute-done | bytes 131104 | tf_op jit(solution)/shard_map/ppermute | solution.py:24
  54.2 3.4 %collective-permute-done.9.lo = f32[2,4,4,8,128]{4,3,2,1,0:T(8,128)S(1)} collective-permute-done((f32[2,4,4,8,128]{4,3,2,1,0:T(8,128)S(1)}, f32[2,4,4,8,128]{4,3,2,1,0:T(8,128)S(1)}, u32[]{:S(2)}, u32[]{:S(2)}) %collective-permute-start.9) | collective-permute-done | bytes 131104 | tf_op jit(solution)/shard_map/ppermute | solution.py:24
  58.3 2.0 %collective-permute-start.11 = (f32[2,4,4,8,128]{4,3,2,1,0:T(8,128)S(1)}, f32[2,4,4,8,128]{4,3,2,1,0:T(8,128)S(1)}, u32[]{:S(2)}, u32[]{:S(2)}) collective-permute-start(f32[2,4,4,8,128]{4,3,2,1,0:T(8,128)S(1)} %early2.1.own), channel_id=1, source_target_pairs={{0,1},{1,2},{2,3},{3,4},{4,5},{5,6},{6,7},{7,8},{8,9},{9,10},{10,1... | collective-permute-start | bytes 393224 | tf_op jit(solution)/shard_map/ppermute | solution.py:24
  60.3 2.9 %collective-permute-done.12.hi = f32[2,4,4,8,128]{4,3,2,1,0:T(8,128)S(1)} collective-permute-done((f32[2,4,4,8,128]{4,3,2,1,0:T(8,128)S(1)}, f32[2,4,4,8,128]{4,3,2,1,0:T(8,128)S(1)}, u32[]{:S(2)}, u32[]{:S(2)}) %collective-permute-start.12) | collective-permute-done | bytes 131104 | tf_op jit(solution)/shard_map/ppermute | solution.py:24
  63.3 3.6 %collective-permute-done.11.lo = f32[2,4,4,8,128]{4,3,2,1,0:T(8,128)S(1)} collective-permute-done((f32[2,4,4,8,128]{4,3,2,1,0:T(8,128)S(1)}, f32[2,4,4,8,128]{4,3,2,1,0:T(8,128)S(1)}, u32[]{:S(2)}, u32[]{:S(2)}) %collective-permute-start.11) | collective-permute-done | bytes 131104 | tf_op jit(solution)/shard_map/ppermute | solution.py:24
  67.5 4.9 %collective-permute-done.13.arrived = f32[4,4,8,128]{3,2,1,0:T(8,128)S(1)} collective-permute-done((f32[4,4,8,128]{3,2,1,0:T(8,128)S(1)}, f32[4,4,8,128]{3,2,1,0:T(8,128)S(1)}, u32[]{:S(2)}, u32[]{:S(2)}) %collective-permute-start.13) | collective-permute-done | bytes 65568 | tf_op jit(solution)/shard_map/ppermute | solution.py:24
  72.5 2.0 %collective-permute-start.14 = (f32[2,4,4,8,128]{4,3,2,1,0:T(8,128)S(1)}, f32[2,4,4,8,128]{4,3,2,1,0:T(8,128)S(1)}, u32[]{:S(2)}, u32[]{:S(2)}) collective-permute-start(f32[2,4,4,8,128]{4,3,2,1,0:T(8,128)S(1)} %change.1.own), channel_id=1, source_target_pairs={{0,1},{1,2},{2,3},{3,4},{4,5},{5,6},{6,7},{7,8},{8,9},{9,10},{10,1... | collective-permute-start | bytes 393224 | tf_op jit(solution)/shard_map/ppermute | solution.py:24
  74.5 2.9 %collective-permute-done.15.hi.change_hi = f32[2,4,4,8,128]{4,3,2,1,0:T(8,128)S(1)} collective-permute-done((f32[2,4,4,8,128]{4,3,2,1,0:T(8,128)S(1)}, f32[2,4,4,8,128]{4,3,2,1,0:T(8,128)S(1)}, u32[]{:S(2)}, u32[]{:S(2)}) %collective-permute-start.15) | collective-permute-done | bytes 131104 | tf_op jit(solution)/shard_map/ppermute | solution.py:24
  77.5 3.4 %collective-permute-done.14.lo.change_lo = f32[2,4,4,8,128]{4,3,2,1,0:T(8,128)S(1)} collective-permute-done((f32[2,4,4,8,128]{4,3,2,1,0:T(8,128)S(1)}, f32[2,4,4,8,128]{4,3,2,1,0:T(8,128)S(1)}, u32[]{:S(2)}, u32[]{:S(2)}) %collective-permute-start.14) | collective-permute-done | bytes 131104 | tf_op jit(solution)/shard_map/ppermute | solution.py:24
  81.6 2.0 %collective-permute-start.16 = (f32[2,4,4,8,128]{4,3,2,1,0:T(8,128)S(1)}, f32[2,4,4,8,128]{4,3,2,1,0:T(8,128)S(1)}, u32[]{:S(2)}, u32[]{:S(2)}) collective-permute-start(f32[2,4,4,8,128]{4,3,2,1,0:T(8,128)S(1)} %late0.1.own), channel_id=1, source_target_pairs={{0,1},{1,2},{2,3},{3,4},{4,5},{5,6},{6,7},{7,8},{8,9},{9,10},{10,1... | collective-permute-start | bytes 393224 | tf_op jit(solution)/shard_map/ppermute | solution.py:24
  83.6 2.9 %collective-permute-done.17.hi = f32[2,4,4,8,128]{4,3,2,1,0:T(8,128)S(1)} collective-permute-done((f32[2,4,4,8,128]{4,3,2,1,0:T(8,128)S(1)}, f32[2,4,4,8,128]{4,3,2,1,0:T(8,128)S(1)}, u32[]{:S(2)}, u32[]{:S(2)}) %collective-permute-start.17) | collective-permute-done | bytes 131104 | tf_op jit(solution)/shard_map/ppermute | solution.py:24
  86.6 3.4 %collective-permute-done.16.lo = f32[2,4,4,8,128]{4,3,2,1,0:T(8,128)S(1)} collective-permute-done((f32[2,4,4,8,128]{4,3,2,1,0:T(8,128)S(1)}, f32[2,4,4,8,128]{4,3,2,1,0:T(8,128)S(1)}, u32[]{:S(2)}, u32[]{:S(2)}) %collective-permute-start.16) | collective-permute-done | bytes 131104 | tf_op jit(solution)/shard_map/ppermute | solution.py:24
  90.7 2.0 %collective-permute-start.18 = (f32[2,4,4,8,128]{4,3,2,1,0:T(8,128)S(1)}, f32[2,4,4,8,128]{4,3,2,1,0:T(8,128)S(1)}, u32[]{:S(2)}, u32[]{:S(2)}) collective-permute-start(f32[2,4,4,8,128]{4,3,2,1,0:T(8,128)S(1)} %late1.1.own), channel_id=1, source_target_pairs={{0,1},{1,2},{2,3},{3,4},{4,5},{5,6},{6,7},{7,8},{8,9},{9,10},{10,1... | collective-permute-start | bytes 393224 | tf_op jit(solution)/shard_map/ppermute | solution.py:24
  92.7 3.3 %collective-permute-done.19.hi = f32[2,4,4,8,128]{4,3,2,1,0:T(8,128)S(1)} collective-permute-done((f32[2,4,4,8,128]{4,3,2,1,0:T(8,128)S(1)}, f32[2,4,4,8,128]{4,3,2,1,0:T(8,128)S(1)}, u32[]{:S(2)}, u32[]{:S(2)}) %collective-permute-start.19) | collective-permute-done | bytes 131104 | tf_op jit(solution)/shard_map/ppermute | solution.py:24
  96.0 3.4 %collective-permute-done.18.lo = f32[2,4,4,8,128]{4,3,2,1,0:T(8,128)S(1)} collective-permute-done((f32[2,4,4,8,128]{4,3,2,1,0:T(8,128)S(1)}, f32[2,4,4,8,128]{4,3,2,1,0:T(8,128)S(1)}, u32[]{:S(2)}, u32[]{:S(2)}) %collective-permute-start.18) | collective-permute-done | bytes 131104 | tf_op jit(solution)/shard_map/ppermute | solution.py:24
  102.1 3.5 %collective-permute-done.21.hi = f32[2,4,4,8,128]{4,3,2,1,0:T(8,128)S(1)} collective-permute-done((f32[2,4,4,8,128]{4,3,2,1,0:T(8,128)S(1)}, f32[2,4,4,8,128]{4,3,2,1,0:T(8,128)S(1)}, u32[]{:S(2)}, u32[]{:S(2)}) %collective-permute-start.21) | collective-permute-done | bytes 131104 | tf_op jit(solution)/shard_map/ppermute | solution.py:24
  105.6 3.4 %collective-permute-done.20.lo = f32[2,4,4,8,128]{4,3,2,1,0:T(8,128)S(1)} collective-permute-done((f32[2,4,4,8,128]{4,3,2,1,0:T(8,128)S(1)}, f32[2,4,4,8,128]{4,3,2,1,0:T(8,128)S(1)}, u32[]{:S(2)}, u32[]{:S(2)}) %collective-permute-start.20) | collective-permute-done | bytes 131104 | tf_op jit(solution)/shard_map/ppermute | solution.py:24
  111.8 2.2 %collective-permute-done.23.hi = f32[4,4,8,128]{3,2,1,0:T(8,128)S(1)} collective-permute-done((f32[4,4,8,128]{3,2,1,0:T(8,128)S(1)}, f32[4,4,8,128]{3,2,1,0:T(8,128)S(1)}, u32[]{:S(2)}, u32[]{:S(2)}) %collective-permute-start.23) | collective-permute-done | bytes 65568 | tf_op jit(solution)/shard_map/ppermute | solution.py:24
  114.0 3.4 %collective-permute-done.22.lo = f32[4,4,8,128]{3,2,1,0:T(8,128)S(1)} collective-permute-done((f32[4,4,8,128]{3,2,1,0:T(8,128)S(1)}, f32[4,4,8,128]{3,2,1,0:T(8,128)S(1)}, u32[]{:S(2)}, u32[]{:S(2)}) %collective-permute-start.22) | collective-permute-done | bytes 65568 | tf_op jit(solution)/shard_map/ppermute | solution.py:24
  118.2 5.4 %collective-permute-done.26.high = f32[4,4,8,128]{3,2,1,0:T(8,128)S(1)} collective-permute-done((f32[4,4,8,128]{3,2,1,0:T(8,128)S(1)}, f32[4,4,8,128]{3,2,1,0:T(8,128)S(1)}, u32[]{:S(2)}, u32[]{:S(2)}) %collective-permute-start.26) | collective-permute-done | bytes 65568 | tf_op jit(solution)/shard_map/ppermute | solution.py:24
  123.7 3.7 %collective-permute-done.24.low = f32[4,4,8,128]{3,2,1,0:T(8,128)S(1)} collective-permute-done((f32[4,4,8,128]{3,2,1,0:T(8,128)S(1)}, f32[4,4,8,128]{3,2,1,0:T(8,128)S(1)}, u32[]{:S(2)}, u32[]{:S(2)}) %collective-permute-start.24) | collective-permute-done | bytes 65568 | tf_op jit(solution)/shard_map/ppermute | solution.py:24
  128.0 2.0 %collective-permute-start.27 = (f32[4,4,8,128]{3,2,1,0:T(8,128)S(1)}, f32[4,4,8,128]{3,2,1,0:T(8,128)S(1)}, u32[]{:S(2)}, u32[]{:S(2)}) collective-permute-start(f32[4,4,8,128]{3,2,1,0:T(8,128)S(1)} %get-tuple-element.31.moved), channel_id=1, source_target_pairs={{0,1},{1,2},{2,3},{3,4},{4,5},{5,6},{6,7},{7,8},{8,9},{9,10},{10,1... | collective-permute-start | bytes 196616 | tf_op jit(solution)/shard_map/ppermute | solution.py:24
  132.3 3.4 %collective-permute-done.27.lo = f32[4,4,8,128]{3,2,1,0:T(8,128)S(1)} collective-permute-done((f32[4,4,8,128]{3,2,1,0:T(8,128)S(1)}, f32[4,4,8,128]{3,2,1,0:T(8,128)S(1)}, u32[]{:S(2)}, u32[]{:S(2)}) %collective-permute-start.27) | collective-permute-done | bytes 65568 | tf_op jit(solution)/shard_map/ppermute | solution.py:24
  (55 shorter events, 20.0 us)
Async XLA Ops:
  0.6 1.0 copy-start
  2.5 0.9 copy-start.2
  3.4 0.9 copy-start.3
  5.3 30.4 %collective-permute-start.3 = (f32[23,4,8,128]{3,2,1,0:T(8,128)S(1)}, f32[23,4,8,128]{3,2,1,0:T(8,128)S(1)}, u32[]{:S(2)}, u32[]{:S(2)}) collective-permute-start(f32[23,4,8,128]{3,2,1,0:T(8,128)S(1)} %get-tuple-element.22), channel_id=1, source_target_pairs={{0,1},{1,2},{2,3},{3,4},{4,5},{5,6},{6,7},{7,8},{8,9},{9,10},{10,1... | collective-permute-start | bytes 1130504 | tf_op jit(solution)/shard_map/ppermute | solution.py:24
  5.4 30.3 %collective-permute-start.4 = (f32[23,4,8,128]{3,2,1,0:T(8,128)S(1)}, f32[23,4,8,128]{3,2,1,0:T(8,128)S(1)}, u32[]{:S(2)}, u32[]{:S(2)}) collective-permute-start(f32[23,4,8,128]{3,2,1,0:T(8,128)S(1)} %get-tuple-element.23), channel_id=1, source_target_pairs={{0,15},{1,0},{2,1},{3,2},{4,3},{5,4},{6,5},{7,6},{8,7},{9,8},{10,9... | collective-permute-start | bytes 1130504 | tf_op jit(solution)/shard_map/ppermute | solution.py:24
  10.8 8.4 %collective-permute-start.2 = (f32[4,4,8,128]{3,2,1,0:T(8,128)S(1)}, f32[4,4,8,128]{3,2,1,0:T(8,128)S(1)}, u32[]{:S(2)}, u32[]{:S(2)}) collective-permute-start(f32[4,4,8,128]{3,2,1,0:T(8,128)S(1)} %get-tuple-element.21), channel_id=1, source_target_pairs={{0,31},{1,16},{2,17},{3,18},{4,19},{5,20},{6,21},{7,22},{8,23},{9,... | collective-permute-start | bytes 196616 | tf_op jit(solution)/shard_map/ppermute | solution.py:24
  10.8 29.5 %collective-permute-start.7 = (f32[2,3,3,4,8,128]{5,4,3,2,1,0:T(8,128)S(1)}, f32[2,3,3,4,8,128]{5,4,3,2,1,0:T(8,128)S(1)}, u32[]{:S(2)}, u32[]{:S(2)}) collective-permute-start(f32[2,3,3,4,8,128]{5,4,3,2,1,0:T(8,128)S(1)} %get-tuple-element.27), channel_id=1, source_target_pairs={{0,1},{1,2},{2,3},{3,4},{4,5},{5,6},{6,7},{7,8},{8,9},{9,10},{10,1... | collective-permute-start | bytes 884744 | tf_op jit(solution)/shard_map/ppermute | solution.py:24
  10.8 29.5 %collective-permute-start.8 = (f32[2,3,3,4,8,128]{5,4,3,2,1,0:T(8,128)S(1)}, f32[2,3,3,4,8,128]{5,4,3,2,1,0:T(8,128)S(1)}, u32[]{:S(2)}, u32[]{:S(2)}) collective-permute-start(f32[2,3,3,4,8,128]{5,4,3,2,1,0:T(8,128)S(1)} %get-tuple-element.28), channel_id=1, source_target_pairs={{0,15},{1,0},{2,1},{3,2},{4,3},{5,4},{6,5},{7,6},{8,7},{9,8},{10,9... | collective-permute-start | bytes 884744 | tf_op jit(solution)/shard_map/ppermute | solution.py:24
  19.2 7.3 %collective-permute-start.1 = (f32[4,4,8,128]{3,2,1,0:T(8,128)S(1)}, f32[4,4,8,128]{3,2,1,0:T(8,128)S(1)}, u32[]{:S(2)}, u32[]{:S(2)}) collective-permute-start(f32[4,4,8,128]{3,2,1,0:T(8,128)S(1)} %get-tuple-element.21), channel_id=1, source_target_pairs={{0,16},{1,17},{2,18},{3,19},{4,20},{5,21},{6,22},{7,23},{8,24},{9,... | collective-permute-start | bytes 196616 | tf_op jit(solution)/shard_map/ppermute | solution.py:24
  26.5 9.2 %collective-permute-start = (f32[4,4,8,128]{3,2,1,0:T(8,128)S(1)}, f32[4,4,8,128]{3,2,1,0:T(8,128)S(1)}, u32[]{:S(2)}, u32[]{:S(2)}) collective-permute-start(f32[4,4,8,128]{3,2,1,0:T(8,128)S(1)} %get-tuple-element.21), channel_id=1, source_target_pairs={{0,17},{1,18},{2,19},{3,20},{4,21},{5,22},{6,23},{7,24},{8,25},{9,... | collective-permute-start | bytes 196616 | tf_op jit(solution)/shard_map/ppermute | solution.py:24
  36.6 6.1 %collective-permute-start.6 = (f32[2,4,4,8,128]{4,3,2,1,0:T(8,128)S(1)}, f32[2,4,4,8,128]{4,3,2,1,0:T(8,128)S(1)}, u32[]{:S(2)}, u32[]{:S(2)}) collective-permute-start(f32[2,4,4,8,128]{4,3,2,1,0:T(8,128)S(1)} %get-tuple-element.26.own.early0), channel_id=1, source_target_pairs={{0,15},{1,0},{2,1},{3,2},{4,3},{5,4},{6,5},{7,6},{8,7},{9,8},{10,9... | collective-permute-start | bytes 393224 | tf_op jit(solution)/shard_map/ppermute | solution.py:24
  40.2 8.3 %collective-permute-start.5 = (f32[2,4,4,8,128]{4,3,2,1,0:T(8,128)S(1)}, f32[2,4,4,8,128]{4,3,2,1,0:T(8,128)S(1)}, u32[]{:S(2)}, u32[]{:S(2)}) collective-permute-start(f32[2,4,4,8,128]{4,3,2,1,0:T(8,128)S(1)} %get-tuple-element.26.own.early0), channel_id=1, source_target_pairs={{0,1},{1,2},{2,3},{3,4},{4,5},{5,6},{6,7},{7,8},{8,9},{9,10},{10,1... | collective-permute-start | bytes 393224 | tf_op jit(solution)/shard_map/ppermute | solution.py:24
  49.1 5.0 %collective-permute-start.10 = (f32[2,4,4,8,128]{4,3,2,1,0:T(8,128)S(1)}, f32[2,4,4,8,128]{4,3,2,1,0:T(8,128)S(1)}, u32[]{:S(2)}, u32[]{:S(2)}) collective-permute-start(f32[2,4,4,8,128]{4,3,2,1,0:T(8,128)S(1)} %early1.1.own), channel_id=1, source_target_pairs={{0,15},{1,0},{2,1},{3,2},{4,3},{5,4},{6,5},{7,6},{8,7},{9,8},{10,9... | collective-permute-start | bytes 393224 | tf_op jit(solution)/shard_map/ppermute | solution.py:24
  49.2 8.4 %collective-permute-start.9 = (f32[2,4,4,8,128]{4,3,2,1,0:T(8,128)S(1)}, f32[2,4,4,8,128]{4,3,2,1,0:T(8,128)S(1)}, u32[]{:S(2)}, u32[]{:S(2)}) collective-permute-start(f32[2,4,4,8,128]{4,3,2,1,0:T(8,128)S(1)} %early1.1.own), channel_id=1, source_target_pairs={{0,1},{1,2},{2,3},{3,4},{4,5},{5,6},{6,7},{7,8},{8,9},{9,10},{10,1... | collective-permute-start | bytes 393224 | tf_op jit(solution)/shard_map/ppermute | solution.py:24
  58.2 5.0 %collective-permute-start.12 = (f32[2,4,4,8,128]{4,3,2,1,0:T(8,128)S(1)}, f32[2,4,4,8,128]{4,3,2,1,0:T(8,128)S(1)}, u32[]{:S(2)}, u32[]{:S(2)}) collective-permute-start(f32[2,4,4,8,128]{4,3,2,1,0:T(8,128)S(1)} %early2.1.own), channel_id=1, source_target_pairs={{0,15},{1,0},{2,1},{3,2},{4,3},{5,4},{6,5},{7,6},{8,7},{9,8},{10,9... | collective-permute-start | bytes 393224 | tf_op jit(solution)/shard_map/ppermute | solution.py:24
  58.3 8.5 %collective-permute-start.11 = (f32[2,4,4,8,128]{4,3,2,1,0:T(8,128)S(1)}, f32[2,4,4,8,128]{4,3,2,1,0:T(8,128)S(1)}, u32[]{:S(2)}, u32[]{:S(2)}) collective-permute-start(f32[2,4,4,8,128]{4,3,2,1,0:T(8,128)S(1)} %early2.1.own), channel_id=1, source_target_pairs={{0,1},{1,2},{2,3},{3,4},{4,5},{5,6},{6,7},{7,8},{8,9},{9,10},{10,1... | collective-permute-start | bytes 393224 | tf_op jit(solution)/shard_map/ppermute | solution.py:24
  67.5 4.9 %collective-permute-start.13 = (f32[4,4,8,128]{3,2,1,0:T(8,128)S(1)}, f32[4,4,8,128]{3,2,1,0:T(8,128)S(1)}, u32[]{:S(2)}, u32[]{:S(2)}) collective-permute-start(f32[4,4,8,128]{3,2,1,0:T(8,128)S(1)} %pass.1), channel_id=1, source_target_pairs={{0,16},{1,17},{2,18},{3,19},{4,20},{5,21},{6,22},{7,23},{8,24},{9,... | collective-permute-start | bytes 196616 | tf_op jit(solution)/shard_map/ppermute | solution.py:24
  72.4 5.0 %collective-permute-start.15 = (f32[2,4,4,8,128]{4,3,2,1,0:T(8,128)S(1)}, f32[2,4,4,8,128]{4,3,2,1,0:T(8,128)S(1)}, u32[]{:S(2)}, u32[]{:S(2)}) collective-permute-start(f32[2,4,4,8,128]{4,3,2,1,0:T(8,128)S(1)} %change.1.own), channel_id=1, source_target_pairs={{0,15},{1,0},{2,1},{3,2},{4,3},{5,4},{6,5},{7,6},{8,7},{9,8},{10,9... | collective-permute-start | bytes 393224 | tf_op jit(solution)/shard_map/ppermute | solution.py:24
  72.5 8.4 %collective-permute-start.14 = (f32[2,4,4,8,128]{4,3,2,1,0:T(8,128)S(1)}, f32[2,4,4,8,128]{4,3,2,1,0:T(8,128)S(1)}, u32[]{:S(2)}, u32[]{:S(2)}) collective-permute-start(f32[2,4,4,8,128]{4,3,2,1,0:T(8,128)S(1)} %change.1.own), channel_id=1, source_target_pairs={{0,1},{1,2},{2,3},{3,4},{4,5},{5,6},{6,7},{7,8},{8,9},{9,10},{10,1... | collective-permute-start | bytes 393224 | tf_op jit(solution)/shard_map/ppermute | solution.py:24
  81.5 5.0 %collective-permute-start.17 = (f32[2,4,4,8,128]{4,3,2,1,0:T(8,128)S(1)}, f32[2,4,4,8,128]{4,3,2,1,0:T(8,128)S(1)}, u32[]{:S(2)}, u32[]{:S(2)}) collective-permute-start(f32[2,4,4,8,128]{4,3,2,1,0:T(8,128)S(1)} %late0.1.own), channel_id=1, source_target_pairs={{0,15},{1,0},{2,1},{3,2},{4,3},{5,4},{6,5},{7,6},{8,7},{9,8},{10,9... | collective-permute-start | bytes 393224 | tf_op jit(solution)/shard_map/ppermute | solution.py:24
  81.6 8.4 %collective-permute-start.16 = (f32[2,4,4,8,128]{4,3,2,1,0:T(8,128)S(1)}, f32[2,4,4,8,128]{4,3,2,1,0:T(8,128)S(1)}, u32[]{:S(2)}, u32[]{:S(2)}) collective-permute-start(f32[2,4,4,8,128]{4,3,2,1,0:T(8,128)S(1)} %late0.1.own), channel_id=1, source_target_pairs={{0,1},{1,2},{2,3},{3,4},{4,5},{5,6},{6,7},{7,8},{8,9},{9,10},{10,1... | collective-permute-start | bytes 393224 | tf_op jit(solution)/shard_map/ppermute | solution.py:24
  90.6 5.4 %collective-permute-start.19 = (f32[2,4,4,8,128]{4,3,2,1,0:T(8,128)S(1)}, f32[2,4,4,8,128]{4,3,2,1,0:T(8,128)S(1)}, u32[]{:S(2)}, u32[]{:S(2)}) collective-permute-start(f32[2,4,4,8,128]{4,3,2,1,0:T(8,128)S(1)} %late1.1.own), channel_id=1, source_target_pairs={{0,15},{1,0},{2,1},{3,2},{4,3},{5,4},{6,5},{7,6},{8,7},{9,8},{10,9... | collective-permute-start | bytes 393224 | tf_op jit(solution)/shard_map/ppermute | solution.py:24
  90.7 8.8 %collective-permute-start.18 = (f32[2,4,4,8,128]{4,3,2,1,0:T(8,128)S(1)}, f32[2,4,4,8,128]{4,3,2,1,0:T(8,128)S(1)}, u32[]{:S(2)}, u32[]{:S(2)}) collective-permute-start(f32[2,4,4,8,128]{4,3,2,1,0:T(8,128)S(1)} %late1.1.own), channel_id=1, source_target_pairs={{0,1},{1,2},{2,3},{3,4},{4,5},{5,6},{6,7},{7,8},{8,9},{9,10},{10,1... | collective-permute-start | bytes 393224 | tf_op jit(solution)/shard_map/ppermute | solution.py:24
  100.0 5.6 %collective-permute-start.21 = (f32[2,4,4,8,128]{4,3,2,1,0:T(8,128)S(1)}, f32[2,4,4,8,128]{4,3,2,1,0:T(8,128)S(1)}, u32[]{:S(2)}, u32[]{:S(2)}) collective-permute-start(f32[2,4,4,8,128]{4,3,2,1,0:T(8,128)S(1)} %late2.1.own), channel_id=1, source_target_pairs={{0,15},{1,0},{2,1},{3,2},{4,3},{5,4},{6,5},{7,6},{8,7},{9,8},{10,9... | collective-permute-start | bytes 393224 | tf_op jit(solution)/shard_map/ppermute | solution.py:24
  100.1 8.9 %collective-permute-start.20 = (f32[2,4,4,8,128]{4,3,2,1,0:T(8,128)S(1)}, f32[2,4,4,8,128]{4,3,2,1,0:T(8,128)S(1)}, u32[]{:S(2)}, u32[]{:S(2)}) collective-permute-start(f32[2,4,4,8,128]{4,3,2,1,0:T(8,128)S(1)} %late2.1.own), channel_id=1, source_target_pairs={{0,1},{1,2},{2,3},{3,4},{4,5},{5,6},{6,7},{7,8},{8,9},{9,10},{10,1... | collective-permute-start | bytes 393224 | tf_op jit(solution)/shard_map/ppermute | solution.py:24
  109.7 4.3 %collective-permute-start.23 = (f32[4,4,8,128]{3,2,1,0:T(8,128)S(1)}, f32[4,4,8,128]{3,2,1,0:T(8,128)S(1)}, u32[]{:S(2)}, u32[]{:S(2)}) collective-permute-start(f32[4,4,8,128]{3,2,1,0:T(8,128)S(1)} %slice_bitcast_fusion), channel_id=1, source_target_pairs={{0,15},{1,0},{2,1},{3,2},{4,3},{5,4},{6,5},{7,6},{8,7},{9,8},{10,9... | collective-permute-start | bytes 196616 | tf_op jit(solution)/shard_map/ppermute | solution.py:24
  109.8 7.6 %collective-permute-start.22 = (f32[4,4,8,128]{3,2,1,0:T(8,128)S(1)}, f32[4,4,8,128]{3,2,1,0:T(8,128)S(1)}, u32[]{:S(2)}, u32[]{:S(2)}) collective-permute-start(f32[4,4,8,128]{3,2,1,0:T(8,128)S(1)} %slice_bitcast_fusion), channel_id=1, source_target_pairs={{0,1},{1,2},{2,3},{3,4},{4,5},{5,6},{6,7},{7,8},{8,9},{9,10},{10,1... | collective-permute-start | bytes 196616 | tf_op jit(solution)/shard_map/ppermute | solution.py:24
  117.8 5.9 %collective-permute-start.26 = (f32[4,4,8,128]{3,2,1,0:T(8,128)S(1)}, f32[4,4,8,128]{3,2,1,0:T(8,128)S(1)}, u32[]{:S(2)}, u32[]{:S(2)}) collective-permute-start(f32[4,4,8,128]{3,2,1,0:T(8,128)S(1)} %get-tuple-element.30), channel_id=1, source_target_pairs={{0,31},{1,16},{2,17},{3,18},{4,19},{5,20},{6,21},{7,22},{8,23},{9,... | collective-permute-start | bytes 196616 | tf_op jit(solution)/shard_map/ppermute | solution.py:24
  117.9 5.8 %collective-permute-start.25 = (f32[4,4,8,128]{3,2,1,0:T(8,128)S(1)}, f32[4,4,8,128]{3,2,1,0:T(8,128)S(1)}, u32[]{:S(2)}, u32[]{:S(2)}) collective-permute-start(f32[4,4,8,128]{3,2,1,0:T(8,128)S(1)} %get-tuple-element.30), channel_id=1, source_target_pairs={{0,16},{1,17},{2,18},{3,19},{4,20},{5,21},{6,22},{7,23},{8,24},{9,... | collective-permute-start | bytes 196616 | tf_op jit(solution)/shard_map/ppermute | solution.py:24
  117.9 9.4 %collective-permute-start.24 = (f32[4,4,8,128]{3,2,1,0:T(8,128)S(1)}, f32[4,4,8,128]{3,2,1,0:T(8,128)S(1)}, u32[]{:S(2)}, u32[]{:S(2)}) collective-permute-start(f32[4,4,8,128]{3,2,1,0:T(8,128)S(1)} %get-tuple-element.30), channel_id=1, source_target_pairs={{0,17},{1,18},{2,19},{3,20},{4,21},{5,22},{6,23},{7,24},{8,25},{9,... | collective-permute-start | bytes 196616 | tf_op jit(solution)/shard_map/ppermute | solution.py:24
  128.0 4.3 %collective-permute-start.28 = (f32[4,4,8,128]{3,2,1,0:T(8,128)S(1)}, f32[4,4,8,128]{3,2,1,0:T(8,128)S(1)}, u32[]{:S(2)}, u32[]{:S(2)}) collective-permute-start(f32[4,4,8,128]{3,2,1,0:T(8,128)S(1)} %get-tuple-element.31.moved), channel_id=1, source_target_pairs={{0,15},{1,0},{2,1},{3,2},{4,3},{5,4},{6,5},{7,6},{8,7},{9,8},{10,9... | collective-permute-start | bytes 196616 | tf_op jit(solution)/shard_map/ppermute | solution.py:24
  128.0 7.7 %collective-permute-start.27 = (f32[4,4,8,128]{3,2,1,0:T(8,128)S(1)}, f32[4,4,8,128]{3,2,1,0:T(8,128)S(1)}, u32[]{:S(2)}, u32[]{:S(2)}) collective-permute-start(f32[4,4,8,128]{3,2,1,0:T(8,128)S(1)} %get-tuple-element.31.moved), channel_id=1, source_target_pairs={{0,1},{1,2},{2,3},{3,4},{4,5},{5,6},{6,7},{7,8},{8,9},{9,10},{10,1... | collective-permute-start | bytes 196616 | tf_op jit(solution)/shard_map/ppermute | solution.py:24
  (2 other events, 1.7 us)

commit v2 on v1

v2 whole, which is shorter than its diff:
```python
import jax
import jax.numpy as jnp
from jax import lax
from jax.experimental import pallas as pl
from jax.experimental.pallas import tpu as pltpu
from jax.sharding import PartitionSpec as P

CF = 4
SLAB = 4
EDGE = SLAB - 1
ROWS = 4

storage_rate = 2.0


def shifted(value, dt, ds):
    times = lax.axis_size("tm")
    slabs = lax.axis_size("space")
    pairs = [
        (t * slabs + s, ((t + dt) % times) * slabs + (s + ds) % slabs)
        for t in range(times)
        for s in range(slabs)
    ]
    return lax.ppermute(value, ("tm", "space"), pairs)


def call(kernel, name, outs, *args, scratch=(), anywhere=0):
    held = [a if i < anywhere else pltpu.with_memory_space_constraint(a, pltpu.VMEM) for i, a in enumerate(args)]
    inside = pl.BlockSpec(memory_space=pltpu.VMEM)
    outside = pl.BlockSpec(memory_space=pl.ANY)
    return pl.pallas_call(
        kernel,
        out_shape=[pltpu.VMEM(shape, jnp.float32) for shape in outs],
        in_specs=[outside if i < anywhere else inside for i in range(len(args))],
        out_specs=[inside] * len(outs),
        scratch_shapes=[pltpu.VMEM(s, jnp.float32) if isinstance(s, tuple) else s for s in scratch],
        name=name,
        compiler_params=pltpu.CompilerParams(vmem_limit_bytes=16 * 2**20),
    )(*held)


PLANE = (ROWS, 8, 128)


def plane_of(ref, *at):
    return [ref[(*at, pl.ds(j, 8, stride=ROWS), slice(None))] for j in range(ROWS)]


def put_plane(ref, at, rows):
    for j in range(ROWS):
        ref[(*at, pl.ds(j, 8, stride=ROWS), slice(None))] = rows[j]


def x_lower(v):
    return pltpu.roll(v, 1, 1)


def x_upper(v):
    return pltpu.roll(v, 127, 1)


def y_lower(rows):
    return [pltpu.roll(rows[-1], 1, 0)] + rows[:-1]


def y_upper(rows):
    return rows[1:] + [pltpu.roll(rows[0], 7, 0)]


def rows_at(ref, *at):
    return [ref[(*at, j)] for j in range(ROWS)]


def put_rows(ref, at, rows):
    for j in range(ROWS):
        ref[(*at, j)] = rows[j]


WEST, EAST, SOUTH, NORTH, BELOW, ABOVE, STORAGE, FINE, COARSE, COARSEST = range(10)
REACH = SLAB + 2 * EDGE
FACTORS = {FINE: 1.0, COARSE: 1.0 / CF, COARSEST: 1.0 / (2 * CF)}


def step(coef, levels, window, source, put, near, far, right):
    count = len(levels)
    for turn in range(4):
        planes = REACH - 2 * turn
        out = [near, far, near, None][turn]
        held = [None, near, far, near][turn]
        for p in range(planes):
            at = p + turn
            links = [rows_at(coef, kind, at) for kind in range(6)]
            inverses = {level: rows_at(coef, level, at) for level in set(levels)}
            for b in range(count):
                if turn == 0:
                    lower, middle, upper = window(b, p), window(b, p + 1), window(b, p + 2)
                    stored = rows_at(coef, STORAGE, at)
                    factor = FACTORS[levels[b]]
                    if factor != 1.0:
                        stored = [s * factor for s in stored]
                    rhs = [s * v for s, v in zip(stored, middle)]
                    if source is not None:
                        rhs = [r + f for r, f in zip(rhs, source(b, p))]
                    if 0 < p < planes - 1:
                        put_rows(right, (b, p - 1), rhs)
                else:
                    lower, middle, upper = [rows_at(held, b, p + k) for k in range(3)]
                    rhs = rows_at(right, b, at - 1)
                south_of, north_of = y_lower(middle), y_upper(middle)
                result = []
                for j in range(ROWS):
                    west, east, south, north, below, above = [link[j] for link in links]
                    total = rhs[j] + (west * x_lower(middle[j]) + east * x_upper(middle[j]))
                    total = total + (south * south_of[j] + north * north_of[j])
                    total = total + (below * lower[j] + above * upper[j])
                    result.append(total * inverses[levels[b]][j])
                if out is None:
                    put(b, p, result)
                else:
                    put_rows(out, (b, p), result)


def scratch_of(count):
    return [(count, 10) + PLANE, (count, 8) + PLANE, (count, 8) + PLANE]


def windows(lo, own, hi):
    def window(b, p):
        if p < SLAB:
            return rows_at(lo, b, p)
        if p < 2 * SLAB:
            return rows_at(own, b, p - SLAB)
        return rows_at(hi, b, p - 2 * SLAB)

    return window


UP_START, UP_FORCE, UP_FIELD = 0, 8, 14
MESSAGE = 30
X, Y, Z, PORE = range(4)


def prepare_kernel(
    forcing, guess, porosity, permeability, up, down, up_later, down_later, force, start, field,
    force_in, guess_in, pore_in, perm_in, arrivals,
):
    copies = [
        pltpu.make_async_copy(source, target, arrivals.at[i])
        for i, (source, target) in enumerate(
            ((guess.at[0], guess_in), (porosity, pore_in), (permeability, perm_in), (forcing, force_in))
        )
    ]
    for copy in copies:
        copy.start()
    for copy in copies[:3]:
        copy.wait()
    for z in range(SLAB):
        rows = plane_of(guess_in, z)
        put_rows(start, (z,), rows)
        for target in (up, down):
            put_rows(target, (UP_START + SLAB + z,), rows)
        for kind in range(4):
            rows = plane_of(pore_in, z) if kind == PORE else plane_of(perm_in, kind, z)
            put_rows(field, (kind, z), rows)
            for target in (up, down):
                put_rows(target, (UP_FIELD + SLAB * kind + z,), rows)
    copies[3].wait()
    for z in range(SLAB):
        for b in range(2):
            for i in range(CF):
                rows = plane_of(force_in, b * CF + i, z)
                put_rows(force, (b, i, z), rows)
                for target, later, skip in ((up, up_later, 1), (down, down_later, 0)):
                    if 0 <= z - skip < EDGE:
                        if i == 0:
                            put_rows(target, (UP_FORCE + EDGE * b + z - skip,), rows)
                        else:
                            put_rows(later, (b, i - 1, z - skip), rows)


def complete_kernel(arrived, guess, up_part, down_part, up, down, start):
    for z in range(SLAB):
        rows = plane_of(arrived, z)
        put_rows(start, (0, z), rows)
        put_rows(start, (1, z), rows_at(guess, z))
        put_rows(up, (UP_START + z,), rows)
        put_rows(down, (UP_START + z,), rows)
    up[SLAB:] = up_part[SLAB:]
    down[SLAB:] = down_part[SLAB:]


def harmonic(lower, upper):
    return [2.0 * a * b / (a + b) for a, b in zip(lower, upper)]


def face_terms(held):
    column = lax.broadcasted_iota(jnp.int32, (8, 128), 1)
    row = lax.broadcasted_iota(jnp.int32, (8, 128), 0)
    zero = jnp.zeros((8, 128), jnp.float32)
    kx, ky, kz = [held(kind, 0) for kind in (X, Y, Z)]
    side = harmonic(kx, [x_upper(k) for k in kx])
    east_link = [jnp.where(column == 127, zero, v) for v in side]
    east = [jnp.where(column == 127, k, v) for k, v in zip(kx, side)]
    side = [x_lower(v) for v in side]
    west_link = [jnp.where(column == 0, zero, v) for v in side]
    west = [jnp.where(column == 0, k, v) for k, v in zip(kx, side)]
    side = harmonic(ky, y_upper(ky))
    north_link, north = list(side), list(side)
    north_link[-1] = jnp.where(row == 7, zero, side[-1])
    north[-1] = jnp.where(row == 7, ky[-1], side[-1])
    side = y_lower(side)
    south_link, south = list(side), list(side)
    south_link[0] = jnp.where(row == 0, zero, side[0])
    south[0] = jnp.where(row == 0, ky[0], side[0])
    links = [west_link, east_link, south_link, north_link]
    return links, [west, east, south, north], kz


def put_coefficients(coef, p, height, held, levels):
    last = SLAB * lax.axis_size("space") - 1
    zero = jnp.zeros((8, 128), jnp.float32)
    links, sides, kz = face_terms(held)
    below = harmonic(held(Z, -1), kz)
    above = harmonic(kz, held(Z, 1))
    floor, top = height == 0, height == last
    links.append([jnp.where(floor, zero, v) for v in below])
    links.append([jnp.where(top, zero, v) for v in above])
    below = [jnp.where(floor, k, v) for k, v in zip(kz, below)]
    above = [jnp.where(top, k, v) for k, v in zip(kz, above)]
    west, east, south, north = sides
    for kind, rows in enumerate(links):
        put_rows(coef, (kind, p), rows)
    stored = [storage_rate * v for v in held(PORE, 0)]
    put_rows(coef, (STORAGE, p), stored)
    for j in range(ROWS):
        coupling = ((west[j] + east[j]) + (south[j] + north[j])) + (below[j] + above[j])
        for level in levels:
            coef[level, p, j] = 1.0 / (stored[j] * FACTORS[level] + coupling)


def first_kernel(start, lo, hi, force, field, coef, state, near, far, right):
    position = lax.axis_index("space")
    cells = SLAB * lax.axis_size("space")
    for p in range(REACH):

        def held(kind, k, p=p):
            part, at = divmod(p + 1 + k, SLAB)
            if part == 1:
                return rows_at(field, kind, at)
            return rows_at([lo, None, hi][part], UP_FIELD + SLAB * kind + at)

        height = lax.rem(position * SLAB + p - EDGE + cells, cells)
        put_coefficients(coef, p, height, held, (FINE,))

    def window(b, p):
        part, at = divmod(p, SLAB)
        if part == 1:
            return rows_at(start, b, at)
        return rows_at([lo, None, hi][part], UP_START + SLAB * b + at)

    def source(b, p):
        if p < EDGE:
            return rows_at(lo, UP_FORCE + EDGE * b + p)
        if p < EDGE + SLAB:
            return rows_at(force, b, 0, p - EDGE)
        return rows_at(hi, UP_FORCE + EDGE * b + p - EDGE - SLAB)

    step(coef, [FINE, FINE], window, source, lambda b, p, rows: put_rows(state, (b, p), rows), near, far, right)


def early_kernel(section):
    def kernel(own, lo, hi, force, force_lo, force_hi, coef, field, state, kept, near, far, right):
        kept[...] = field[...]

        def source(b, p):
            if p < EDGE:
                return rows_at(force_lo, b, section - 1, p)
            if p < EDGE + SLAB:
                return rows_at(force, b, section, p - EDGE)
            return rows_at(force_hi, b, section - 1, p - EDGE - SLAB)

        put = lambda b, p, rows: put_rows(state, (b, p), rows)
        step(coef, [FINE, FINE], windows(lo, own, hi), source, put, near, far, right)

    return kernel


def pass_kernel(relaxed, initial, on):
    last_time = lax.axis_index("tm") == lax.axis_size("tm") - 1
    for z in range(SLAB):
        rows = [jnp.where(last_time, a, b) for a, b in zip(plane_of(initial, z), rows_at(relaxed, 1, z))]
        put_rows(on, (z,), rows)


def change_kernel(arrived, relaxed, start, change):
    for z in range(SLAB):
        for j in range(ROWS):
            change[0, z, j] = arrived[z, j] - start[0, z, j]
            change[1, z, j] = relaxed[0, z, j] - start[1, z, j]


HALO = 24
SPAN = 2 * HALO + SLAB
PACK = 16
INNER = 8


def pack_kernel(own, lo, hi, lo_two, hi_two, up, down):
    for k in range(own.shape[0]):
        for z in range(SLAB):
            for j in range(ROWS):
                parts = [lo_two[k, z, j], lo[k, z, j], own[k, z, j], hi[k, z, j], hi_two[k, z, j]]
                for i in range(4):
                    up[k, SLAB * i + z, j] = parts[i]
                    down[k, SLAB * i + z, j] = parts[i + 1]


def pack_field_kernel(own, lo, hi, lo_two, hi_two, up, down):
    for k in range(4):
        for z in range(SLAB):
            at = UP_FIELD + SLAB * k + z
            for j in range(ROWS):
                parts = [lo_two[k, z, j], lo[at, j], own[k, z, j], hi[at, j], hi_two[k, z, j]]
                for i in range(4):
                    up[k, SLAB * i + z, j] = parts[i]
                    down[k, SLAB * i + z, j] = parts[i + 1]


def wide_kernel(own, lo, hi, lo_two, hi_two, lo_far, hi_far, coef, wide):
    def fill(target, z, part, at):
        for k in range(4):
            put_rows(wide, (k, target + z), rows_at(part, *at(k)))

    for z in range(PACK):
        fill(0, z, lo_far, lambda k: (k, z))
        fill(HALO + 3 * SLAB, z, hi_far, lambda k: (k, z))
    for z in range(SLAB):
        fill(HALO - 2 * SLAB, z, lo_two, lambda k: (k, z))
        fill(HALO - SLAB, z, lo, lambda k: (UP_FIELD + SLAB * k + z,))
        fill(HALO, z, own, lambda k: (k, z))
        fill(HALO + SLAB, z, hi, lambda k: (UP_FIELD + SLAB * k + z,))
        fill(HALO + 2 * SLAB, z, hi_two, lambda k: (k, z))
    position = lax.axis_index("space")
    cells = SLAB * lax.axis_size("space")

    def body(start, size):
        for k in range(size):
            p = start + k
            height = lax.rem(position * SLAB + p + (cells - HALO + 1), cells)
            held = lambda kind, i, p=p: rows_at(wide, kind, p + 1 + i)
            put_coefficients(coef, p, height, held, (FINE, COARSE, COARSEST))

    in_chunks(SPAN - 2, 10, body)


CHUNK = 26


def in_chunks(count, chunk, body):
    pieces = max(1, round(count / chunk))
    size = -(-count // pieces)
    if pieces == 1:
        body(0, size)
        return

    def turn(i, carry):
        body(jnp.minimum(i * size, count - size), size)
        return carry

    lax.fori_loop(0, pieces, turn, 0)


def sweep_planes(coef, level, blocks, old, new, right, low, high, shift, first):
    factor = FACTORS[level]

    def body(start, size):
        for k in range(size):
            w = low + start + k
            at = w + shift
            links = [rows_at(coef, kind, at) for kind in range(6)]
            inverse = rows_at(coef, level, at)
            if first:
                stored = rows_at(coef, STORAGE, at)
                if factor != 1.0:
                    stored = [s * factor for s in stored]
            for b in blocks:
                lower, middle, upper = [rows_at(old, b, w + i) for i in (-1, 0, 1)]
                if first:
                    rhs = [s * v for s, v in zip(stored, middle)]
                    put_rows(right, (b, w), rhs)
                else:
                    rhs = rows_at(right, b, w)
                south_of, north_of = y_lower(middle), y_upper(middle)
                for j in range(ROWS):
                    west, east, south, north, below, above = [link[j] for link in links]
                    total = rhs[j] + (west * x_lower(middle[j]) + east * x_upper(middle[j]))
                    total = total + (south * south_of[j] + north * north_of[j])
                    total = total + (below * lower[j] + above * upper[j])
                    new[b, w, j] = total * inverse[j]

    in_chunks(high - low, CHUNK * 2 // len(blocks), body)


def wide_step(coef, level, blocks, near, far, right, low, high, shift):
    for turn in range(4):
        old, new = (near, far) if turn % 2 == 0 else (far, near)
        sweep_planes(coef, level, blocks, old, new, right, low + turn + 1, high - turn - 1, shift, turn == 0)


def late_kernel(
    own, lo, hi, lo_two, hi_two, lo_far, hi_far, relaxed, coef, late0, late1, late2, change, last, on, near, far, right
):
    last_time = lax.axis_index("tm") == lax.axis_size("tm") - 1
    for b in range(2):
        for z in range(PACK):
            put_rows(near, (b, z), rows_at(lo_far, b, z))
            put_rows(near, (b, HALO + 3 * SLAB + z), rows_at(hi_far, b, z))
        for i, part in enumerate((lo_two, lo, own, hi, hi_two)):
            for z in range(SLAB):
                put_rows(near, (b, HALO + SLAB * (i - 2) + z), rows_at(part, b, z))
    for section, late in enumerate((late0, late1, late2, change)):
        wide_step(coef, FINE, (0, 1), near, far, right, SLAB * section, SPAN - SLAB * section, -1)
        for b in range(2):
            for z in range(SLAB):
                put_rows(late, (b, z), rows_at(near, b, HALO + z))
    wide_step(coef, COARSE, (0,), near, far, right, HALO - INNER, HALO + SLAB + INNER, -1)
    for z in range(3 * SLAB):
        w = HALO - SLAB + z
        rows = [a + d for a, d in zip(rows_at(near, 1, w), rows_at(near, 0, w))]
        put_rows(on, (z,), [jnp.where(last_time, 0.0, d) for d in rows])
        if SLAB <= z < 2 * SLAB:
            put_rows(last, (z - SLAB,), [u + d for u, d in zip(rows_at(relaxed, 1, z - SLAB), rows)])


def fine_kernel(early0, early1, early2, relaxed, late0, late1, late2, fine):
    for b in range(2):
        for z in range(SLAB):
            for i, (early, late) in enumerate(((early0, late0), (early1, late1), (early2, late2))):
                rows = [u + d for u, d in zip(rows_at(early, b, z), rows_at(late, b, z))]
                put_plane(fine, (b * CF + i, z), rows)
            put_plane(fine, (b * CF + CF - 1, z), rows_at(relaxed, b, z))


def coarse_kernel(
    below, above, arrived, lo, hi, change_lo, change_hi, change, relaxed, last, coef, state, source, near, far, right
):
    for z in range(3 * SLAB):
        put_rows(near, (0, z), rows_at(below, z))
        if z >= SLAB:
            put_rows(near, (0, INNER + z), rows_at(above, z))
    for z in range(3 * SLAB):
        part, at = divmod(z, SLAB)
        if part == 1:
            rows = rows_at(arrived, at)
        else:
            halo, moved = (lo, change_lo) if part == 0 else (hi, change_hi)
            rows = [u + d for u, d in zip(rows_at(halo, UP_START + at), rows_at(moved, 0, at))]
        put_rows(near, (1, SLAB + z), [u + d for u, d in zip(rows, rows_at(near, 0, SLAB + z))])
    shift = HALO - INNER - 1
    wide_step(coef, COARSE, (0,), near, far, right, 0, SLAB + 2 * INNER, shift)
    for z in range(SLAB):
        point = [u + d for u, d in zip(rows_at(relaxed, 0, z), rows_at(change, 0, z))]
        put_plane(state, (0, z), [u + d for u, d in zip(point, rows_at(near, 0, INNER + z))])
        put_plane(state, (1, z), rows_at(last, z))
    wide_step(coef, COARSE, (0,), near, far, right, SLAB, SLAB + 3 * SLAB, shift)
    wide_step(coef, COARSEST, (1,), near, far, right, SLAB, SLAB + 3 * SLAB, shift)
    for z in range(SLAB):
        both = zip(rows_at(near, 0, INNER + z), rows_at(last, z), rows_at(near, 1, INNER + z))
        put_plane(source, (0, z), [(d + u) - w for d, u, w in both])


def on_device(forcing, c_guess, initial, porosity, permeability):
    four = (SLAB,) + PLANE
    both = (2,) + four
    last_time = lax.axis_index("tm") == lax.axis_size("tm") - 1

    arrived = shifted(jnp.where(last_time, initial, c_guess[1]), 1, 0)
    later = (2, CF - 1, EDGE) + PLANE
    message = (MESSAGE,) + PLANE
    up, down, up_later, down_later, force, guess, field = call(
        prepare_kernel, "prepare", [message, message, later, later, (2, CF) + four, four, (4,) + four],
        forcing, c_guess, porosity, permeability, anywhere=4,
        scratch=[forcing.shape, initial.shape, porosity.shape, permeability.shape, pltpu.SemaphoreType.DMA((4,))],
    )
    up, down, start = call(complete_kernel, "complete", [message, message, both], arrived, guess, up, down)
    lo, hi = shifted(up, 0, 1), shifted(down, 0, -1)
    force_lo, force_hi = shifted(up_later, 0, 1), shifted(down_later, 0, -1)
    coef, state = call(
        first_kernel, "first", [(8, REACH) + PLANE, both], start, lo, hi, force, field, scratch=scratch_of(2)
    )
    early = [state]
    for section in range(1, CF):
        state_lo, state_hi = shifted(state, 0, 1), shifted(state, 0, -1)
        state, kept = call(
            early_kernel(section), f"early{section}", [both, (4,) + four], state, state_lo, state_hi, force,
            force_lo, force_hi, coef, field, scratch=scratch_of(2),
        )
        early.append(state)
        if section == 1:
            field_lo, field_hi = shifted(kept, 0, 2), shifted(kept, 0, -2)
            packed = (4, PACK) + PLANE
            field_up, field_down = call(
                pack_field_kernel, "pack_field", [packed, packed], kept, lo, hi, field_lo, field_hi
            )
            field_far_lo, field_far_hi = shifted(field_up, 0, 4), shifted(field_down, 0, -4)
    relaxed = early[-1]

    (on,) = call(pass_kernel, "pass", [four], relaxed, initial)
    arrived = shifted(on, 1, 0)
    (change,) = call(change_kernel, "change", [both], arrived, relaxed, start)
    change_lo, change_hi = shifted(change, 0, 1), shifted(change, 0, -1)
    two_lo, two_hi = shifted(change, 0, 2), shifted(change, 0, -2)
    packed = (2, PACK) + PLANE
    change_up, change_down = call(pack_kernel, "pack", [packed, packed], change, change_lo, change_hi, two_lo, two_hi)
    far_lo, far_hi = shifted(change_up, 0, 4), shifted(change_down, 0, -4)
    (coef,) = call(
        wide_kernel, "wide", [(10, SPAN - 2) + PLANE], field, lo, hi, field_lo, field_hi, field_far_lo, field_far_hi,
        scratch=[(4, SPAN) + PLANE],
    )
    late0, late1, late2, changed, last, on = call(
        late_kernel, "late", [both] * 4 + [four, (3 * SLAB,) + PLANE], change, change_lo, change_hi, two_lo, two_hi,
        far_lo, far_hi, relaxed, coef, scratch=[(2, SPAN) + PLANE] * 3,
    )
    below, above = shifted(on, 1, 1), shifted(on, 1, -1)
    (fine_state,) = call(fine_kernel, "fine", [forcing.shape], *early, late0, late1, late2)
    coarse_state, coarse_source = call(
        coarse_kernel, "coarse", [(2,) + initial.shape, (1,) + initial.shape], below, above, arrived, lo, hi,
        change_lo, change_hi, changed, relaxed, last, coef, scratch=[(2, SLAB + 2 * INNER) + PLANE] * 3,
    )
    return (fine_state, coarse_state, coarse_source)


def solution(mesh):
    return jax.shard_map(
        on_device,
        mesh=mesh,
        in_specs=(
            P("tm", "space", None, None),
            P("tm", "space", None, None),
            P("space", None, None),
            P("space", None, None),
            P(None, "space", None, None),
        ),
        out_specs=(
            P("tm", "space", None, None),
            P("tm", "space", None, None),
            P("tm", "space", None, None),
        ),
        check_vma=False,
    )
```

time: 138 us -> 131 us (0.949)
  the two profiles are of different devices: /device:TPU:0 before, /device:TPU:1 now
where the time goes in v2:
time: 131 us; the launch traced here: 130 us
  starting transfers between devices  52.8 us (40%)
  waiting for transfers between devices  51.1 us (39%)
  Pallas kernels  19.1 us (15%)
  local copies, waits for them, and re-layouts  5.8 us (4%)
    ppermute x24, starting transfers between devices, shifted(): return lax.ppermute(value, ('tm', 'space'), pairs)  52.8 us
    ppermute x24, waiting for transfers between devices, shifted(): return lax.ppermute(value, ('tm', 'space'), pairs)  51.1 us
    pallas_call x14, Pallas kernels, call(): pl.pallas_call(kernel, out_shape=[pltpu.VMEM(shape, jnp.float32) for shap...  19.1 us
    unnamed x13, local copies, waits for them, and re-layouts  5.8 us
  transfers between devices with their start and end apart: 24, of which 17 were waited for; matrix products, arithmetic and copies ran while one was open for 1% of the time, Pallas kernels for 5%

profile of v2, /device:TPU:1, one launch (start us, length us, event | category | flops | bytes accessed | tf_op | source)
XLA Modules:
  0.0 130.4 jit_solution(18200220906181816242)
XLA Ops:
  1.5 3.0 %collective-permute-start = (f32[4,32,128]{2,1,0:T(8,128)S(1)}, f32[4,32,128]{2,1,0:T(8,128)S(1)}, u32[]{:S(2)}, u32[]{:S(2)}) collective-permute-start(f32[4,32,128]{2,1,0:T(8,128)S(1)} %bitcast_select_fusion), channel_id=1, source_target_pairs={{0,16},{1,17},{2,18},{3,19},{4,20},{5,21},{6,22},{7,23},{8,24},{9,... | collective-permute-start | bytes 196616 | tf_op jit(solution)/shard_map/ppermute | solution.py:24
  4.6 1.0 copy-done
  9.0 1.3 collective-permute-start.1
  10.3 3.8 %collective-permute-start.2 = (f32[30,4,8,128]{3,2,1,0:T(8,128)S(1)}, f32[30,4,8,128]{3,2,1,0:T(8,128)S(1)}, u32[]{:S(2)}, u32[]{:S(2)}) collective-permute-start(f32[30,4,8,128]{3,2,1,0:T(8,128)S(1)} %get-tuple-element.36), channel_id=1, source_target_pairs={{0,15},{1,0},{2,1},{3,2},{4,3},{5,4},{6,5},{7,6},{8,7},{9,8},{10,9... | collective-permute-start | bytes 1474568 | tf_op jit(solution)/shard_map/ppermute | solution.py:24
  14.1 4.8 %collective-permute-start.6 = (f32[2,3,3,4,8,128]{5,4,3,2,1,0:T(8,128)S(1)}, f32[2,3,3,4,8,128]{5,4,3,2,1,0:T(8,128)S(1)}, u32[]{:S(2)}, u32[]{:S(2)}) collective-permute-start(f32[2,3,3,4,8,128]{5,4,3,2,1,0:T(8,128)S(1)} %get-tuple-element.41), channel_id=1, source_target_pairs={{0,15},{1,0},{2,1},{3,2},{4,3},{5,4},{6,5},{7,6},{8,7},{9,8},{10,9... | collective-permute-start | bytes 884744 | tf_op jit(solution)/shard_map/ppermute | solution.py:24
  18.9 5.1 %collective-permute-done.1.lo = f32[30,4,8,128]{3,2,1,0:T(8,128)S(1)} collective-permute-done((f32[30,4,8,128]{3,2,1,0:T(8,128)S(1)}, f32[30,4,8,128]{3,2,1,0:T(8,128)S(1)}, u32[]{:S(2)}, u32[]{:S(2)}) %collective-permute-start.1) | collective-permute-done | bytes 491552 | tf_op jit(solution)/shard_map/ppermute | solution.py:24
  24.9 4.7 %collective-permute-start.4 = (f32[2,4,4,8,128]{4,3,2,1,0:T(8,128)S(1)}, f32[2,4,4,8,128]{4,3,2,1,0:T(8,128)S(1)}, u32[]{:S(2)}, u32[]{:S(2)}) collective-permute-start(f32[2,4,4,8,128]{4,3,2,1,0:T(8,128)S(1)} %get-tuple-element.39.own.early0), channel_id=1, source_target_pairs={{0,15},{1,0},{2,1},{3,2},{4,3},{5,4},{6,5},{7,6},{8,7},{9,8},{10,9... | collective-permute-start | bytes 393224 | tf_op jit(solution)/shard_map/ppermute | solution.py:24
  30.3 2.6 %collective-permute-done.4.hi = f32[2,4,4,8,128]{4,3,2,1,0:T(8,128)S(1)} collective-permute-done((f32[2,4,4,8,128]{4,3,2,1,0:T(8,128)S(1)}, f32[2,4,4,8,128]{4,3,2,1,0:T(8,128)S(1)}, u32[]{:S(2)}, u32[]{:S(2)}) %collective-permute-start.4) | collective-permute-done | bytes 131104 | tf_op jit(solution)/shard_map/ppermute | solution.py:24
  32.9 3.8 %collective-permute-done.3.lo = f32[2,4,4,8,128]{4,3,2,1,0:T(8,128)S(1)} collective-permute-done((f32[2,4,4,8,128]{4,3,2,1,0:T(8,128)S(1)}, f32[2,4,4,8,128]{4,3,2,1,0:T(8,128)S(1)}, u32[]{:S(2)}, u32[]{:S(2)}) %collective-permute-start.3) | collective-permute-done | bytes 131104 | tf_op jit(solution)/shard_map/ppermute | solution.py:24
  37.5 3.0 %collective-permute-start.18 = (f32[4,4,4,8,128]{4,3,2,1,0:T(8,128)S(1)}, f32[4,4,4,8,128]{4,3,2,1,0:T(8,128)S(1)}, u32[]{:S(2)}, u32[]{:S(2)}) collective-permute-start(f32[4,4,4,8,128]{4,3,2,1,0:T(8,128)S(1)} %get-tuple-element.48.own), channel_id=1, source_target_pairs={{0,2},{1,3},{2,4},{3,5},{4,6},{5,7},{6,8},{7,9},{8,10},{9,11},{10,... | collective-permute-start | bytes 786440 | tf_op jit(solution)/shard_map/ppermute | solution.py:24
  40.5 3.6 %collective-permute-start.8 = (f32[2,4,4,8,128]{4,3,2,1,0:T(8,128)S(1)}, f32[2,4,4,8,128]{4,3,2,1,0:T(8,128)S(1)}, u32[]{:S(2)}, u32[]{:S(2)}) collective-permute-start(f32[2,4,4,8,128]{4,3,2,1,0:T(8,128)S(1)} %get-tuple-element.43.own.early1), channel_id=1, source_target_pairs={{0,15},{1,0},{2,1},{3,2},{4,3},{5,4},{6,5},{7,6},{8,7},{9,8},{10,9... | collective-permute-start | bytes 393224 | tf_op jit(solution)/shard_map/ppermute | solution.py:24
  44.5 1.9 %collective-permute-done.18.lo_two = f32[4,4,4,8,128]{4,3,2,1,0:T(8,128)S(1)} collective-permute-done((f32[4,4,4,8,128]{4,3,2,1,0:T(8,128)S(1)}, f32[4,4,4,8,128]{4,3,2,1,0:T(8,128)S(1)}, u32[]{:S(2)}, u32[]{:S(2)}) %collective-permute-start.18) | collective-permute-done | bytes 262176 | tf_op jit(solution)/shard_map/ppermute | solution.py:24
  46.6 2.0 %collective-permute-start.20 = (f32[4,16,4,8,128]{4,3,2,1,0:T(8,128)S(1)}, f32[4,16,4,8,128]{4,3,2,1,0:T(8,128)S(1)}, u32[]{:S(2)}, u32[]{:S(2)}) collective-permute-start(f32[4,16,4,8,128]{4,3,2,1,0:T(8,128)S(1)} %get-tuple-element.49), channel_id=1, source_target_pairs={{0,4},{1,5},{2,6},{3,7},{4,8},{5,9},{6,10},{7,11},{8,12},{9,13},{1... | collective-permute-start | bytes 3145736 | tf_op jit(solution)/shard_map/ppermute | solution.py:24
  49.3 1.9 %collective-permute-done.7.lo = f32[2,4,4,8,128]{4,3,2,1,0:T(8,128)S(1)} collective-permute-done((f32[2,4,4,8,128]{4,3,2,1,0:T(8,128)S(1)}, f32[2,4,4,8,128]{4,3,2,1,0:T(8,128)S(1)}, u32[]{:S(2)}, u32[]{:S(2)}) %collective-permute-start.7) | collective-permute-done | bytes 131104 | tf_op jit(solution)/shard_map/ppermute | solution.py:24
  51.3 1.3 early2.1
  54.0 4.1 %collective-permute-done.10.hi = f32[2,4,4,8,128]{4,3,2,1,0:T(8,128)S(1)} collective-permute-done((f32[2,4,4,8,128]{4,3,2,1,0:T(8,128)S(1)}, f32[2,4,4,8,128]{4,3,2,1,0:T(8,128)S(1)}, u32[]{:S(2)}, u32[]{:S(2)}) %collective-permute-start.10) | collective-permute-done | bytes 131104 | tf_op jit(solution)/shard_map/ppermute | solution.py:24
  58.1 3.6 %collective-permute-done.9.lo = f32[2,4,4,8,128]{4,3,2,1,0:T(8,128)S(1)} collective-permute-done((f32[2,4,4,8,128]{4,3,2,1,0:T(8,128)S(1)}, f32[2,4,4,8,128]{4,3,2,1,0:T(8,128)S(1)}, u32[]{:S(2)}, u32[]{:S(2)}) %collective-permute-start.9) | collective-permute-done | bytes 131104 | tf_op jit(solution)/shard_map/ppermute | solution.py:24
  61.7 1.3 early3.1
  63.0 10.4 %collective-permute-start.11 = (f32[4,4,8,128]{3,2,1,0:T(8,128)S(1)}, f32[4,4,8,128]{3,2,1,0:T(8,128)S(1)}, u32[]{:S(2)}, u32[]{:S(2)}) collective-permute-start(f32[4,4,8,128]{3,2,1,0:T(8,128)S(1)} %pass.1), channel_id=1, source_target_pairs={{0,16},{1,17},{2,18},{3,19},{4,20},{5,21},{6,22},{7,23},{8,24},{9,... | collective-permute-start | bytes 196616 | tf_op jit(solution)/shard_map/ppermute | solution.py:24
  73.5 1.7 %collective-permute-done.11.arrived = f32[4,4,8,128]{3,2,1,0:T(8,128)S(1)} collective-permute-done((f32[4,4,8,128]{3,2,1,0:T(8,128)S(1)}, f32[4,4,8,128]{3,2,1,0:T(8,128)S(1)}, u32[]{:S(2)}, u32[]{:S(2)}) %collective-permute-start.11) | collective-permute-done | bytes 65568 | tf_op jit(solution)/shard_map/ppermute | solution.py:24
  75.3 3.0 %collective-permute-start.14 = (f32[2,4,4,8,128]{4,3,2,1,0:T(8,128)S(1)}, f32[2,4,4,8,128]{4,3,2,1,0:T(8,128)S(1)}, u32[]{:S(2)}, u32[]{:S(2)}) collective-permute-start(f32[2,4,4,8,128]{4,3,2,1,0:T(8,128)S(1)} %change.1.own), channel_id=1, source_target_pairs={{0,2},{1,3},{2,4},{3,5},{4,6},{5,7},{6,8},{7,9},{8,10},{9,11},{10,... | collective-permute-start | bytes 393224 | tf_op jit(solution)/shard_map/ppermute | solution.py:24
  78.3 1.8 %collective-permute-start.13 = (f32[2,4,4,8,128]{4,3,2,1,0:T(8,128)S(1)}, f32[2,4,4,8,128]{4,3,2,1,0:T(8,128)S(1)}, u32[]{:S(2)}, u32[]{:S(2)}) collective-permute-start(f32[2,4,4,8,128]{4,3,2,1,0:T(8,128)S(1)} %change.1.own), channel_id=1, source_target_pairs={{0,15},{1,0},{2,1},{3,2},{4,3},{5,4},{6,5},{7,6},{8,7},{9,8},{10,9... | collective-permute-start | bytes 393224 | tf_op jit(solution)/shard_map/ppermute | solution.py:24
  80.6 3.2 %collective-permute-done.14.lo_two = f32[2,4,4,8,128]{4,3,2,1,0:T(8,128)S(1)} collective-permute-done((f32[2,4,4,8,128]{4,3,2,1,0:T(8,128)S(1)}, f32[2,4,4,8,128]{4,3,2,1,0:T(8,128)S(1)}, u32[]{:S(2)}, u32[]{:S(2)}) %collective-permute-start.14) | collective-permute-done | bytes 131104 | tf_op jit(solution)/shard_map/ppermute | solution.py:24
  84.7 4.2 %collective-permute-done.12.lo.change_lo = f32[2,4,4,8,128]{4,3,2,1,0:T(8,128)S(1)} collective-permute-done((f32[2,4,4,8,128]{4,3,2,1,0:T(8,128)S(1)}, f32[2,4,4,8,128]{4,3,2,1,0:T(8,128)S(1)}, u32[]{:S(2)}, u32[]{:S(2)}) %collective-permute-start.12) | collective-permute-done | bytes 131104 | tf_op jit(solution)/shard_map/ppermute | solution.py:24
  89.1 2.7 %collective-permute-start.17 = (f32[2,16,4,8,128]{4,3,2,1,0:T(8,128)S(1)}, f32[2,16,4,8,128]{4,3,2,1,0:T(8,128)S(1)}, u32[]{:S(2)}, u32[]{:S(2)}) collective-permute-start(f32[2,16,4,8,128]{4,3,2,1,0:T(8,128)S(1)} %get-tuple-element.47), channel_id=1, source_target_pairs={{0,12},{1,13},{2,14},{3,15},{4,0},{5,1},{6,2},{7,3},{8,4},{9,5},{1... | collective-permute-start | bytes 1572872 | tf_op jit(solution)/shard_map/ppermute | solution.py:24
  91.8 1.8 %wide.1.coef = f32[10,50,4,8,128]{4,3,2,1,0:T(8,128)S(1)} custom-call(f32[4,4,4,8,128]{4,3,2,1,0:T(8,128)S(1)} %get-tuple-element.38.field.own, f32[30,4,8,128]{3,2,1,0:T(8,128)S(1)} %collective-permute-done.1.lo, f32[30,4,8,128]{3,2,1,0:T(8,128)S(1)} %collective-permute-done.2.hi, f32[4,4,4,8,128]{4,3,2,1,0:T(8,128)S(1)} %collective-permute-done.18.lo_two, ...), custom_call_target="tpu_custom_call" | custom-call | tf_op jit(solution)/shard_map/wide/pallas_call | solution.py:31
  93.5 6.5 %collective-permute-done.16.lo_far = f32[2,16,4,8,128]{4,3,2,1,0:T(8,128)S(1)} collective-permute-done((f32[2,16,4,8,128]{4,3,2,1,0:T(8,128)S(1)}, f32[2,16,4,8,128]{4,3,2,1,0:T(8,128)S(1)}, u32[]{:S(2)}, u32[]{:S(2)}) %collective-permute-start.16) | collective-permute-done | bytes 524320 | tf_op jit(solution)/shard_map/ppermute | solution.py:24
  100.1 11.0 %late.1 = (f32[2,4,4,8,128]{4,3,2,1,0:T(8,128)S(1)}, f32[2,4,4,8,128]{4,3,2,1,0:T(8,128)S(1)}, f32[2,4,4,8,128]{4,3,2,1,0:T(8,128)S(1)}, f32[2,4,4,8,128]{4,3,2,...) custom-call(f32[2,4,4,8,128]{4,3,2,1,0:T(8,128)S(1)} %change.1.own, ...), custom_call_target="tpu_custom_call" | custom-call | tf_op jit(solution)/shard_map/late/pallas_call | solution.py:31
  111.1 6.2 %collective-permute-start.23 = (f32[12,4,8,128]{3,2,1,0:T(8,128)S(1)}, f32[12,4,8,128]{3,2,1,0:T(8,128)S(1)}, u32[]{:S(2)}, u32[]{:S(2)}) collective-permute-start(f32[12,4,8,128]{3,2,1,0:T(8,128)S(1)} %get-tuple-element.54), channel_id=1, source_target_pairs={{0,31},{1,16},{2,17},{3,18},{4,19},{5,20},{6,21},{7,22},{8,23},{9,... | collective-permute-start | bytes 589832 | tf_op jit(solution)/shard_map/ppermute | solution.py:24
  118.2 1.8 %collective-permute-done.23.above = f32[12,4,8,128]{3,2,1,0:T(8,128)S(1)} collective-permute-done((f32[12,4,8,128]{3,2,1,0:T(8,128)S(1)}, f32[12,4,8,128]{3,2,1,0:T(8,128)S(1)}, u32[]{:S(2)}, u32[]{:S(2)}) %collective-permute-start.23) | collective-permute-done | bytes 196640 | tf_op jit(solution)/shard_map/ppermute | solution.py:24
  119.9 7.9 %collective-permute-done.22.below = f32[12,4,8,128]{3,2,1,0:T(8,128)S(1)} collective-permute-done((f32[12,4,8,128]{3,2,1,0:T(8,128)S(1)}, f32[12,4,8,128]{3,2,1,0:T(8,128)S(1)}, u32[]{:S(2)}, u32[]{:S(2)}) %collective-permute-start.22) | collective-permute-done | bytes 196640 | tf_op jit(solution)/shard_map/ppermute | solution.py:24
  127.8 1.2 coarse.1
  (44 shorter events, 13.2 us)
Async XLA Ops:
  0.6 62.4 %copy-start.2 = (f32[4,32,128]{2,1,0:T(8,128)S(1)}, f32[4,32,128]{2,1,0:T(8,128)}, u32[]{:S(2)}) copy-start(f32[4,32,128]{2,1,0:T(8,128)} %initial.1) | copy-start | bytes 196612
  1.5 7.4 %collective-permute-start = (f32[4,32,128]{2,1,0:T(8,128)S(1)}, f32[4,32,128]{2,1,0:T(8,128)S(1)}, u32[]{:S(2)}, u32[]{:S(2)}) collective-permute-start(f32[4,32,128]{2,1,0:T(8,128)S(1)} %bitcast_select_fusion), channel_id=1, source_target_pairs={{0,16},{1,17},{2,18},{3,19},{4,20},{5,21},{6,22},{7,23},{8,24},{9,... | collective-permute-start | bytes 196616 | tf_op jit(solution)/shard_map/ppermute | solution.py:24
  4.6 1.0 copy-start
  5.6 0.9 copy-start.1
  6.5 0.9 copy-start.3
  7.5 0.8 copy-start.4
  9.0 15.0 %collective-permute-start.1 = (f32[30,4,8,128]{3,2,1,0:T(8,128)S(1)}, f32[30,4,8,128]{3,2,1,0:T(8,128)S(1)}, u32[]{:S(2)}, u32[]{:S(2)}) collective-permute-start(f32[30,4,8,128]{3,2,1,0:T(8,128)S(1)} %get-tuple-element.35), channel_id=1, source_target_pairs={{0,1},{1,2},{2,3},{3,4},{4,5},{5,6},{6,7},{7,8},{8,9},{9,10},{10,1... | collective-permute-start | bytes 1474568 | tf_op jit(solution)/shard_map/ppermute | solution.py:24
  10.3 13.7 %collective-permute-start.2 = (f32[30,4,8,128]{3,2,1,0:T(8,128)S(1)}, f32[30,4,8,128]{3,2,1,0:T(8,128)S(1)}, u32[]{:S(2)}, u32[]{:S(2)}) collective-permute-start(f32[30,4,8,128]{3,2,1,0:T(8,128)S(1)} %get-tuple-element.36), channel_id=1, source_target_pairs={{0,15},{1,0},{2,1},{3,2},{4,3},{5,4},{6,5},{7,6},{8,7},{9,8},{10,9... | collective-permute-start | bytes 1474568 | tf_op jit(solution)/shard_map/ppermute | solution.py:24
  14.1 16.2 %collective-permute-start.5 = (f32[2,3,3,4,8,128]{5,4,3,2,1,0:T(8,128)S(1)}, f32[2,3,3,4,8,128]{5,4,3,2,1,0:T(8,128)S(1)}, u32[]{:S(2)}, u32[]{:S(2)}) collective-permute-start(f32[2,3,3,4,8,128]{5,4,3,2,1,0:T(8,128)S(1)} %get-tuple-element.40), channel_id=1, source_target_pairs={{0,1},{1,2},{2,3},{3,4},{4,5},{5,6},{6,7},{7,8},{8,9},{9,10},{10,1... | collective-permute-start | bytes 884744 | tf_op jit(solution)/shard_map/ppermute | solution.py:24
  14.1 16.2 %collective-permute-start.6 = (f32[2,3,3,4,8,128]{5,4,3,2,1,0:T(8,128)S(1)}, f32[2,3,3,4,8,128]{5,4,3,2,1,0:T(8,128)S(1)}, u32[]{:S(2)}, u32[]{:S(2)}) collective-permute-start(f32[2,3,3,4,8,128]{5,4,3,2,1,0:T(8,128)S(1)} %get-tuple-element.41), channel_id=1, source_target_pairs={{0,15},{1,0},{2,1},{3,2},{4,3},{5,4},{6,5},{7,6},{8,7},{9,8},{10,9... | collective-permute-start | bytes 884744 | tf_op jit(solution)/shard_map/ppermute | solution.py:24
  24.9 8.0 %collective-permute-start.4 = (f32[2,4,4,8,128]{4,3,2,1,0:T(8,128)S(1)}, f32[2,4,4,8,128]{4,3,2,1,0:T(8,128)S(1)}, u32[]{:S(2)}, u32[]{:S(2)}) collective-permute-start(f32[2,4,4,8,128]{4,3,2,1,0:T(8,128)S(1)} %get-tuple-element.39.own.early0), channel_id=1, source_target_pairs={{0,15},{1,0},{2,1},{3,2},{4,3},{5,4},{6,5},{7,6},{8,7},{9,8},{10,9... | collective-permute-start | bytes 393224 | tf_op jit(solution)/shard_map/ppermute | solution.py:24
  29.6 7.1 %collective-permute-start.3 = (f32[2,4,4,8,128]{4,3,2,1,0:T(8,128)S(1)}, f32[2,4,4,8,128]{4,3,2,1,0:T(8,128)S(1)}, u32[]{:S(2)}, u32[]{:S(2)}) collective-permute-start(f32[2,4,4,8,128]{4,3,2,1,0:T(8,128)S(1)} %get-tuple-element.39.own.early0), channel_id=1, source_target_pairs={{0,1},{1,2},{2,3},{3,4},{4,5},{5,6},{6,7},{7,8},{8,9},{9,10},{10,1... | collective-permute-start | bytes 393224 | tf_op jit(solution)/shard_map/ppermute | solution.py:24
  37.4 7.1 %collective-permute-start.19 = (f32[4,4,4,8,128]{4,3,2,1,0:T(8,128)S(1)}, f32[4,4,4,8,128]{4,3,2,1,0:T(8,128)S(1)}, u32[]{:S(2)}, u32[]{:S(2)}) collective-permute-start(f32[4,4,4,8,128]{4,3,2,1,0:T(8,128)S(1)} %get-tuple-element.48.own), channel_id=1, source_target_pairs={{0,14},{1,15},{2,0},{3,1},{4,2},{5,3},{6,4},{7,5},{8,6},{9,7},{10,... | collective-permute-start | bytes 786440 | tf_op jit(solution)/shard_map/ppermute | solution.py:24
  37.5 8.9 %collective-permute-start.18 = (f32[4,4,4,8,128]{4,3,2,1,0:T(8,128)S(1)}, f32[4,4,4,8,128]{4,3,2,1,0:T(8,128)S(1)}, u32[]{:S(2)}, u32[]{:S(2)}) collective-permute-start(f32[4,4,4,8,128]{4,3,2,1,0:T(8,128)S(1)} %get-tuple-element.48.own), channel_id=1, source_target_pairs={{0,2},{1,3},{2,4},{3,5},{4,6},{5,7},{6,8},{7,9},{8,10},{9,11},{10,... | collective-permute-start | bytes 786440 | tf_op jit(solution)/shard_map/ppermute | solution.py:24
  40.5 8.9 %collective-permute-start.8 = (f32[2,4,4,8,128]{4,3,2,1,0:T(8,128)S(1)}, f32[2,4,4,8,128]{4,3,2,1,0:T(8,128)S(1)}, u32[]{:S(2)}, u32[]{:S(2)}) collective-permute-start(f32[2,4,4,8,128]{4,3,2,1,0:T(8,128)S(1)} %get-tuple-element.43.own.early1), channel_id=1, source_target_pairs={{0,15},{1,0},{2,1},{3,2},{4,3},{5,4},{6,5},{7,6},{8,7},{9,8},{10,9... | collective-permute-start | bytes 393224 | tf_op jit(solution)/shard_map/ppermute | solution.py:24
  44.0 7.2 %collective-permute-start.7 = (f32[2,4,4,8,128]{4,3,2,1,0:T(8,128)S(1)}, f32[2,4,4,8,128]{4,3,2,1,0:T(8,128)S(1)}, u32[]{:S(2)}, u32[]{:S(2)}) collective-permute-start(f32[2,4,4,8,128]{4,3,2,1,0:T(8,128)S(1)} %get-tuple-element.43.own.early1), channel_id=1, source_target_pairs={{0,1},{1,2},{2,3},{3,4},{4,5},{5,6},{6,7},{7,8},{8,9},{9,10},{10,1... | collective-permute-start | bytes 393224 | tf_op jit(solution)/shard_map/ppermute | solution.py:24
  46.6 45.2 %collective-permute-start.20 = (f32[4,16,4,8,128]{4,3,2,1,0:T(8,128)S(1)}, f32[4,16,4,8,128]{4,3,2,1,0:T(8,128)S(1)}, u32[]{:S(2)}, u32[]{:S(2)}) collective-permute-start(f32[4,16,4,8,128]{4,3,2,1,0:T(8,128)S(1)} %get-tuple-element.49), channel_id=1, source_target_pairs={{0,4},{1,5},{2,6},{3,7},{4,8},{5,9},{6,10},{7,11},{8,12},{9,13},{1... | collective-permute-start | bytes 3145736 | tf_op jit(solution)/shard_map/ppermute | solution.py:24
  48.5 43.2 %collective-permute-start.21 = (f32[4,16,4,8,128]{4,3,2,1,0:T(8,128)S(1)}, f32[4,16,4,8,128]{4,3,2,1,0:T(8,128)S(1)}, u32[]{:S(2)}, u32[]{:S(2)}) collective-permute-start(f32[4,16,4,8,128]{4,3,2,1,0:T(8,128)S(1)} %get-tuple-element.50), channel_id=1, source_target_pairs={{0,12},{1,13},{2,14},{3,15},{4,0},{5,1},{6,2},{7,3},{8,4},{9,5},{1... | collective-permute-start | bytes 3145736 | tf_op jit(solution)/shard_map/ppermute | solution.py:24
  52.5 5.6 %collective-permute-start.10 = (f32[2,4,4,8,128]{4,3,2,1,0:T(8,128)S(1)}, f32[2,4,4,8,128]{4,3,2,1,0:T(8,128)S(1)}, u32[]{:S(2)}, u32[]{:S(2)}) collective-permute-start(f32[2,4,4,8,128]{4,3,2,1,0:T(8,128)S(1)} %get-tuple-element.44.own.early2), channel_id=1, source_target_pairs={{0,15},{1,0},{2,1},{3,2},{4,3},{5,4},{6,5},{7,6},{8,7},{9,8},{10,9... | collective-permute-start | bytes 393224 | tf_op jit(solution)/shard_map/ppermute | solution.py:24
  53.3 8.5 %collective-permute-start.9 = (f32[2,4,4,8,128]{4,3,2,1,0:T(8,128)S(1)}, f32[2,4,4,8,128]{4,3,2,1,0:T(8,128)S(1)}, u32[]{:S(2)}, u32[]{:S(2)}) collective-permute-start(f32[2,4,4,8,128]{4,3,2,1,0:T(8,128)S(1)} %get-tuple-element.44.own.early2), channel_id=1, source_target_pairs={{0,1},{1,2},{2,3},{3,4},{4,5},{5,6},{6,7},{7,8},{8,9},{9,10},{10,1... | collective-permute-start | bytes 393224 | tf_op jit(solution)/shard_map/ppermute | solution.py:24
  63.0 12.2 %collective-permute-start.11 = (f32[4,4,8,128]{3,2,1,0:T(8,128)S(1)}, f32[4,4,8,128]{3,2,1,0:T(8,128)S(1)}, u32[]{:S(2)}, u32[]{:S(2)}) collective-permute-start(f32[4,4,8,128]{3,2,1,0:T(8,128)S(1)} %pass.1), channel_id=1, source_target_pairs={{0,16},{1,17},{2,18},{3,19},{4,20},{5,21},{6,22},{7,23},{8,24},{9,... | collective-permute-start | bytes 196616 | tf_op jit(solution)/shard_map/ppermute | solution.py:24
  75.2 5.4 %collective-permute-start.15 = (f32[2,4,4,8,128]{4,3,2,1,0:T(8,128)S(1)}, f32[2,4,4,8,128]{4,3,2,1,0:T(8,128)S(1)}, u32[]{:S(2)}, u32[]{:S(2)}) collective-permute-start(f32[2,4,4,8,128]{4,3,2,1,0:T(8,128)S(1)} %change.1.own), channel_id=1, source_target_pairs={{0,14},{1,15},{2,0},{3,1},{4,2},{5,3},{6,4},{7,5},{8,6},{9,7},{10,... | collective-permute-start | bytes 393224 | tf_op jit(solution)/shard_map/ppermute | solution.py:24
  75.3 8.5 %collective-permute-start.14 = (f32[2,4,4,8,128]{4,3,2,1,0:T(8,128)S(1)}, f32[2,4,4,8,128]{4,3,2,1,0:T(8,128)S(1)}, u32[]{:S(2)}, u32[]{:S(2)}) collective-permute-start(f32[2,4,4,8,128]{4,3,2,1,0:T(8,128)S(1)} %change.1.own), channel_id=1, source_target_pairs={{0,2},{1,3},{2,4},{3,5},{4,6},{5,7},{6,8},{7,9},{8,10},{9,11},{10,... | collective-permute-start | bytes 393224 | tf_op jit(solution)/shard_map/ppermute | solution.py:24
  78.3 6.4 %collective-permute-start.13 = (f32[2,4,4,8,128]{4,3,2,1,0:T(8,128)S(1)}, f32[2,4,4,8,128]{4,3,2,1,0:T(8,128)S(1)}, u32[]{:S(2)}, u32[]{:S(2)}) collective-permute-start(f32[2,4,4,8,128]{4,3,2,1,0:T(8,128)S(1)} %change.1.own), channel_id=1, source_target_pairs={{0,15},{1,0},{2,1},{3,2},{4,3},{5,4},{6,5},{7,6},{8,7},{9,8},{10,9... | collective-permute-start | bytes 393224 | tf_op jit(solution)/shard_map/ppermute | solution.py:24
  80.6 8.3 %collective-permute-start.12 = (f32[2,4,4,8,128]{4,3,2,1,0:T(8,128)S(1)}, f32[2,4,4,8,128]{4,3,2,1,0:T(8,128)S(1)}, u32[]{:S(2)}, u32[]{:S(2)}) collective-permute-start(f32[2,4,4,8,128]{4,3,2,1,0:T(8,128)S(1)} %change.1.own), channel_id=1, source_target_pairs={{0,1},{1,2},{2,3},{3,4},{4,5},{5,6},{6,7},{7,8},{8,9},{9,10},{10,1... | collective-permute-start | bytes 393224 | tf_op jit(solution)/shard_map/ppermute | solution.py:24
  89.0 11.1 %collective-permute-start.16 = (f32[2,16,4,8,128]{4,3,2,1,0:T(8,128)S(1)}, f32[2,16,4,8,128]{4,3,2,1,0:T(8,128)S(1)}, u32[]{:S(2)}, u32[]{:S(2)}) collective-permute-start(f32[2,16,4,8,128]{4,3,2,1,0:T(8,128)S(1)} %get-tuple-element.46), channel_id=1, source_target_pairs={{0,4},{1,5},{2,6},{3,7},{4,8},{5,9},{6,10},{7,11},{8,12},{9,13},{1... | collective-permute-start | bytes 1572872 | tf_op jit(solution)/shard_map/ppermute | solution.py:24
  89.1 11.0 %collective-permute-start.17 = (f32[2,16,4,8,128]{4,3,2,1,0:T(8,128)S(1)}, f32[2,16,4,8,128]{4,3,2,1,0:T(8,128)S(1)}, u32[]{:S(2)}, u32[]{:S(2)}) collective-permute-start(f32[2,16,4,8,128]{4,3,2,1,0:T(8,128)S(1)} %get-tuple-element.47), channel_id=1, source_target_pairs={{0,12},{1,13},{2,14},{3,15},{4,0},{5,1},{6,2},{7,3},{8,4},{9,5},{1... | collective-permute-start | bytes 1572872 | tf_op jit(solution)/shard_map/ppermute | solution.py:24
  111.1 8.8 %collective-permute-start.23 = (f32[12,4,8,128]{3,2,1,0:T(8,128)S(1)}, f32[12,4,8,128]{3,2,1,0:T(8,128)S(1)}, u32[]{:S(2)}, u32[]{:S(2)}) collective-permute-start(f32[12,4,8,128]{3,2,1,0:T(8,128)S(1)} %get-tuple-element.54), channel_id=1, source_target_pairs={{0,31},{1,16},{2,17},{3,18},{4,19},{5,20},{6,21},{7,22},{8,23},{9,... | collective-permute-start | bytes 589832 | tf_op jit(solution)/shard_map/ppermute | solution.py:24
  117.3 10.5 %collective-permute-start.22 = (f32[12,4,8,128]{3,2,1,0:T(8,128)S(1)}, f32[12,4,8,128]{3,2,1,0:T(8,128)S(1)}, u32[]{:S(2)}, u32[]{:S(2)}) collective-permute-start(f32[12,4,8,128]{3,2,1,0:T(8,128)S(1)} %get-tuple-element.54), channel_id=1, source_target_pairs={{0,17},{1,18},{2,19},{3,20},{4,21},{5,22},{6,23},{7,24},{8,25},{9,... | collective-permute-start | bytes 589832 | tf_op jit(solution)/shard_map/ppermute | solution.py:24

commit v3 on v2

--- a/solution.py
+++ b/solution.py
@@ -24,15 +24,21 @@
     return lax.ppermute(value, ("tm", "space"), pairs)
 
 
-def call(kernel, name, outs, *args, scratch=(), anywhere=0):
-    held = [a if i < anywhere else pltpu.with_memory_space_constraint(a, pltpu.VMEM) for i, a in enumerate(args)]
+def swapped(value):
+    return lax.ppermute(value, "tm", [(t, t ^ 1) for t in range(lax.axis_size("tm"))])
+
+
+def call(kernel, name, outs, *args, scratch=(), anywhere=0, stored=False):
+    held = [
+        pltpu.with_memory_space_constraint(a, pltpu.HBM if i < anywhere else pltpu.VMEM) for i, a in enumerate(args)
+    ]
     inside = pl.BlockSpec(memory_space=pltpu.VMEM)
     outside = pl.BlockSpec(memory_space=pl.ANY)
     return pl.pallas_call(
         kernel,
-        out_shape=[pltpu.VMEM(shape, jnp.float32) for shape in outs],
+        out_shape=[(pltpu.HBM if stored else pltpu.VMEM)(shape, jnp.float32) for shape in outs],
         in_specs=[outside if i < anywhere else inside for i in range(len(args))],
-        out_specs=[inside] * len(outs),
+        out_specs=[outside if stored else inside] * len(outs),
         scratch_shapes=[pltpu.VMEM(s, jnp.float32) if isinstance(s, tuple) else s for s in scratch],
         name=name,
         compiler_params=pltpu.CompilerParams(vmem_limit_bytes=16 * 2**20),
@@ -140,8 +146,13 @@
 X, Y, Z, PORE = range(4)
 
 
+def own_half(first, second):
+    even = lax.rem(lax.axis_index("tm"), 2) == 0
+    return [jnp.where(even, a, b) for a, b in zip(first, second)]
+
+
 def prepare_kernel(
-    forcing, guess, porosity, permeability, up, down, up_later, down_later, force, start, field,
+    forcing, guess, porosity, permeability, up, down, up_later, down_later, force, start, field, half,
     force_in, guess_in, pore_in, perm_in, arrivals,
 ):
     copies = [
@@ -164,6 +175,8 @@
             put_rows(field, (kind, z), rows)
             for target in (up, down):
                 put_rows(target, (UP_FIELD + SLAB * kind + z,), rows)
+        for kind in range(2):
+            put_rows(half, (kind, z), own_half(rows_at(field, kind, z), rows_at(field, kind + 2, z)))
     copies[3].wait()
     for z in range(SLAB):
         for b in range(2):
@@ -269,9 +282,7 @@
 
 
 def early_kernel(section):
-    def kernel(own, lo, hi, force, force_lo, force_hi, coef, field, state, kept, near, far, right):
-        kept[...] = field[...]
-
+    def kernel(own, lo, hi, force, force_lo, force_hi, coef, state, near, far, right):
         def source(b, p):
             if p < EDGE:
                 return rows_at(force_lo, b, section - 1, p)
@@ -315,31 +326,38 @@
                     down[k, SLAB * i + z, j] = parts[i + 1]
 
 
-def pack_field_kernel(own, lo, hi, lo_two, hi_two, up, down):
+def pack_field_kernel(own, lo, hi, lo_two, hi_two, after, up, down):
+    for k in range(2):
+        for z in range(SLAB):
+            at = UP_FIELD + SLAB * k + z
+            near_lo = own_half(rows_at(lo, at), rows_at(lo, at + 2 * SLAB))
+            near_hi = own_half(rows_at(hi, at), rows_at(hi, at + 2 * SLAB))
+            parts = [rows_at(lo_two, k, z), near_lo, rows_at(own, k, z), near_hi, rows_at(hi_two, k, z)]
+            for i in range(4):
+                put_rows(up, (k, SLAB * i + z), parts[i])
+                put_rows(down, (k, SLAB * i + z), parts[i + 1])
+
+
+def share_kernel(lo_two, hi_two, lo_far, hi_far, after, share):
+    share[:, :PACK] = lo_far[...]
+    share[:, PACK : PACK + SLAB] = lo_two[...]
+    share[:, PACK + SLAB : PACK + 2 * SLAB] = hi_two[...]
+    share[:, PACK + 2 * SLAB :] = hi_far[...]
+
+
+def wide_kernel(own, lo, hi, mine, other, coef, wide):
+    for k in range(2):
+        for z in range(PACK + SLAB):
+            for at, target in ((z, z), (PACK + SLAB + z, HALO + 2 * SLAB + z)):
+                a, b = rows_at(mine, k, at), rows_at(other, k, at)
+                put_rows(wide, (k, target), own_half(a, b))
+                put_rows(wide, (k + 2, target), own_half(b, a))
     for k in range(4):
         for z in range(SLAB):
             at = UP_FIELD + SLAB * k + z
-            for j in range(ROWS):
-                parts = [lo_two[k, z, j], lo[at, j], own[k, z, j], hi[at, j], hi_two[k, z, j]]
-                for i in range(4):
-                    up[k, SLAB * i + z, j] = parts[i]
-                    down[k, SLAB * i + z, j] = parts[i + 1]
-
-
-def wide_kernel(own, lo, hi, lo_two, hi_two, lo_far, hi_far, coef, wide):
-    def fill(target, z, part, at):
-        for k in range(4):
-            put_rows(wide, (k, target + z), rows_at(part, *at(k)))
-
-    for z in range(PACK):
-        fill(0, z, lo_far, lambda k: (k, z))
-        fill(HALO + 3 * SLAB, z, hi_far, lambda k: (k, z))
-    for z in range(SLAB):
-        fill(HALO - 2 * SLAB, z, lo_two, lambda k: (k, z))
-        fill(HALO - SLAB, z, lo, lambda k: (UP_FIELD + SLAB * k + z,))
-        fill(HALO, z, own, lambda k: (k, z))
-        fill(HALO + SLAB, z, hi, lambda k: (UP_FIELD + SLAB * k + z,))
-        fill(HALO + 2 * SLAB, z, hi_two, lambda k: (k, z))
+            put_rows(wide, (k, HALO - SLAB + z), rows_at(lo, at))
+            put_rows(wide, (k, HALO + z), rows_at(own, k, z))
+            put_rows(wide, (k, HALO + SLAB + z), rows_at(hi, at))
     position = lax.axis_index("space")
     cells = SLAB * lax.axis_size("space")
 
@@ -442,7 +460,8 @@
 
 
 def coarse_kernel(
-    below, above, arrived, lo, hi, change_lo, change_hi, change, relaxed, last, coef, state, source, near, far, right
+    below, above, arrived, lo, hi, change_lo, change_hi, change, relaxed, last, coef, state, source,
+    near, far, right, state_out, source_out, leaving,
 ):
     for z in range(3 * SLAB):
         put_rows(near, (0, z), rows_at(below, z))
@@ -460,13 +479,19 @@
     wide_step(coef, COARSE, (0,), near, far, right, 0, SLAB + 2 * INNER, shift)
     for z in range(SLAB):
         point = [u + d for u, d in zip(rows_at(relaxed, 0, z), rows_at(change, 0, z))]
-        put_plane(state, (0, z), [u + d for u, d in zip(point, rows_at(near, 0, INNER + z))])
-        put_plane(state, (1, z), rows_at(last, z))
+        put_plane(state_out, (0, z), [u + d for u, d in zip(point, rows_at(near, 0, INNER + z))])
+        put_plane(state_out, (1, z), rows_at(last, z))
+    state_copy = pltpu.make_async_copy(state_out, state, leaving.at[0])
+    state_copy.start()
     wide_step(coef, COARSE, (0,), near, far, right, SLAB, SLAB + 3 * SLAB, shift)
     wide_step(coef, COARSEST, (1,), near, far, right, SLAB, SLAB + 3 * SLAB, shift)
     for z in range(SLAB):
         both = zip(rows_at(near, 0, INNER + z), rows_at(last, z), rows_at(near, 1, INNER + z))
-        put_plane(source, (0, z), [(d + u) - w for d, u, w in both])
+        put_plane(source_out, (0, z), [(d + u) - w for d, u, w in both])
+    source_copy = pltpu.make_async_copy(source_out, source, leaving.at[1])
+    source_copy.start()
+    state_copy.wait()
+    source_copy.wait()
 
 
 def on_device(forcing, c_guess, initial, porosity, permeability):
@@ -477,8 +502,8 @@
     arrived = shifted(jnp.where(last_time, initial, c_guess[1]), 1, 0)
     later = (2, CF - 1, EDGE) + PLANE
     message = (MESSAGE,) + PLANE
-    up, down, up_later, down_later, force, guess, field = call(
-        prepare_kernel, "prepare", [message, message, later, later, (2, CF) + four, four, (4,) + four],
+    up, down, up_later, down_later, force, guess, field, half = call(
+        prepare_kernel, "prepare", [message, message, later, later, (2, CF) + four, four, (4,) + four, both],
         forcing, c_guess, porosity, permeability, anywhere=4,
         scratch=[forcing.shape, initial.shape, porosity.shape, permeability.shape, pltpu.SemaphoreType.DMA((4,))],
     )
@@ -488,33 +513,36 @@
     coef, state = call(
         first_kernel, "first", [(8, REACH) + PLANE, both], start, lo, hi, force, field, scratch=scratch_of(2)
     )
+    half_lo, half_hi = shifted(half, 0, 2), shifted(half, 0, -2)
+    packed = (2, PACK) + PLANE
     early = [state]
     for section in range(1, CF):
         state_lo, state_hi = shifted(state, 0, 1), shifted(state, 0, -1)
-        state, kept = call(
-            early_kernel(section), f"early{section}", [both, (4,) + four], state, state_lo, state_hi, force,
-            force_lo, force_hi, coef, field, scratch=scratch_of(2),
+        (state,) = call(
+            early_kernel(section), f"early{section}", [both], state, state_lo, state_hi, force, force_lo, force_hi,
+            coef, scratch=scratch_of(2),
         )
         early.append(state)
         if section == 1:
-            field_lo, field_hi = shifted(kept, 0, 2), shifted(kept, 0, -2)
-            packed = (4, PACK) + PLANE
-            field_up, field_down = call(
-                pack_field_kernel, "pack_field", [packed, packed], kept, lo, hi, field_lo, field_hi
+            half_up, half_down = call(
+                pack_field_kernel, "pack_field", [packed, packed], half, lo, hi, half_lo, half_hi, state
             )
-            field_far_lo, field_far_hi = shifted(field_up, 0, 4), shifted(field_down, 0, -4)
+            half_far_lo, half_far_hi = shifted(half_up, 0, 4), shifted(half_down, 0, -4)
     relaxed = early[-1]
 
     (on,) = call(pass_kernel, "pass", [four], relaxed, initial)
     arrived = shifted(on, 1, 0)
+    (share,) = call(
+        share_kernel, "share", [(2, 2 * (PACK + SLAB)) + PLANE], half_lo, half_hi, half_far_lo, half_far_hi, relaxed
+    )
+    other_share = swapped(share)
     (change,) = call(change_kernel, "change", [both], arrived, relaxed, start)
     change_lo, change_hi = shifted(change, 0, 1), shifted(change, 0, -1)
     two_lo, two_hi = shifted(change, 0, 2), shifted(change, 0, -2)
-    packed = (2, PACK) + PLANE
     change_up, change_down = call(pack_kernel, "pack", [packed, packed], change, change_lo, change_hi, two_lo, two_hi)
     far_lo, far_hi = shifted(change_up, 0, 4), shifted(change_down, 0, -4)
     (coef,) = call(
-        wide_kernel, "wide", [(10, SPAN - 2) + PLANE], field, lo, hi, field_lo, field_hi, field_far_lo, field_far_hi,
+        wide_kernel, "wide", [(10, SPAN - 2) + PLANE], field, lo, hi, share, other_share,
         scratch=[(4, SPAN) + PLANE],
     )
     late0, late1, late2, changed, last, on = call(
@@ -525,7 +553,9 @@
     (fine_state,) = call(fine_kernel, "fine", [forcing.shape], *early, late0, late1, late2)
     coarse_state, coarse_source = call(
         coarse_kernel, "coarse", [(2,) + initial.shape, (1,) + initial.shape], below, above, arrived, lo, hi,
-        change_lo, change_hi, changed, relaxed, last, coef, scratch=[(2, SLAB + 2 * INNER) + PLANE] * 3,
+        change_lo, change_hi, changed, relaxed, last, coef, stored=True,
+        scratch=[(2, SLAB + 2 * INNER) + PLANE] * 3
+        + [(2,) + initial.shape, (1,) + initial.shape, pltpu.SemaphoreType.DMA((2,))],
     )
     return (fine_state, coarse_state, coarse_source)
 

time: 131 us -> 125 us (0.954)
  the two profiles are of different devices: /device:TPU:1 before, /device:TPU:0 now
where the time goes in v3:
time: 125 us; the launch traced here: 124 us
  starting transfers between devices  53.8 us (43%)
  waiting for transfers between devices  47.4 us (38%)
  Pallas kernels  19.1 us (15%)
  local copies, waits for them, and re-layouts  1.41 us (1%)
    ppermute x24, starting transfers between devices, shifted(): return lax.ppermute(value, ('tm', 'space'), pairs)  53.7 us
    ppermute x24, waiting for transfers between devices, shifted(): return lax.ppermute(value, ('tm', 'space'), pairs)  47.4 us
    pallas_call x15, Pallas kernels, call(): pl.pallas_call(kernel, out_shape=[(pltpu.HBM if stored else pltpu.VMEM)(s...  19.1 us
  transfers between devices with their start and end apart: 25, of which 11 were waited for; matrix products, arithmetic and copies ran while one was open for 1% of the time, Pallas kernels for 5%

profile of v3, /device:TPU:0, one launch (start us, length us, event | category | flops | bytes accessed | tf_op | source)
XLA Modules:
  0.0 123.6 jit_solution(12530457660161786556)
XLA Ops:
  0.6 0.9 bitcast_select_fusion
  1.5 1.3 %prepare.1 = (f32[30,4,8,128]{3,2,1,0:T(8,128)S(1)}, f32[30,4,8,128]{3,2,1,0:T(8,128)S(1)}, f32[2,3,3,4,8,128]{5,4,3,2,1,0:T(8,128)S(1)}, f32[2,3,3,4,8,128]{5,4...) custom-call(f32[8,4,32,128]{3,2,1,0:T(8,128)} %forcing.1, ...), custom_call_target="tpu_custom_call" | custom-call | tf_op jit(solution)/shard_map/prepare/pallas_call | solution.py:37
  2.9 4.2 %collective-permute-done.arrived = f32[4,32,128]{2,1,0:T(8,128)S(1)} collective-permute-done((f32[4,32,128]{2,1,0:T(8,128)S(1)}, f32[4,32,128]{2,1,0:T(8,128)S(1)}, u32[]{:S(2)}, u32[]{:S(2)}) %collective-permute-start) | collective-permute-done | bytes 65568 | tf_op jit(solution)/shard_map/ppermute | solution.py:24
  7.1 1.6 %collective-permute-start.1 = (f32[30,4,8,128]{3,2,1,0:T(8,128)S(1)}, f32[30,4,8,128]{3,2,1,0:T(8,128)S(1)}, u32[]{:S(2)}, u32[]{:S(2)}) collective-permute-start(f32[30,4,8,128]{3,2,1,0:T(8,128)S(1)} %get-tuple-element.32), channel_id=1, source_target_pairs={{0,1},{1,2},{2,3},{3,4},{4,5},{5,6},{6,7},{7,8},{8,9},{9,10},{10,1... | collective-permute-start | bytes 1474568 | tf_op jit(solution)/shard_map/ppermute | solution.py:24
  8.7 3.9 %collective-permute-start.2 = (f32[30,4,8,128]{3,2,1,0:T(8,128)S(1)}, f32[30,4,8,128]{3,2,1,0:T(8,128)S(1)}, u32[]{:S(2)}, u32[]{:S(2)}) collective-permute-start(f32[30,4,8,128]{3,2,1,0:T(8,128)S(1)} %get-tuple-element.33), channel_id=1, source_target_pairs={{0,15},{1,0},{2,1},{3,2},{4,3},{5,4},{6,5},{7,6},{8,7},{9,8},{10,9... | collective-permute-start | bytes 1474568 | tf_op jit(solution)/shard_map/ppermute | solution.py:24
  12.6 5.3 %collective-permute-start.6 = (f32[2,3,3,4,8,128]{5,4,3,2,1,0:T(8,128)S(1)}, f32[2,3,3,4,8,128]{5,4,3,2,1,0:T(8,128)S(1)}, u32[]{:S(2)}, u32[]{:S(2)}) collective-permute-start(f32[2,3,3,4,8,128]{5,4,3,2,1,0:T(8,128)S(1)} %get-tuple-element.38), channel_id=1, source_target_pairs={{0,15},{1,0},{2,1},{3,2},{4,3},{5,4},{6,5},{7,6},{8,7},{9,8},{10,9... | collective-permute-start | bytes 884744 | tf_op jit(solution)/shard_map/ppermute | solution.py:24
  17.9 6.1 %collective-permute-done.1.lo = f32[30,4,8,128]{3,2,1,0:T(8,128)S(1)} collective-permute-done((f32[30,4,8,128]{3,2,1,0:T(8,128)S(1)}, f32[30,4,8,128]{3,2,1,0:T(8,128)S(1)}, u32[]{:S(2)}, u32[]{:S(2)}) %collective-permute-start.1) | collective-permute-done | bytes 491552 | tf_op jit(solution)/shard_map/ppermute | solution.py:24
  24.0 2.1 %collective-permute-done.2.hi = f32[30,4,8,128]{3,2,1,0:T(8,128)S(1)} collective-permute-done((f32[30,4,8,128]{3,2,1,0:T(8,128)S(1)}, f32[30,4,8,128]{3,2,1,0:T(8,128)S(1)}, u32[]{:S(2)}, u32[]{:S(2)}) %collective-permute-start.2) | collective-permute-done | bytes 491552 | tf_op jit(solution)/shard_map/ppermute | solution.py:24
  26.1 0.9 first.1
  27.0 6.3 %collective-permute-start.4 = (f32[2,4,4,8,128]{4,3,2,1,0:T(8,128)S(1)}, f32[2,4,4,8,128]{4,3,2,1,0:T(8,128)S(1)}, u32[]{:S(2)}, u32[]{:S(2)}) collective-permute-start(f32[2,4,4,8,128]{4,3,2,1,0:T(8,128)S(1)} %get-tuple-element.36.own.early0), channel_id=1, source_target_pairs={{0,15},{1,0},{2,1},{3,2},{4,3},{5,4},{6,5},{7,6},{8,7},{9,8},{10,9... | collective-permute-start | bytes 393224 | tf_op jit(solution)/shard_map/ppermute | solution.py:24
  33.4 5.6 %collective-permute-start.19 = (f32[2,4,4,8,128]{4,3,2,1,0:T(8,128)S(1)}, f32[2,4,4,8,128]{4,3,2,1,0:T(8,128)S(1)}, u32[]{:S(2)}, u32[]{:S(2)}) collective-permute-start(f32[2,4,4,8,128]{4,3,2,1,0:T(8,128)S(1)} %get-tuple-element.42.own), channel_id=1, source_target_pairs={{0,14},{1,15},{2,0},{3,1},{4,2},{5,3},{6,4},{7,5},{8,6},{9,7},{10,... | collective-permute-start | bytes 393224 | tf_op jit(solution)/shard_map/ppermute | solution.py:24
  39.0 0.6 early1.1.own.after
  39.6 2.4 %collective-permute-done.18.lo_two = f32[2,4,4,8,128]{4,3,2,1,0:T(8,128)S(1)} collective-permute-done((f32[2,4,4,8,128]{4,3,2,1,0:T(8,128)S(1)}, f32[2,4,4,8,128]{4,3,2,1,0:T(8,128)S(1)}, u32[]{:S(2)}, u32[]{:S(2)}) %collective-permute-start.18) | collective-permute-done | bytes 131104 | tf_op jit(solution)/shard_map/ppermute | solution.py:24
  42.2 3.2 %collective-permute-start.21 = (f32[2,16,4,8,128]{4,3,2,1,0:T(8,128)S(1)}, f32[2,16,4,8,128]{4,3,2,1,0:T(8,128)S(1)}, u32[]{:S(2)}, u32[]{:S(2)}) collective-permute-start(f32[2,16,4,8,128]{4,3,2,1,0:T(8,128)S(1)} %get-tuple-element.44), channel_id=1, source_target_pairs={{0,12},{1,13},{2,14},{3,15},{4,0},{5,1},{6,2},{7,3},{8,4},{9,5},{1... | collective-permute-start | bytes 1572872 | tf_op jit(solution)/shard_map/ppermute | solution.py:24
  45.4 5.4 %collective-permute-start.8 = (f32[2,4,4,8,128]{4,3,2,1,0:T(8,128)S(1)}, f32[2,4,4,8,128]{4,3,2,1,0:T(8,128)S(1)}, u32[]{:S(2)}, u32[]{:S(2)}) collective-permute-start(f32[2,4,4,8,128]{4,3,2,1,0:T(8,128)S(1)} %early1.1.own.after), channel_id=1, source_target_pairs={{0,15},{1,0},{2,1},{3,2},{4,3},{5,4},{6,5},{7,6},{8,7},{9,8},{10,9... | collective-permute-start | bytes 393224 | tf_op jit(solution)/shard_map/ppermute | solution.py:24
  50.8 3.8 %collective-permute-done.7.lo = f32[2,4,4,8,128]{4,3,2,1,0:T(8,128)S(1)} collective-permute-done((f32[2,4,4,8,128]{4,3,2,1,0:T(8,128)S(1)}, f32[2,4,4,8,128]{4,3,2,1,0:T(8,128)S(1)}, u32[]{:S(2)}, u32[]{:S(2)}) %collective-permute-start.7) | collective-permute-done | bytes 131104 | tf_op jit(solution)/shard_map/ppermute | solution.py:24
  54.6 0.6 early2.1.own
  55.2 4.7 %collective-permute-start.10 = (f32[2,4,4,8,128]{4,3,2,1,0:T(8,128)S(1)}, f32[2,4,4,8,128]{4,3,2,1,0:T(8,128)S(1)}, u32[]{:S(2)}, u32[]{:S(2)}) collective-permute-start(f32[2,4,4,8,128]{4,3,2,1,0:T(8,128)S(1)} %early2.1.own), channel_id=1, source_target_pairs={{0,15},{1,0},{2,1},{3,2},{4,3},{5,4},{6,5},{7,6},{8,7},{9,8},{10,9... | collective-permute-start | bytes 393224 | tf_op jit(solution)/shard_map/ppermute | solution.py:24
  59.9 2.5 %collective-permute-done.10.hi = f32[2,4,4,8,128]{4,3,2,1,0:T(8,128)S(1)} collective-permute-done((f32[2,4,4,8,128]{4,3,2,1,0:T(8,128)S(1)}, f32[2,4,4,8,128]{4,3,2,1,0:T(8,128)S(1)}, u32[]{:S(2)}, u32[]{:S(2)}) %collective-permute-start.10) | collective-permute-done | bytes 131104 | tf_op jit(solution)/shard_map/ppermute | solution.py:24
  62.5 5.8 %collective-permute-done.9.lo = f32[2,4,4,8,128]{4,3,2,1,0:T(8,128)S(1)} collective-permute-done((f32[2,4,4,8,128]{4,3,2,1,0:T(8,128)S(1)}, f32[2,4,4,8,128]{4,3,2,1,0:T(8,128)S(1)}, u32[]{:S(2)}, u32[]{:S(2)}) %collective-permute-start.9) | collective-permute-done | bytes 131104 | tf_op jit(solution)/shard_map/ppermute | solution.py:24
  69.7 4.9 %collective-permute-done.11.arrived = f32[4,4,8,128]{3,2,1,0:T(8,128)S(1)} collective-permute-done((f32[4,4,8,128]{3,2,1,0:T(8,128)S(1)}, f32[4,4,8,128]{3,2,1,0:T(8,128)S(1)}, u32[]{:S(2)}, u32[]{:S(2)}) %collective-permute-start.11) | collective-permute-done | bytes 65568 | tf_op jit(solution)/shard_map/ppermute | solution.py:24
  74.7 5.3 %collective-permute-start.13 = (f32[2,4,4,8,128]{4,3,2,1,0:T(8,128)S(1)}, f32[2,4,4,8,128]{4,3,2,1,0:T(8,128)S(1)}, u32[]{:S(2)}, u32[]{:S(2)}) collective-permute-start(f32[2,4,4,8,128]{4,3,2,1,0:T(8,128)S(1)} %change.1.own), channel_id=1, source_target_pairs={{0,15},{1,0},{2,1},{3,2},{4,3},{5,4},{6,5},{7,6},{8,7},{9,8},{10,9... | collective-permute-start | bytes 393224 | tf_op jit(solution)/shard_map/ppermute | solution.py:24
  80.1 5.6 %collective-permute-start.15 = (f32[2,4,4,8,128]{4,3,2,1,0:T(8,128)S(1)}, f32[2,4,4,8,128]{4,3,2,1,0:T(8,128)S(1)}, u32[]{:S(2)}, u32[]{:S(2)}) collective-permute-start(f32[2,4,4,8,128]{4,3,2,1,0:T(8,128)S(1)} %change.1.own), channel_id=1, source_target_pairs={{0,14},{1,15},{2,0},{3,1},{4,2},{5,3},{6,4},{7,5},{8,6},{9,7},{10,... | collective-permute-start | bytes 393224 | tf_op jit(solution)/shard_map/ppermute | solution.py:24
  85.7 3.0 %collective-permute-done.14.lo_two = f32[2,4,4,8,128]{4,3,2,1,0:T(8,128)S(1)} collective-permute-done((f32[2,4,4,8,128]{4,3,2,1,0:T(8,128)S(1)}, f32[2,4,4,8,128]{4,3,2,1,0:T(8,128)S(1)}, u32[]{:S(2)}, u32[]{:S(2)}) %collective-permute-start.14) | collective-permute-done | bytes 131104 | tf_op jit(solution)/shard_map/ppermute | solution.py:24
  88.8 3.2 %collective-permute-start.17 = (f32[2,16,4,8,128]{4,3,2,1,0:T(8,128)S(1)}, f32[2,16,4,8,128]{4,3,2,1,0:T(8,128)S(1)}, u32[]{:S(2)}, u32[]{:S(2)}) collective-permute-start(f32[2,16,4,8,128]{4,3,2,1,0:T(8,128)S(1)} %get-tuple-element.41), channel_id=1, source_target_pairs={{0,12},{1,13},{2,14},{3,15},{4,0},{5,1},{6,2},{7,3},{8,4},{9,5},{1... | collective-permute-start | bytes 1572872 | tf_op jit(solution)/shard_map/ppermute | solution.py:24
  92.1 1.8 %wide.1.coef = f32[10,50,4,8,128]{4,3,2,1,0:T(8,128)S(1)} custom-call(f32[4,4,4,8,128]{4,3,2,1,0:T(8,128)S(1)} %get-tuple-element.35.field.own, f32[30,4,8,128]{3,2,1,0:T(8,128)S(1)} %collective-permute-done.1.lo, f32[30,4,8,128]{3,2,1,0:T(8,128)S(1)} %collective-permute-done.2.hi, f32[2,40,4,8,128]{4,3,2,1,0:T(8,128)S(1)} %share.1.mine, ...), custom_call_target="tpu_custom_call" | custom-call | tf_op jit(solution)/shard_map/wide/pallas_call | solution.py:37
  93.8 6.0 %collective-permute-done.16.lo_far = f32[2,16,4,8,128]{4,3,2,1,0:T(8,128)S(1)} collective-permute-done((f32[2,16,4,8,128]{4,3,2,1,0:T(8,128)S(1)}, f32[2,16,4,8,128]{4,3,2,1,0:T(8,128)S(1)}, u32[]{:S(2)}, u32[]{:S(2)}) %collective-permute-start.16) | collective-permute-done | bytes 524320 | tf_op jit(solution)/shard_map/ppermute | solution.py:24
  99.9 11.0 %late.1 = (f32[2,4,4,8,128]{4,3,2,1,0:T(8,128)S(1)}, f32[2,4,4,8,128]{4,3,2,1,0:T(8,128)S(1)}, f32[2,4,4,8,128]{4,3,2,1,0:T(8,128)S(1)}, f32[2,4,4,8,128]{4,3,2,...) custom-call(f32[2,4,4,8,128]{4,3,2,1,0:T(8,128)S(1)} %change.1.own, ...), custom_call_target="tpu_custom_call" | custom-call | tf_op jit(solution)/shard_map/late/pallas_call | solution.py:37
  111.0 3.1 %collective-permute-start.24 = (f32[12,4,8,128]{3,2,1,0:T(8,128)S(1)}, f32[12,4,8,128]{3,2,1,0:T(8,128)S(1)}, u32[]{:S(2)}, u32[]{:S(2)}) collective-permute-start(f32[12,4,8,128]{3,2,1,0:T(8,128)S(1)} %get-tuple-element.48), channel_id=1, source_target_pairs={{0,31},{1,16},{2,17},{3,18},{4,19},{5,20},{6,21},{7,22},{8,23},{9,... | collective-permute-start | bytes 589832 | tf_op jit(solution)/shard_map/ppermute | solution.py:24
  114.1 0.8 copy.8
  114.9 6.6 %collective-permute-done.23.below = f32[12,4,8,128]{3,2,1,0:T(8,128)S(1)} collective-permute-done((f32[12,4,8,128]{3,2,1,0:T(8,128)S(1)}, f32[12,4,8,128]{3,2,1,0:T(8,128)S(1)}, u32[]{:S(2)}, u32[]{:S(2)}) %collective-permute-start.23) | collective-permute-done | bytes 196640 | tf_op jit(solution)/shard_map/ppermute | solution.py:24
  121.5 1.9 %coarse.1 = (f32[2,4,32,128]{3,2,1,0:T(8,128)}, f32[1,4,32,128]{3,2,1,0:T(8,128)}) custom-call(f32[12,4,8,128]{3,2,1,0:T(8,128)S(1)} %collective-permute-done.23.below, f32[12,4,8,128]{3,2,1,0:T(8,128)S(1)} %collective-permute-done.24.above, f32[4,4,8,128]{3,2,1,0:T(8,128)S(1)} %collective-permute-done.11.arrived, ...), custom_call_target="tpu_custom_call" | custom-call | tf_op jit(solution)/shard_map/coarse/pallas_call | solution.py:37
  (37 shorter events, 2.2 us)
Async XLA Ops:
  1.5 5.6 %collective-permute-start = (f32[4,32,128]{2,1,0:T(8,128)S(1)}, f32[4,32,128]{2,1,0:T(8,128)S(1)}, u32[]{:S(2)}, u32[]{:S(2)}) collective-permute-start(f32[4,32,128]{2,1,0:T(8,128)S(1)} %bitcast_select_fusion), channel_id=1, source_target_pairs={{0,16},{1,17},{2,18},{3,19},{4,20},{5,21},{6,22},{7,23},{8,24},{9,... | collective-permute-start | bytes 196616 | tf_op jit(solution)/shard_map/ppermute | solution.py:24
  7.1 16.8 %collective-permute-start.1 = (f32[30,4,8,128]{3,2,1,0:T(8,128)S(1)}, f32[30,4,8,128]{3,2,1,0:T(8,128)S(1)}, u32[]{:S(2)}, u32[]{:S(2)}) collective-permute-start(f32[30,4,8,128]{3,2,1,0:T(8,128)S(1)} %get-tuple-element.32), channel_id=1, source_target_pairs={{0,1},{1,2},{2,3},{3,4},{4,5},{5,6},{6,7},{7,8},{8,9},{9,10},{10,1... | collective-permute-start | bytes 1474568 | tf_op jit(solution)/shard_map/ppermute | solution.py:24
  8.7 17.4 %collective-permute-start.2 = (f32[30,4,8,128]{3,2,1,0:T(8,128)S(1)}, f32[30,4,8,128]{3,2,1,0:T(8,128)S(1)}, u32[]{:S(2)}, u32[]{:S(2)}) collective-permute-start(f32[30,4,8,128]{3,2,1,0:T(8,128)S(1)} %get-tuple-element.33), channel_id=1, source_target_pairs={{0,15},{1,0},{2,1},{3,2},{4,3},{5,4},{6,5},{7,6},{8,7},{9,8},{10,9... | collective-permute-start | bytes 1474568 | tf_op jit(solution)/shard_map/ppermute | solution.py:24
  12.6 20.8 %collective-permute-start.5 = (f32[2,3,3,4,8,128]{5,4,3,2,1,0:T(8,128)S(1)}, f32[2,3,3,4,8,128]{5,4,3,2,1,0:T(8,128)S(1)}, u32[]{:S(2)}, u32[]{:S(2)}) collective-permute-start(f32[2,3,3,4,8,128]{5,4,3,2,1,0:T(8,128)S(1)} %get-tuple-element.37), channel_id=1, source_target_pairs={{0,1},{1,2},{2,3},{3,4},{4,5},{5,6},{6,7},{7,8},{8,9},{9,10},{10,1... | collective-permute-start | bytes 884744 | tf_op jit(solution)/shard_map/ppermute | solution.py:24
  12.6 26.5 %collective-permute-start.6 = (f32[2,3,3,4,8,128]{5,4,3,2,1,0:T(8,128)S(1)}, f32[2,3,3,4,8,128]{5,4,3,2,1,0:T(8,128)S(1)}, u32[]{:S(2)}, u32[]{:S(2)}) collective-permute-start(f32[2,3,3,4,8,128]{5,4,3,2,1,0:T(8,128)S(1)} %get-tuple-element.38), channel_id=1, source_target_pairs={{0,15},{1,0},{2,1},{3,2},{4,3},{5,4},{6,5},{7,6},{8,7},{9,8},{10,9... | collective-permute-start | bytes 884744 | tf_op jit(solution)/shard_map/ppermute | solution.py:24
  27.0 12.1 %collective-permute-start.3 = (f32[2,4,4,8,128]{4,3,2,1,0:T(8,128)S(1)}, f32[2,4,4,8,128]{4,3,2,1,0:T(8,128)S(1)}, u32[]{:S(2)}, u32[]{:S(2)}) collective-permute-start(f32[2,4,4,8,128]{4,3,2,1,0:T(8,128)S(1)} %get-tuple-element.36.own.early0), channel_id=1, source_target_pairs={{0,1},{1,2},{2,3},{3,4},{4,5},{5,6},{6,7},{7,8},{8,9},{9,10},{10,1... | collective-permute-start | bytes 393224 | tf_op jit(solution)/shard_map/ppermute | solution.py:24
  27.0 12.0 %collective-permute-start.4 = (f32[2,4,4,8,128]{4,3,2,1,0:T(8,128)S(1)}, f32[2,4,4,8,128]{4,3,2,1,0:T(8,128)S(1)}, u32[]{:S(2)}, u32[]{:S(2)}) collective-permute-start(f32[2,4,4,8,128]{4,3,2,1,0:T(8,128)S(1)} %get-tuple-element.36.own.early0), channel_id=1, source_target_pairs={{0,15},{1,0},{2,1},{3,2},{4,3},{5,4},{6,5},{7,6},{8,7},{9,8},{10,9... | collective-permute-start | bytes 393224 | tf_op jit(solution)/shard_map/ppermute | solution.py:24
  33.4 8.6 %collective-permute-start.18 = (f32[2,4,4,8,128]{4,3,2,1,0:T(8,128)S(1)}, f32[2,4,4,8,128]{4,3,2,1,0:T(8,128)S(1)}, u32[]{:S(2)}, u32[]{:S(2)}) collective-permute-start(f32[2,4,4,8,128]{4,3,2,1,0:T(8,128)S(1)} %get-tuple-element.42.own), channel_id=1, source_target_pairs={{0,2},{1,3},{2,4},{3,5},{4,6},{5,7},{6,8},{7,9},{8,10},{9,11},{10,... | collective-permute-start | bytes 393224 | tf_op jit(solution)/shard_map/ppermute | solution.py:24
  33.4 8.6 %collective-permute-start.19 = (f32[2,4,4,8,128]{4,3,2,1,0:T(8,128)S(1)}, f32[2,4,4,8,128]{4,3,2,1,0:T(8,128)S(1)}, u32[]{:S(2)}, u32[]{:S(2)}) collective-permute-start(f32[2,4,4,8,128]{4,3,2,1,0:T(8,128)S(1)} %get-tuple-element.42.own), channel_id=1, source_target_pairs={{0,14},{1,15},{2,0},{3,1},{4,2},{5,3},{6,4},{7,5},{8,6},{9,7},{10,... | collective-permute-start | bytes 393224 | tf_op jit(solution)/shard_map/ppermute | solution.py:24
  42.1 26.8 %collective-permute-start.20 = (f32[2,16,4,8,128]{4,3,2,1,0:T(8,128)S(1)}, f32[2,16,4,8,128]{4,3,2,1,0:T(8,128)S(1)}, u32[]{:S(2)}, u32[]{:S(2)}) collective-permute-start(f32[2,16,4,8,128]{4,3,2,1,0:T(8,128)S(1)} %get-tuple-element.43), channel_id=1, source_target_pairs={{0,4},{1,5},{2,6},{3,7},{4,8},{5,9},{6,10},{7,11},{8,12},{9,13},{1... | collective-permute-start | bytes 1572872 | tf_op jit(solution)/shard_map/ppermute | solution.py:24
  42.2 26.7 %collective-permute-start.21 = (f32[2,16,4,8,128]{4,3,2,1,0:T(8,128)S(1)}, f32[2,16,4,8,128]{4,3,2,1,0:T(8,128)S(1)}, u32[]{:S(2)}, u32[]{:S(2)}) collective-permute-start(f32[2,16,4,8,128]{4,3,2,1,0:T(8,128)S(1)} %get-tuple-element.44), channel_id=1, source_target_pairs={{0,12},{1,13},{2,14},{3,15},{4,0},{5,1},{6,2},{7,3},{8,4},{9,5},{1... | collective-permute-start | bytes 1572872 | tf_op jit(solution)/shard_map/ppermute | solution.py:24
  45.4 9.2 %collective-permute-start.7 = (f32[2,4,4,8,128]{4,3,2,1,0:T(8,128)S(1)}, f32[2,4,4,8,128]{4,3,2,1,0:T(8,128)S(1)}, u32[]{:S(2)}, u32[]{:S(2)}) collective-permute-start(f32[2,4,4,8,128]{4,3,2,1,0:T(8,128)S(1)} %early1.1.own.after), channel_id=1, source_target_pairs={{0,1},{1,2},{2,3},{3,4},{4,5},{5,6},{6,7},{7,8},{8,9},{9,10},{10,1... | collective-permute-start | bytes 393224 | tf_op jit(solution)/shard_map/ppermute | solution.py:24
  45.4 9.2 %collective-permute-start.8 = (f32[2,4,4,8,128]{4,3,2,1,0:T(8,128)S(1)}, f32[2,4,4,8,128]{4,3,2,1,0:T(8,128)S(1)}, u32[]{:S(2)}, u32[]{:S(2)}) collective-permute-start(f32[2,4,4,8,128]{4,3,2,1,0:T(8,128)S(1)} %early1.1.own.after), channel_id=1, source_target_pairs={{0,15},{1,0},{2,1},{3,2},{4,3},{5,4},{6,5},{7,6},{8,7},{9,8},{10,9... | collective-permute-start | bytes 393224 | tf_op jit(solution)/shard_map/ppermute | solution.py:24
  55.2 7.2 %collective-permute-start.10 = (f32[2,4,4,8,128]{4,3,2,1,0:T(8,128)S(1)}, f32[2,4,4,8,128]{4,3,2,1,0:T(8,128)S(1)}, u32[]{:S(2)}, u32[]{:S(2)}) collective-permute-start(f32[2,4,4,8,128]{4,3,2,1,0:T(8,128)S(1)} %early2.1.own), channel_id=1, source_target_pairs={{0,15},{1,0},{2,1},{3,2},{4,3},{5,4},{6,5},{7,6},{8,7},{9,8},{10,9... | collective-permute-start | bytes 393224 | tf_op jit(solution)/shard_map/ppermute | solution.py:24
  59.9 8.3 %collective-permute-start.9 = (f32[2,4,4,8,128]{4,3,2,1,0:T(8,128)S(1)}, f32[2,4,4,8,128]{4,3,2,1,0:T(8,128)S(1)}, u32[]{:S(2)}, u32[]{:S(2)}) collective-permute-start(f32[2,4,4,8,128]{4,3,2,1,0:T(8,128)S(1)} %early2.1.own), channel_id=1, source_target_pairs={{0,1},{1,2},{2,3},{3,4},{4,5},{5,6},{6,7},{7,8},{8,9},{9,10},{10,1... | collective-permute-start | bytes 393224 | tf_op jit(solution)/shard_map/ppermute | solution.py:24
  68.8 0.8 copy-start
  69.0 23.1 %collective-permute-start.22 = (f32[2,40,4,8,128]{4,3,2,1,0:T(8,128)S(1)}, f32[2,40,4,8,128]{4,3,2,1,0:T(8,128)S(1)}, u32[]{:S(2)}, u32[]{:S(2)}) collective-permute-start(f32[2,40,4,8,128]{4,3,2,1,0:T(8,128)S(1)} %share.1.mine), channel_id=1, source_target_pairs={{0,16},{16,0},{32,48},{48,32},{64,80},{80,64},{96,112},{112,96},{1... | collective-permute-start | bytes 3932168 | tf_op jit(solution)/shard_map/ppermute | solution.py:28
  69.7 4.9 %collective-permute-start.11 = (f32[4,4,8,128]{3,2,1,0:T(8,128)S(1)}, f32[4,4,8,128]{3,2,1,0:T(8,128)S(1)}, u32[]{:S(2)}, u32[]{:S(2)}) collective-permute-start(f32[4,4,8,128]{3,2,1,0:T(8,128)S(1)} %pass.1), channel_id=1, source_target_pairs={{0,16},{1,17},{2,18},{3,19},{4,20},{5,21},{6,22},{7,23},{8,24},{9,... | collective-permute-start | bytes 196616 | tf_op jit(solution)/shard_map/ppermute | solution.py:24
  74.6 11.1 %collective-permute-start.12 = (f32[2,4,4,8,128]{4,3,2,1,0:T(8,128)S(1)}, f32[2,4,4,8,128]{4,3,2,1,0:T(8,128)S(1)}, u32[]{:S(2)}, u32[]{:S(2)}) collective-permute-start(f32[2,4,4,8,128]{4,3,2,1,0:T(8,128)S(1)} %change.1.own), channel_id=1, source_target_pairs={{0,1},{1,2},{2,3},{3,4},{4,5},{5,6},{6,7},{7,8},{8,9},{9,10},{10,1... | collective-permute-start | bytes 393224 | tf_op jit(solution)/shard_map/ppermute | solution.py:24
  74.7 11.0 %collective-permute-start.13 = (f32[2,4,4,8,128]{4,3,2,1,0:T(8,128)S(1)}, f32[2,4,4,8,128]{4,3,2,1,0:T(8,128)S(1)}, u32[]{:S(2)}, u32[]{:S(2)}) collective-permute-start(f32[2,4,4,8,128]{4,3,2,1,0:T(8,128)S(1)} %change.1.own), channel_id=1, source_target_pairs={{0,15},{1,0},{2,1},{3,2},{4,3},{5,4},{6,5},{7,6},{8,7},{9,8},{10,9... | collective-permute-start | bytes 393224 | tf_op jit(solution)/shard_map/ppermute | solution.py:24
  80.1 8.6 %collective-permute-start.14 = (f32[2,4,4,8,128]{4,3,2,1,0:T(8,128)S(1)}, f32[2,4,4,8,128]{4,3,2,1,0:T(8,128)S(1)}, u32[]{:S(2)}, u32[]{:S(2)}) collective-permute-start(f32[2,4,4,8,128]{4,3,2,1,0:T(8,128)S(1)} %change.1.own), channel_id=1, source_target_pairs={{0,2},{1,3},{2,4},{3,5},{4,6},{5,7},{6,8},{7,9},{8,10},{9,11},{10,... | collective-permute-start | bytes 393224 | tf_op jit(solution)/shard_map/ppermute | solution.py:24
  80.1 8.6 %collective-permute-start.15 = (f32[2,4,4,8,128]{4,3,2,1,0:T(8,128)S(1)}, f32[2,4,4,8,128]{4,3,2,1,0:T(8,128)S(1)}, u32[]{:S(2)}, u32[]{:S(2)}) collective-permute-start(f32[2,4,4,8,128]{4,3,2,1,0:T(8,128)S(1)} %change.1.own), channel_id=1, source_target_pairs={{0,14},{1,15},{2,0},{3,1},{4,2},{5,3},{6,4},{7,5},{8,6},{9,7},{10,... | collective-permute-start | bytes 393224 | tf_op jit(solution)/shard_map/ppermute | solution.py:24
  88.7 11.1 %collective-permute-start.16 = (f32[2,16,4,8,128]{4,3,2,1,0:T(8,128)S(1)}, f32[2,16,4,8,128]{4,3,2,1,0:T(8,128)S(1)}, u32[]{:S(2)}, u32[]{:S(2)}) collective-permute-start(f32[2,16,4,8,128]{4,3,2,1,0:T(8,128)S(1)} %get-tuple-element.40), channel_id=1, source_target_pairs={{0,4},{1,5},{2,6},{3,7},{4,8},{5,9},{6,10},{7,11},{8,12},{9,13},{1... | collective-permute-start | bytes 1572872 | tf_op jit(solution)/shard_map/ppermute | solution.py:24
  88.8 11.1 %collective-permute-start.17 = (f32[2,16,4,8,128]{4,3,2,1,0:T(8,128)S(1)}, f32[2,16,4,8,128]{4,3,2,1,0:T(8,128)S(1)}, u32[]{:S(2)}, u32[]{:S(2)}) collective-permute-start(f32[2,16,4,8,128]{4,3,2,1,0:T(8,128)S(1)} %get-tuple-element.41), channel_id=1, source_target_pairs={{0,12},{1,13},{2,14},{3,15},{4,0},{5,1},{6,2},{7,3},{8,4},{9,5},{1... | collective-permute-start | bytes 1572872 | tf_op jit(solution)/shard_map/ppermute | solution.py:24
  110.9 10.6 %collective-permute-start.23 = (f32[12,4,8,128]{3,2,1,0:T(8,128)S(1)}, f32[12,4,8,128]{3,2,1,0:T(8,128)S(1)}, u32[]{:S(2)}, u32[]{:S(2)}) collective-permute-start(f32[12,4,8,128]{3,2,1,0:T(8,128)S(1)} %get-tuple-element.48), channel_id=1, source_target_pairs={{0,17},{1,18},{2,19},{3,20},{4,21},{5,22},{6,23},{7,24},{8,25},{9,... | collective-permute-start | bytes 589832 | tf_op jit(solution)/shard_map/ppermute | solution.py:24
  111.0 10.5 %collective-permute-start.24 = (f32[12,4,8,128]{3,2,1,0:T(8,128)S(1)}, f32[12,4,8,128]{3,2,1,0:T(8,128)S(1)}, u32[]{:S(2)}, u32[]{:S(2)}) collective-permute-start(f32[12,4,8,128]{3,2,1,0:T(8,128)S(1)} %get-tuple-element.48), channel_id=1, source_target_pairs={{0,31},{1,16},{2,17},{3,18},{4,19},{5,20},{6,21},{7,22},{8,23},{9,... | collective-permute-start | bytes 589832 | tf_op jit(solution)/shard_map/ppermute | solution.py:24

commit v4 on v3

--- a/solution.py
+++ b/solution.py
@@ -251,7 +251,7 @@
             coef[level, p, j] = 1.0 / (stored[j] * FACTORS[level] + coupling)
 
 
-def first_kernel(start, lo, hi, force, field, coef, state, near, far, right):
+def first_kernel(start, lo, hi, force, field, coef, state, up, down, near, far, right):
     position = lax.axis_index("space")
     cells = SLAB * lax.axis_size("space")
     for p in range(REACH):
@@ -278,7 +278,16 @@
             return rows_at(force, b, 0, p - EDGE)
         return rows_at(hi, UP_FORCE + EDGE * b + p - EDGE - SLAB)
 
-    step(coef, [FINE, FINE], window, source, lambda b, p, rows: put_rows(state, (b, p), rows), near, far, right)
+    def put(b, p, rows):
+        for target in (state, up, down):
+            put_rows(target, (b, p), rows)
+
+    step(coef, [FINE, FINE], window, source, put, near, far, right)
+    for part, target in ((lo, up), (hi, down)):
+        for k in range(2):
+            for z in range(SLAB):
+                at = UP_FIELD + SLAB * k + z
+                put_rows(target, (2 + k, z), own_half(rows_at(part, at), rows_at(part, at + 2 * SLAB)))
 
 
 def early_kernel(section):
@@ -316,14 +325,19 @@
 INNER = 8
 
 
+THIN = PACK - SLAB
+
+
 def pack_kernel(own, lo, hi, lo_two, hi_two, up, down):
-    for k in range(own.shape[0]):
-        for z in range(SLAB):
-            for j in range(ROWS):
-                parts = [lo_two[k, z, j], lo[k, z, j], own[k, z, j], hi[k, z, j], hi_two[k, z, j]]
-                for i in range(4):
-                    up[k, SLAB * i + z, j] = parts[i]
-                    down[k, SLAB * i + z, j] = parts[i + 1]
+    for z in range(SLAB):
+        parts = [rows_at(part, 0, z) for part in (lo_two, lo, own, hi, hi_two)]
+        for i in range(4):
+            put_rows(up, (SLAB * i + z,), parts[i])
+            put_rows(down, (SLAB * i + z,), parts[i + 1])
+        for i, part in enumerate((lo, own, hi)):
+            rows = rows_at(part, 1, z)
+            put_rows(up, (PACK + SLAB * i + z,), rows)
+            put_rows(down, (PACK + SLAB * i + z,), rows)
 
 
 def pack_field_kernel(own, lo, hi, lo_two, hi_two, after, up, down):
@@ -332,7 +346,7 @@
             at = UP_FIELD + SLAB * k + z
             near_lo = own_half(rows_at(lo, at), rows_at(lo, at + 2 * SLAB))
             near_hi = own_half(rows_at(hi, at), rows_at(hi, at + 2 * SLAB))
-            parts = [rows_at(lo_two, k, z), near_lo, rows_at(own, k, z), near_hi, rows_at(hi_two, k, z)]
+            parts = [rows_at(lo_two, 2 + k, z), near_lo, rows_at(own, k, z), near_hi, rows_at(hi_two, 2 + k, z)]
             for i in range(4):
                 put_rows(up, (k, SLAB * i + z), parts[i])
                 put_rows(down, (k, SLAB * i + z), parts[i + 1])
@@ -340,8 +354,8 @@
 
 def share_kernel(lo_two, hi_two, lo_far, hi_far, after, share):
     share[:, :PACK] = lo_far[...]
-    share[:, PACK : PACK + SLAB] = lo_two[...]
-    share[:, PACK + SLAB : PACK + 2 * SLAB] = hi_two[...]
+    share[:, PACK : PACK + SLAB] = lo_two[2:]
+    share[:, PACK + SLAB : PACK + 2 * SLAB] = hi_two[2:]
     share[:, PACK + 2 * SLAB :] = hi_far[...]
 
 
@@ -429,10 +443,17 @@
     own, lo, hi, lo_two, hi_two, lo_far, hi_far, relaxed, coef, late0, late1, late2, change, last, on, near, far, right
 ):
     last_time = lax.axis_index("tm") == lax.axis_size("tm") - 1
+    for z in range(PACK):
+        put_rows(near, (0, z), rows_at(lo_far, z))
+        put_rows(near, (0, HALO + 3 * SLAB + z), rows_at(hi_far, z))
+    empty = [jnp.zeros((8, 128), jnp.float32)] * ROWS
+    for z in range(SLAB):
+        put_rows(near, (1, z), empty)
+        put_rows(near, (1, SPAN - SLAB + z), empty)
+    for z in range(THIN):
+        put_rows(near, (1, SLAB + z), rows_at(lo_far, PACK + z))
+        put_rows(near, (1, HALO + 3 * SLAB + z), rows_at(hi_far, PACK + z))
     for b in range(2):
-        for z in range(PACK):
-            put_rows(near, (b, z), rows_at(lo_far, b, z))
-            put_rows(near, (b, HALO + 3 * SLAB + z), rows_at(hi_far, b, z))
         for i, part in enumerate((lo_two, lo, own, hi, hi_two)):
             for z in range(SLAB):
                 put_rows(near, (b, HALO + SLAB * (i - 2) + z), rows_at(part, b, z))
@@ -510,14 +531,16 @@
     up, down, start = call(complete_kernel, "complete", [message, message, both], arrived, guess, up, down)
     lo, hi = shifted(up, 0, 1), shifted(down, 0, -1)
     force_lo, force_hi = shifted(up_later, 0, 1), shifted(down_later, 0, -1)
-    coef, state = call(
-        first_kernel, "first", [(8, REACH) + PLANE, both], start, lo, hi, force, field, scratch=scratch_of(2)
+    coef, state, up, down = call(
+        first_kernel, "first", [(8, REACH) + PLANE, both, (4,) + four, (4,) + four], start, lo, hi, force, field, scratch=scratch_of(2)
     )
-    half_lo, half_hi = shifted(half, 0, 2), shifted(half, 0, -2)
     packed = (2, PACK) + PLANE
     early = [state]
     for section in range(1, CF):
-        state_lo, state_hi = shifted(state, 0, 1), shifted(state, 0, -1)
+        if section == 1:
+            state_lo, state_hi = half_lo, half_hi = shifted(up, 0, 1), shifted(down, 0, -1)
+        else:
+            state_lo, state_hi = shifted(state, 0, 1), shifted(state, 0, -1)
         (state,) = call(
             early_kernel(section), f"early{section}", [both], state, state_lo, state_hi, force, force_lo, force_hi,
             coef, scratch=scratch_of(2),
@@ -539,6 +562,7 @@
     (change,) = call(change_kernel, "change", [both], arrived, relaxed, start)
     change_lo, change_hi = shifted(change, 0, 1), shifted(change, 0, -1)
     two_lo, two_hi = shifted(change, 0, 2), shifted(change, 0, -2)
+    packed = (PACK + THIN,) + PLANE
     change_up, change_down = call(pack_kernel, "pack", [packed, packed], change, change_lo, change_hi, two_lo, two_hi)
     far_lo, far_hi = shifted(change_up, 0, 4), shifted(change_down, 0, -4)
     (coef,) = call(

time: 125 us -> 119 us (0.952)
  the two profiles are of different devices: /device:TPU:0 before, /device:TPU:95 now
where the time goes in v4:
time: 119 us
  waiting for transfers between devices  56.9 us (48%)
  starting transfers between devices  40.5 us (34%)
  Pallas kernels  19.1 us (16%)
    ppermute x22, waiting for transfers between devices, shifted(): return lax.ppermute(value, ('tm', 'space'), pairs)  56.9 us
    ppermute x22, starting transfers between devices, shifted(): return lax.ppermute(value, ('tm', 'space'), pairs)  34.2 us
    pallas_call x15, Pallas kernels, call(): pl.pallas_call(kernel, out_shape=[(pltpu.HBM if stored else pltpu.VMEM)(s...  19.1 us
    ppermute x1, starting transfers between devices, swapped(): lax.ppermute(value, 'tm', [(t, t ^ 1) for t in range(lax.axis_size('tm'))])  6.3 us
  transfers between devices with their start and end apart: 23, of which 15 were waited for; matrix products, arithmetic and copies ran while one was open for 1% of the time, Pallas kernels for 5%

profile of v4, /device:TPU:95, one launch (start us, length us, event | category | flops | bytes accessed | tf_op | source)
XLA Modules:
  0.0 119.2 jit_solution(527804762910413217)
XLA Ops:
  1.5 2.2 %collective-permute-start = (f32[4,32,128]{2,1,0:T(8,128)S(1)}, f32[4,32,128]{2,1,0:T(8,128)S(1)}, u32[]{:S(2)}, u32[]{:S(2)}) collective-permute-start(f32[4,32,128]{2,1,0:T(8,128)S(1)} %bitcast_select_fusion), channel_id=1, source_target_pairs={{0,16},{1,17},{2,18},{3,19},{4,20},{5,21},{6,22},{7,23},{8,24},{9,... | collective-permute-start | bytes 196616 | tf_op jit(solution)/shard_map/ppermute | solution.py:24
  3.7 1.3 %prepare.1 = (f32[30,4,8,128]{3,2,1,0:T(8,128)S(1)}, f32[30,4,8,128]{3,2,1,0:T(8,128)S(1)}, f32[2,3,3,4,8,128]{5,4,3,2,1,0:T(8,128)S(1)}, f32[2,3,3,4,8,128]{5,4...) custom-call(f32[8,4,32,128]{3,2,1,0:T(8,128)} %forcing.1, ...), custom_call_target="tpu_custom_call" | custom-call | tf_op jit(solution)/shard_map/prepare/pallas_call | solution.py:37
  5.2 1.5 %collective-permute-start.2 = (f32[30,4,8,128]{3,2,1,0:T(8,128)S(1)}, f32[30,4,8,128]{3,2,1,0:T(8,128)S(1)}, u32[]{:S(2)}, u32[]{:S(2)}) collective-permute-start(f32[30,4,8,128]{3,2,1,0:T(8,128)S(1)} %get-tuple-element.35), channel_id=1, source_target_pairs={{0,15},{1,0},{2,1},{3,2},{4,3},{5,4},{6,5},{7,6},{8,7},{9,8},{10,9... | collective-permute-start | bytes 1474568 | tf_op jit(solution)/shard_map/ppermute | solution.py:24
  6.7 3.4 %collective-permute-start.5 = (f32[2,3,3,4,8,128]{5,4,3,2,1,0:T(8,128)S(1)}, f32[2,3,3,4,8,128]{5,4,3,2,1,0:T(8,128)S(1)}, u32[]{:S(2)}, u32[]{:S(2)}) collective-permute-start(f32[2,3,3,4,8,128]{5,4,3,2,1,0:T(8,128)S(1)} %get-tuple-element.41), channel_id=1, source_target_pairs={{0,1},{1,2},{2,3},{3,4},{4,5},{5,6},{6,7},{7,8},{8,9},{9,10},{10,1... | collective-permute-start | bytes 884744 | tf_op jit(solution)/shard_map/ppermute | solution.py:24
  10.1 7.0 %collective-permute-done.1.lo = f32[30,4,8,128]{3,2,1,0:T(8,128)S(1)} collective-permute-done((f32[30,4,8,128]{3,2,1,0:T(8,128)S(1)}, f32[30,4,8,128]{3,2,1,0:T(8,128)S(1)}, u32[]{:S(2)}, u32[]{:S(2)}) %collective-permute-start.1) | collective-permute-done | bytes 491552 | tf_op jit(solution)/shard_map/ppermute | solution.py:24
  17.1 3.4 %collective-permute-done.2.hi = f32[30,4,8,128]{3,2,1,0:T(8,128)S(1)} collective-permute-done((f32[30,4,8,128]{3,2,1,0:T(8,128)S(1)}, f32[30,4,8,128]{3,2,1,0:T(8,128)S(1)}, u32[]{:S(2)}, u32[]{:S(2)}) %collective-permute-start.2) | collective-permute-done | bytes 491552 | tf_op jit(solution)/shard_map/ppermute | solution.py:24
  21.6 1.3 %collective-permute-start.4 = (f32[4,4,4,8,128]{4,3,2,1,0:T(8,128)S(1)}, f32[4,4,4,8,128]{4,3,2,1,0:T(8,128)S(1)}, u32[]{:S(2)}, u32[]{:S(2)}) collective-permute-start(f32[4,4,4,8,128]{4,3,2,1,0:T(8,128)S(1)} %get-tuple-element.40), channel_id=1, source_target_pairs={{0,15},{1,0},{2,1},{3,2},{4,3},{5,4},{6,5},{7,6},{8,7},{9,8},{10,9... | collective-permute-start | bytes 786440 | tf_op jit(solution)/shard_map/ppermute | solution.py:24
  23.5 3.4 %collective-permute-done.6.force_hi = f32[2,3,3,4,8,128]{5,4,3,2,1,0:T(8,128)S(1)} collective-permute-done((f32[2,3,3,4,8,128]{5,4,3,2,1,0:T(8,128)S(1)}, f32[2,3,3,4,8,128]{5,4,3,2,1,0:T(8,128)S(1)}, u32[]{:S(2)}, u32[]{:S(2)}) %collective-permute-start.6) | collective-permute-done | bytes 294944 | tf_op jit(solution)/shard_map/ppermute | solution.py:24
  27.6 3.1 %collective-permute-done.4.hi.hi_two = f32[4,4,4,8,128]{4,3,2,1,0:T(8,128)S(1)} collective-permute-done((f32[4,4,4,8,128]{4,3,2,1,0:T(8,128)S(1)}, f32[4,4,4,8,128]{4,3,2,1,0:T(8,128)S(1)}, u32[]{:S(2)}, u32[]{:S(2)}) %collective-permute-start.4) | collective-permute-done | bytes 262176 | tf_op jit(solution)/shard_map/ppermute | solution.py:24
  31.4 0.9 collective-permute-start.18
  33.0 1.5 %collective-permute-start.7 = (f32[2,4,4,8,128]{4,3,2,1,0:T(8,128)S(1)}, f32[2,4,4,8,128]{4,3,2,1,0:T(8,128)S(1)}, u32[]{:S(2)}, u32[]{:S(2)}) collective-permute-start(f32[2,4,4,8,128]{4,3,2,1,0:T(8,128)S(1)} %early1.1.own.after), channel_id=1, source_target_pairs={{0,1},{1,2},{2,3},{3,4},{4,5},{5,6},{6,7},{7,8},{8,9},{9,10},{10,1... | collective-permute-start | bytes 393224 | tf_op jit(solution)/shard_map/ppermute | solution.py:24
  34.4 2.4 %collective-permute-done.7.lo = f32[2,4,4,8,128]{4,3,2,1,0:T(8,128)S(1)} collective-permute-done((f32[2,4,4,8,128]{4,3,2,1,0:T(8,128)S(1)}, f32[2,4,4,8,128]{4,3,2,1,0:T(8,128)S(1)}, u32[]{:S(2)}, u32[]{:S(2)}) %collective-permute-start.7) | collective-permute-done | bytes 131104 | tf_op jit(solution)/shard_map/ppermute | solution.py:24
  36.8 4.9 %collective-permute-done.8.hi = f32[2,4,4,8,128]{4,3,2,1,0:T(8,128)S(1)} collective-permute-done((f32[2,4,4,8,128]{4,3,2,1,0:T(8,128)S(1)}, f32[2,4,4,8,128]{4,3,2,1,0:T(8,128)S(1)}, u32[]{:S(2)}, u32[]{:S(2)}) %collective-permute-start.8) | collective-permute-done | bytes 131104 | tf_op jit(solution)/shard_map/ppermute | solution.py:24
  42.4 4.8 %collective-permute-start.9 = (f32[2,4,4,8,128]{4,3,2,1,0:T(8,128)S(1)}, f32[2,4,4,8,128]{4,3,2,1,0:T(8,128)S(1)}, u32[]{:S(2)}, u32[]{:S(2)}) collective-permute-start(f32[2,4,4,8,128]{4,3,2,1,0:T(8,128)S(1)} %early2.1.own), channel_id=1, source_target_pairs={{0,1},{1,2},{2,3},{3,4},{4,5},{5,6},{6,7},{7,8},{8,9},{9,10},{10,1... | collective-permute-start | bytes 393224 | tf_op jit(solution)/shard_map/ppermute | solution.py:24
  47.1 2.5 %collective-permute-done.10.hi = f32[2,4,4,8,128]{4,3,2,1,0:T(8,128)S(1)} collective-permute-done((f32[2,4,4,8,128]{4,3,2,1,0:T(8,128)S(1)}, f32[2,4,4,8,128]{4,3,2,1,0:T(8,128)S(1)}, u32[]{:S(2)}, u32[]{:S(2)}) %collective-permute-start.10) | collective-permute-done | bytes 131104 | tf_op jit(solution)/shard_map/ppermute | solution.py:24
  50.4 6.3 %collective-permute-start.20 = (f32[2,40,4,8,128]{4,3,2,1,0:T(8,128)S(1)}, f32[2,40,4,8,128]{4,3,2,1,0:T(8,128)S(1)}, u32[]{:S(2)}, u32[]{:S(2)}) collective-permute-start(f32[2,40,4,8,128]{4,3,2,1,0:T(8,128)S(1)} %share.1.mine), channel_id=1, source_target_pairs={{0,16},{16,0},{32,48},{48,32},{64,80},{80,64},{96,112},{112,96},{1... | collective-permute-start | bytes 3932168 | tf_op jit(solution)/shard_map/ppermute | solution.py:28
  56.7 4.0 %collective-permute-start.11 = (f32[4,4,8,128]{3,2,1,0:T(8,128)S(1)}, f32[4,4,8,128]{3,2,1,0:T(8,128)S(1)}, u32[]{:S(2)}, u32[]{:S(2)}) collective-permute-start(f32[4,4,8,128]{3,2,1,0:T(8,128)S(1)} %pass.1), channel_id=1, source_target_pairs={{0,16},{1,17},{2,18},{3,19},{4,20},{5,21},{6,22},{7,23},{8,24},{9,... | collective-permute-start | bytes 196616 | tf_op jit(solution)/shard_map/ppermute | solution.py:24
  60.7 1.3 %collective-permute-done.11.arrived = f32[4,4,8,128]{3,2,1,0:T(8,128)S(1)} collective-permute-done((f32[4,4,8,128]{3,2,1,0:T(8,128)S(1)}, f32[4,4,8,128]{3,2,1,0:T(8,128)S(1)}, u32[]{:S(2)}, u32[]{:S(2)}) %collective-permute-start.11) | collective-permute-done | bytes 65568 | tf_op jit(solution)/shard_map/ppermute | solution.py:24
  62.0 5.1 %collective-permute-start.12 = (f32[2,4,4,8,128]{4,3,2,1,0:T(8,128)S(1)}, f32[2,4,4,8,128]{4,3,2,1,0:T(8,128)S(1)}, u32[]{:S(2)}, u32[]{:S(2)}) collective-permute-start(f32[2,4,4,8,128]{4,3,2,1,0:T(8,128)S(1)} %change.1.own), channel_id=1, source_target_pairs={{0,1},{1,2},{2,3},{3,4},{4,5},{5,6},{6,7},{7,8},{8,9},{9,10},{10,1... | collective-permute-start | bytes 393224 | tf_op jit(solution)/shard_map/ppermute | solution.py:24
  67.2 1.3 %collective-permute-start.14 = (f32[2,4,4,8,128]{4,3,2,1,0:T(8,128)S(1)}, f32[2,4,4,8,128]{4,3,2,1,0:T(8,128)S(1)}, u32[]{:S(2)}, u32[]{:S(2)}) collective-permute-start(f32[2,4,4,8,128]{4,3,2,1,0:T(8,128)S(1)} %change.1.own), channel_id=1, source_target_pairs={{0,2},{1,3},{2,4},{3,5},{4,6},{5,7},{6,8},{7,9},{8,10},{9,11},{10,... | collective-permute-start | bytes 393224 | tf_op jit(solution)/shard_map/ppermute | solution.py:24
  68.5 1.7 %collective-permute-start.15 = (f32[2,4,4,8,128]{4,3,2,1,0:T(8,128)S(1)}, f32[2,4,4,8,128]{4,3,2,1,0:T(8,128)S(1)}, u32[]{:S(2)}, u32[]{:S(2)}) collective-permute-start(f32[2,4,4,8,128]{4,3,2,1,0:T(8,128)S(1)} %change.1.own), channel_id=1, source_target_pairs={{0,14},{1,15},{2,0},{3,1},{4,2},{5,3},{6,4},{7,5},{8,6},{9,7},{10,... | collective-permute-start | bytes 393224 | tf_op jit(solution)/shard_map/ppermute | solution.py:24
  70.2 10.2 %collective-permute-done.13.hi.change_hi = f32[2,4,4,8,128]{4,3,2,1,0:T(8,128)S(1)} collective-permute-done((f32[2,4,4,8,128]{4,3,2,1,0:T(8,128)S(1)}, f32[2,4,4,8,128]{4,3,2,1,0:T(8,128)S(1)}, u32[]{:S(2)}, u32[]{:S(2)}) %collective-permute-start.13) | collective-permute-done | bytes 131104 | tf_op jit(solution)/shard_map/ppermute | solution.py:24
  80.5 1.5 %collective-permute-start.17 = (f32[28,4,8,128]{3,2,1,0:T(8,128)S(1)}, f32[28,4,8,128]{3,2,1,0:T(8,128)S(1)}, u32[]{:S(2)}, u32[]{:S(2)}) collective-permute-start(f32[28,4,8,128]{3,2,1,0:T(8,128)S(1)} %get-tuple-element.45), channel_id=1, source_target_pairs={{0,12},{1,13},{2,14},{3,15},{4,0},{5,1},{6,2},{7,3},{8,4},{9,5},{1... | collective-permute-start | bytes 1376264 | tf_op jit(solution)/shard_map/ppermute | solution.py:24
  82.0 1.8 %wide.1.coef = f32[10,50,4,8,128]{4,3,2,1,0:T(8,128)S(1)} custom-call(f32[4,4,4,8,128]{4,3,2,1,0:T(8,128)S(1)} %get-tuple-element.37.field.own, f32[30,4,8,128]{3,2,1,0:T(8,128)S(1)} %collective-permute-done.1.lo, f32[30,4,8,128]{3,2,1,0:T(8,128)S(1)} %collective-permute-done.2.hi, f32[2,40,4,8,128]{4,3,2,1,0:T(8,128)S(1)} %share.1.mine, ...), custom_call_target="tpu_custom_call" | custom-call | tf_op jit(solution)/shard_map/wide/pallas_call | solution.py:37
  83.8 8.5 %collective-permute-done.16.lo_far = f32[28,4,8,128]{3,2,1,0:T(8,128)S(1)} collective-permute-done((f32[28,4,8,128]{3,2,1,0:T(8,128)S(1)}, f32[28,4,8,128]{3,2,1,0:T(8,128)S(1)}, u32[]{:S(2)}, u32[]{:S(2)}) %collective-permute-start.16) | collective-permute-done | bytes 458784 | tf_op jit(solution)/shard_map/ppermute | solution.py:24
  92.2 1.3 %collective-permute-done.17.hi_far = f32[28,4,8,128]{3,2,1,0:T(8,128)S(1)} collective-permute-done((f32[28,4,8,128]{3,2,1,0:T(8,128)S(1)}, f32[28,4,8,128]{3,2,1,0:T(8,128)S(1)}, u32[]{:S(2)}, u32[]{:S(2)}) %collective-permute-start.17) | collective-permute-done | bytes 458784 | tf_op jit(solution)/shard_map/ppermute | solution.py:24
  93.5 11.0 %late.1 = (f32[2,4,4,8,128]{4,3,2,1,0:T(8,128)S(1)}, f32[2,4,4,8,128]{4,3,2,1,0:T(8,128)S(1)}, f32[2,4,4,8,128]{4,3,2,1,0:T(8,128)S(1)}, f32[2,4,4,8,128]{4,3,2,...) custom-call(f32[2,4,4,8,128]{4,3,2,1,0:T(8,128)S(1)} %change.1.own, ...), custom_call_target="tpu_custom_call" | custom-call | tf_op jit(solution)/shard_map/late/pallas_call | solution.py:37
  104.6 2.6 %collective-permute-start.21 = (f32[12,4,8,128]{3,2,1,0:T(8,128)S(1)}, f32[12,4,8,128]{3,2,1,0:T(8,128)S(1)}, u32[]{:S(2)}, u32[]{:S(2)}) collective-permute-start(f32[12,4,8,128]{3,2,1,0:T(8,128)S(1)} %get-tuple-element.52), channel_id=1, source_target_pairs={{0,17},{1,18},{2,19},{3,20},{4,21},{5,22},{6,23},{7,24},{8,25},{9,... | collective-permute-start | bytes 589832 | tf_op jit(solution)/shard_map/ppermute | solution.py:24
  107.2 1.3 %collective-permute-start.22 = (f32[12,4,8,128]{3,2,1,0:T(8,128)S(1)}, f32[12,4,8,128]{3,2,1,0:T(8,128)S(1)}, u32[]{:S(2)}, u32[]{:S(2)}) collective-permute-start(f32[12,4,8,128]{3,2,1,0:T(8,128)S(1)} %get-tuple-element.52), channel_id=1, source_target_pairs={{0,31},{1,16},{2,17},{3,18},{4,19},{5,20},{6,21},{7,22},{8,23},{9,... | collective-permute-start | bytes 589832 | tf_op jit(solution)/shard_map/ppermute | solution.py:24
  109.4 2.9 %collective-permute-done.21.below = f32[12,4,8,128]{3,2,1,0:T(8,128)S(1)} collective-permute-done((f32[12,4,8,128]{3,2,1,0:T(8,128)S(1)}, f32[12,4,8,128]{3,2,1,0:T(8,128)S(1)}, u32[]{:S(2)}, u32[]{:S(2)}) %collective-permute-start.21) | collective-permute-done | bytes 196640 | tf_op jit(solution)/shard_map/ppermute | solution.py:24
  112.2 4.9 %collective-permute-done.22.above = f32[12,4,8,128]{3,2,1,0:T(8,128)S(1)} collective-permute-done((f32[12,4,8,128]{3,2,1,0:T(8,128)S(1)}, f32[12,4,8,128]{3,2,1,0:T(8,128)S(1)}, u32[]{:S(2)}, u32[]{:S(2)}) %collective-permute-start.22) | collective-permute-done | bytes 196640 | tf_op jit(solution)/shard_map/ppermute | solution.py:24
  117.1 1.9 %coarse.1 = (f32[2,4,32,128]{3,2,1,0:T(8,128)}, f32[1,4,32,128]{3,2,1,0:T(8,128)}) custom-call(f32[12,4,8,128]{3,2,1,0:T(8,128)S(1)} %collective-permute-done.21.below, f32[12,4,8,128]{3,2,1,0:T(8,128)S(1)} %collective-permute-done.22.above, f32[4,4,8,128]{3,2,1,0:T(8,128)S(1)} %collective-permute-done.11.arrived, ...), custom_call_target="tpu_custom_call" | custom-call | tf_op jit(solution)/shard_map/coarse/pallas_call | solution.py:37
  (33 shorter events, 7.2 us)
Async XLA Ops:
  1.5 3.6 %collective-permute-start = (f32[4,32,128]{2,1,0:T(8,128)S(1)}, f32[4,32,128]{2,1,0:T(8,128)S(1)}, u32[]{:S(2)}, u32[]{:S(2)}) collective-permute-start(f32[4,32,128]{2,1,0:T(8,128)S(1)} %bitcast_select_fusion), channel_id=1, source_target_pairs={{0,16},{1,17},{2,18},{3,19},{4,20},{5,21},{6,22},{7,23},{8,24},{9,... | collective-permute-start | bytes 196616 | tf_op jit(solution)/shard_map/ppermute | solution.py:24
  5.1 12.0 %collective-permute-start.1 = (f32[30,4,8,128]{3,2,1,0:T(8,128)S(1)}, f32[30,4,8,128]{3,2,1,0:T(8,128)S(1)}, u32[]{:S(2)}, u32[]{:S(2)}) collective-permute-start(f32[30,4,8,128]{3,2,1,0:T(8,128)S(1)} %get-tuple-element.34), channel_id=1, source_target_pairs={{0,1},{1,2},{2,3},{3,4},{4,5},{5,6},{6,7},{7,8},{8,9},{9,10},{10,1... | collective-permute-start | bytes 1474568 | tf_op jit(solution)/shard_map/ppermute | solution.py:24
  5.2 15.3 %collective-permute-start.2 = (f32[30,4,8,128]{3,2,1,0:T(8,128)S(1)}, f32[30,4,8,128]{3,2,1,0:T(8,128)S(1)}, u32[]{:S(2)}, u32[]{:S(2)}) collective-permute-start(f32[30,4,8,128]{3,2,1,0:T(8,128)S(1)} %get-tuple-element.35), channel_id=1, source_target_pairs={{0,15},{1,0},{2,1},{3,2},{4,3},{5,4},{6,5},{7,6},{8,7},{9,8},{10,9... | collective-permute-start | bytes 1474568 | tf_op jit(solution)/shard_map/ppermute | solution.py:24
  6.7 16.8 %collective-permute-start.5 = (f32[2,3,3,4,8,128]{5,4,3,2,1,0:T(8,128)S(1)}, f32[2,3,3,4,8,128]{5,4,3,2,1,0:T(8,128)S(1)}, u32[]{:S(2)}, u32[]{:S(2)}) collective-permute-start(f32[2,3,3,4,8,128]{5,4,3,2,1,0:T(8,128)S(1)} %get-tuple-element.41), channel_id=1, source_target_pairs={{0,1},{1,2},{2,3},{3,4},{4,5},{5,6},{6,7},{7,8},{8,9},{9,10},{10,1... | collective-permute-start | bytes 884744 | tf_op jit(solution)/shard_map/ppermute | solution.py:24
  10.1 16.7 %collective-permute-start.6 = (f32[2,3,3,4,8,128]{5,4,3,2,1,0:T(8,128)S(1)}, f32[2,3,3,4,8,128]{5,4,3,2,1,0:T(8,128)S(1)}, u32[]{:S(2)}, u32[]{:S(2)}) collective-permute-start(f32[2,3,3,4,8,128]{5,4,3,2,1,0:T(8,128)S(1)} %get-tuple-element.42), channel_id=1, source_target_pairs={{0,15},{1,0},{2,1},{3,2},{4,3},{5,4},{6,5},{7,6},{8,7},{9,8},{10,9... | collective-permute-start | bytes 884744 | tf_op jit(solution)/shard_map/ppermute | solution.py:24
  21.4 6.2 %collective-permute-start.3 = (f32[4,4,4,8,128]{4,3,2,1,0:T(8,128)S(1)}, f32[4,4,4,8,128]{4,3,2,1,0:T(8,128)S(1)}, u32[]{:S(2)}, u32[]{:S(2)}) collective-permute-start(f32[4,4,4,8,128]{4,3,2,1,0:T(8,128)S(1)} %get-tuple-element.39), channel_id=1, source_target_pairs={{0,1},{1,2},{2,3},{3,4},{4,5},{5,6},{6,7},{7,8},{8,9},{9,10},{10,1... | collective-permute-start | bytes 786440 | tf_op jit(solution)/shard_map/ppermute | solution.py:24
  21.6 9.1 %collective-permute-start.4 = (f32[4,4,4,8,128]{4,3,2,1,0:T(8,128)S(1)}, f32[4,4,4,8,128]{4,3,2,1,0:T(8,128)S(1)}, u32[]{:S(2)}, u32[]{:S(2)}) collective-permute-start(f32[4,4,4,8,128]{4,3,2,1,0:T(8,128)S(1)} %get-tuple-element.40), channel_id=1, source_target_pairs={{0,15},{1,0},{2,1},{3,2},{4,3},{5,4},{6,5},{7,6},{8,7},{9,8},{10,9... | collective-permute-start | bytes 786440 | tf_op jit(solution)/shard_map/ppermute | solution.py:24
  31.4 18.8 %collective-permute-start.18 = (f32[2,16,4,8,128]{4,3,2,1,0:T(8,128)S(1)}, f32[2,16,4,8,128]{4,3,2,1,0:T(8,128)S(1)}, u32[]{:S(2)}, u32[]{:S(2)}) collective-permute-start(f32[2,16,4,8,128]{4,3,2,1,0:T(8,128)S(1)} %get-tuple-element.47), channel_id=1, source_target_pairs={{0,4},{1,5},{2,6},{3,7},{4,8},{5,9},{6,10},{7,11},{8,12},{9,13},{1... | collective-permute-start | bytes 1572872 | tf_op jit(solution)/shard_map/ppermute | solution.py:24
  32.3 17.9 %collective-permute-start.19 = (f32[2,16,4,8,128]{4,3,2,1,0:T(8,128)S(1)}, f32[2,16,4,8,128]{4,3,2,1,0:T(8,128)S(1)}, u32[]{:S(2)}, u32[]{:S(2)}) collective-permute-start(f32[2,16,4,8,128]{4,3,2,1,0:T(8,128)S(1)} %get-tuple-element.48), channel_id=1, source_target_pairs={{0,12},{1,13},{2,14},{3,15},{4,0},{5,1},{6,2},{7,3},{8,4},{9,5},{1... | collective-permute-start | bytes 1572872 | tf_op jit(solution)/shard_map/ppermute | solution.py:24
  33.0 3.8 %collective-permute-start.7 = (f32[2,4,4,8,128]{4,3,2,1,0:T(8,128)S(1)}, f32[2,4,4,8,128]{4,3,2,1,0:T(8,128)S(1)}, u32[]{:S(2)}, u32[]{:S(2)}) collective-permute-start(f32[2,4,4,8,128]{4,3,2,1,0:T(8,128)S(1)} %early1.1.own.after), channel_id=1, source_target_pairs={{0,1},{1,2},{2,3},{3,4},{4,5},{5,6},{6,7},{7,8},{8,9},{9,10},{10,1... | collective-permute-start | bytes 393224 | tf_op jit(solution)/shard_map/ppermute | solution.py:24
  34.4 7.2 %collective-permute-start.8 = (f32[2,4,4,8,128]{4,3,2,1,0:T(8,128)S(1)}, f32[2,4,4,8,128]{4,3,2,1,0:T(8,128)S(1)}, u32[]{:S(2)}, u32[]{:S(2)}) collective-permute-start(f32[2,4,4,8,128]{4,3,2,1,0:T(8,128)S(1)} %early1.1.own.after), channel_id=1, source_target_pairs={{0,15},{1,0},{2,1},{3,2},{4,3},{5,4},{6,5},{7,6},{8,7},{9,8},{10,9... | collective-permute-start | bytes 393224 | tf_op jit(solution)/shard_map/ppermute | solution.py:24
  42.3 7.3 %collective-permute-start.10 = (f32[2,4,4,8,128]{4,3,2,1,0:T(8,128)S(1)}, f32[2,4,4,8,128]{4,3,2,1,0:T(8,128)S(1)}, u32[]{:S(2)}, u32[]{:S(2)}) collective-permute-start(f32[2,4,4,8,128]{4,3,2,1,0:T(8,128)S(1)} %early2.1.own), channel_id=1, source_target_pairs={{0,15},{1,0},{2,1},{3,2},{4,3},{5,4},{6,5},{7,6},{8,7},{9,8},{10,9... | collective-permute-start | bytes 393224 | tf_op jit(solution)/shard_map/ppermute | solution.py:24
  42.4 7.2 %collective-permute-start.9 = (f32[2,4,4,8,128]{4,3,2,1,0:T(8,128)S(1)}, f32[2,4,4,8,128]{4,3,2,1,0:T(8,128)S(1)}, u32[]{:S(2)}, u32[]{:S(2)}) collective-permute-start(f32[2,4,4,8,128]{4,3,2,1,0:T(8,128)S(1)} %early2.1.own), channel_id=1, source_target_pairs={{0,1},{1,2},{2,3},{3,4},{4,5},{5,6},{6,7},{7,8},{8,9},{9,10},{10,1... | collective-permute-start | bytes 393224 | tf_op jit(solution)/shard_map/ppermute | solution.py:24
  50.2 6.4 %copy-start = (f32[4,32,128]{2,1,0:T(8,128)S(1)}, f32[4,32,128]{2,1,0:T(8,128)}, u32[]{:S(2)}) copy-start(f32[4,32,128]{2,1,0:T(8,128)} %initial.1) | copy-start | bytes 196612
  50.4 31.6 %collective-permute-start.20 = (f32[2,40,4,8,128]{4,3,2,1,0:T(8,128)S(1)}, f32[2,40,4,8,128]{4,3,2,1,0:T(8,128)S(1)}, u32[]{:S(2)}, u32[]{:S(2)}) collective-permute-start(f32[2,40,4,8,128]{4,3,2,1,0:T(8,128)S(1)} %share.1.mine), channel_id=1, source_target_pairs={{0,16},{16,0},{32,48},{48,32},{64,80},{80,64},{96,112},{112,96},{1... | collective-permute-start | bytes 3932168 | tf_op jit(solution)/shard_map/ppermute | solution.py:28
  56.7 5.3 %collective-permute-start.11 = (f32[4,4,8,128]{3,2,1,0:T(8,128)S(1)}, f32[4,4,8,128]{3,2,1,0:T(8,128)S(1)}, u32[]{:S(2)}, u32[]{:S(2)}) collective-permute-start(f32[4,4,8,128]{3,2,1,0:T(8,128)S(1)} %pass.1), channel_id=1, source_target_pairs={{0,16},{1,17},{2,18},{3,19},{4,20},{5,21},{6,22},{7,23},{8,24},{9,... | collective-permute-start | bytes 196616 | tf_op jit(solution)/shard_map/ppermute | solution.py:24
  62.0 8.1 %collective-permute-start.12 = (f32[2,4,4,8,128]{4,3,2,1,0:T(8,128)S(1)}, f32[2,4,4,8,128]{4,3,2,1,0:T(8,128)S(1)}, u32[]{:S(2)}, u32[]{:S(2)}) collective-permute-start(f32[2,4,4,8,128]{4,3,2,1,0:T(8,128)S(1)} %change.1.own), channel_id=1, source_target_pairs={{0,1},{1,2},{2,3},{3,4},{4,5},{5,6},{6,7},{7,8},{8,9},{9,10},{10,1... | collective-permute-start | bytes 393224 | tf_op jit(solution)/shard_map/ppermute | solution.py:24
  67.2 13.2 %collective-permute-start.13 = (f32[2,4,4,8,128]{4,3,2,1,0:T(8,128)S(1)}, f32[2,4,4,8,128]{4,3,2,1,0:T(8,128)S(1)}, u32[]{:S(2)}, u32[]{:S(2)}) collective-permute-start(f32[2,4,4,8,128]{4,3,2,1,0:T(8,128)S(1)} %change.1.own), channel_id=1, source_target_pairs={{0,15},{1,0},{2,1},{3,2},{4,3},{5,4},{6,5},{7,6},{8,7},{9,8},{10,9... | collective-permute-start | bytes 393224 | tf_op jit(solution)/shard_map/ppermute | solution.py:24
  67.2 13.2 %collective-permute-start.14 = (f32[2,4,4,8,128]{4,3,2,1,0:T(8,128)S(1)}, f32[2,4,4,8,128]{4,3,2,1,0:T(8,128)S(1)}, u32[]{:S(2)}, u32[]{:S(2)}) collective-permute-start(f32[2,4,4,8,128]{4,3,2,1,0:T(8,128)S(1)} %change.1.own), channel_id=1, source_target_pairs={{0,2},{1,3},{2,4},{3,5},{4,6},{5,7},{6,8},{7,9},{8,10},{9,11},{10,... | collective-permute-start | bytes 393224 | tf_op jit(solution)/shard_map/ppermute | solution.py:24
  68.5 11.9 %collective-permute-start.15 = (f32[2,4,4,8,128]{4,3,2,1,0:T(8,128)S(1)}, f32[2,4,4,8,128]{4,3,2,1,0:T(8,128)S(1)}, u32[]{:S(2)}, u32[]{:S(2)}) collective-permute-start(f32[2,4,4,8,128]{4,3,2,1,0:T(8,128)S(1)} %change.1.own), channel_id=1, source_target_pairs={{0,14},{1,15},{2,0},{3,1},{4,2},{5,3},{6,4},{7,5},{8,6},{9,7},{10,... | collective-permute-start | bytes 393224 | tf_op jit(solution)/shard_map/ppermute | solution.py:24
  80.4 11.8 %collective-permute-start.16 = (f32[28,4,8,128]{3,2,1,0:T(8,128)S(1)}, f32[28,4,8,128]{3,2,1,0:T(8,128)S(1)}, u32[]{:S(2)}, u32[]{:S(2)}) collective-permute-start(f32[28,4,8,128]{3,2,1,0:T(8,128)S(1)} %get-tuple-element.44), channel_id=1, source_target_pairs={{0,4},{1,5},{2,6},{3,7},{4,8},{5,9},{6,10},{7,11},{8,12},{9,13},{1... | collective-permute-start | bytes 1376264 | tf_op jit(solution)/shard_map/ppermute | solution.py:24
  80.5 13.0 %collective-permute-start.17 = (f32[28,4,8,128]{3,2,1,0:T(8,128)S(1)}, f32[28,4,8,128]{3,2,1,0:T(8,128)S(1)}, u32[]{:S(2)}, u32[]{:S(2)}) collective-permute-start(f32[28,4,8,128]{3,2,1,0:T(8,128)S(1)} %get-tuple-element.45), channel_id=1, source_target_pairs={{0,12},{1,13},{2,14},{3,15},{4,0},{5,1},{6,2},{7,3},{8,4},{9,5},{1... | collective-permute-start | bytes 1376264 | tf_op jit(solution)/shard_map/ppermute | solution.py:24
  104.6 7.7 %collective-permute-start.21 = (f32[12,4,8,128]{3,2,1,0:T(8,128)S(1)}, f32[12,4,8,128]{3,2,1,0:T(8,128)S(1)}, u32[]{:S(2)}, u32[]{:S(2)}) collective-permute-start(f32[12,4,8,128]{3,2,1,0:T(8,128)S(1)} %get-tuple-element.52), channel_id=1, source_target_pairs={{0,17},{1,18},{2,19},{3,20},{4,21},{5,22},{6,23},{7,24},{8,25},{9,... | collective-permute-start | bytes 589832 | tf_op jit(solution)/shard_map/ppermute | solution.py:24
  107.2 9.9 %collective-permute-start.22 = (f32[12,4,8,128]{3,2,1,0:T(8,128)S(1)}, f32[12,4,8,128]{3,2,1,0:T(8,128)S(1)}, u32[]{:S(2)}, u32[]{:S(2)}) collective-permute-start(f32[12,4,8,128]{3,2,1,0:T(8,128)S(1)} %get-tuple-element.52), channel_id=1, source_target_pairs={{0,31},{1,16},{2,17},{3,18},{4,19},{5,20},{6,21},{7,22},{8,23},{9,... | collective-permute-start | bytes 589832 | tf_op jit(solution)/shard_map/ppermute | solution.py:24
